TPU v7x, 256 devices: a whole 4x4x8 slice. The times are simulated.
256 devices in a mesh: outer: 16 (over x, y), inner: 4 (over z_hi, core), cell: 4 (over z_lo).
Axes of the slice: x: 4, y: 4, z: 8 (z_hi: 2, z_lo: 4; z = z_hi * 4 + z_lo), core: 2. Of those that a mesh axis runs over, the one named last changes fastest.
Arguments:
- premium: float32 [48, 8192], P('outer', 'cell'), may hold values from 0.1 to 1
- charge: float32 [48, 8192], P('outer', 'cell'), may hold values from 0.05 to 2
- mortality: float32 [48, 8192], P('outer', 'cell'), may hold values from 0.0005 to 0.01
- lapse_table: float32 [16, 48], replicated, may hold values from 0.001 to 0.02
- lapse_index: int32 [8192], P('cell'), may hold values from 0 to 15
- guarantee_type: int32 [8192], P('cell'), may hold values from 0 to 2
- block_index: int32 [8192], P('cell'), may hold values from 0 to 255, never falling along the last dimension, each value on 1 to 128 neighbouring positions
- account_start: float32 [8192], P('cell'), may hold values from 5 to 50
- guarantee_start: float32 [8192], P('cell'), may hold values from 5 to 60
- fee_rate: float32 [8192], P('cell'), may hold values from 0.0003 to 0.002
- first_rates: float32 [64, 64, 36], P('outer', 'inner'), may hold values from 0 to 0.006
- second_rates: float32 [64, 64, 24], P('outer', 'inner'), may hold values from 0 to 0.006
- world_rates: float32 [64, 24], P('outer'), may hold values from 0 to 0.006
- spread: float32 [64], P('outer'), may hold values from 0.0005 to 0.002
Outputs:
- cell_reserve: float32 [2, 64, 8192], P(None, ('outer', 'inner'), 'cell')
- block_reserve: float32 [2, 64, 256], P(None, ('outer', 'inner'), 'cell')
- capital: float32 [1], replicated
Inputs may be any that keep to these rules, and one draw needn't show every extreme that they name: `block_index`: block numbers never fall along the cells; every block holds 1 to 128 cells.
All inputs are finite; a program needn't handle non-finite values.
Results may differ from a plain program's by a relative error of at most 0.0003.
Values sent between devices are 32-bit elements; how exact they have to be, the bound alone decides.
No kernel may reach another device: no remote copies, remote signals or barrier semaphores. Data moves between devices by JAX's collectives and lax.ppermute only.
A program may use at most 64 MiB of HBM per device.

v0:
```python
import jax
import jax.numpy as jnp
from jax import lax
from jax.sharding import PartitionSpec as P

PERIOD = 12
BLOCK = 128


credit_floor = 0.001
rollup_growth = 0.05


def sent_together(arrays, axis, dim, along):
    both = jnp.concatenate(arrays, axis=along)
    whole, at, finished = (lax.all_gather(both, axis, axis=dim, tiled=True), 0, [])
    for a in arrays:
        finished.append(lax.slice_in_dim(whole, at, at + a.shape[along], axis=along))
        at += a.shape[along]
    return tuple(finished)


def from_everyone(value, axis):
    devices = lax.axis_size(axis)
    return lax.all_to_all(
        jnp.broadcast_to(value[None], (devices, *value.shape)), axis, 0, 0, tiled=True
    )


def over_copies(value, axis):
    return from_everyone(value, axis).sum(axis=0)


def cut_along(value, dim, devices):
    lengths = value.shape
    tiles = value.reshape(*lengths[:dim], devices, lengths[dim] // devices, *lengths[dim + 1 :])
    return jnp.moveaxis(tiles, dim, 0)


def sum_at_owner(value, axis, dim):
    devices = lax.axis_size(axis)
    tiles = lax.all_to_all(cut_along(value, dim, devices), axis, 0, 0, tiled=True)
    return jnp.sum(tiles, axis=0)


def laid_out(tiles, dim):
    tiles = jnp.moveaxis(tiles, 0, dim)
    lengths = tiles.shape
    return tiles.reshape(*lengths[:dim], lengths[dim] * lengths[dim + 1], *lengths[dim + 2 :])


def gather_directly(value, axis, dim):
    return laid_out(from_everyone(value, axis), dim)


def month_step(
    account,
    surviving,
    guarantee,
    log_discount,
    present,
    short_rate,
    net_flow,
    mortality,
    lapse_base,
    fee_rate,
    spread,
):
    rider_fee = fee_rate * account
    before = jnp.maximum(account + net_flow - rider_fee, 0.0)
    credited = before * (1.0 + jnp.maximum(short_rate - spread, credit_floor))
    log_discount = log_discount + short_rate
    lapse_rate = lapse_base * jnp.clip(credited / guarantee, 0.5, 1.5)
    claims = surviving * (mortality * jnp.maximum(guarantee - credited, 0.0) - rider_fee)
    present = present + jnp.exp(-log_discount) * claims
    surviving = surviving * (1.0 - mortality - lapse_rate)
    return (credited, surviving, log_discount, present)


def anniversary(account, guarantee, ratchet, rollup):
    return (
        guarantee
        + ratchet * (jnp.maximum(guarantee, account) - guarantee)
        + rollup * rollup_growth * guarantee
    )


def project(
    account,
    surviving,
    guarantee,
    short_rates,
    start_month,
    spread,
    plans,
    fee_rate,
    ratchet,
    rollup,
):
    net_flow, mortality, lapse_base = plans
    full_shape = (short_rates.shape[0], short_rates.shape[1], account.shape[2])
    account = jnp.broadcast_to(account, full_shape)
    surviving = jnp.broadcast_to(surviving, full_shape)
    guarantee = jnp.broadcast_to(guarantee, full_shape)
    log_discount = jnp.zeros(full_shape[:2] + (1,), jnp.float32)
    present = jnp.zeros(full_shape, jnp.float32)
    for period in range(short_rates.shape[2] // PERIOD):

        def advance(within, loop_state, period=period, guarantee=guarantee):
            offset = period * PERIOD + within
            calendar = start_month + offset
            short_rate = lax.dynamic_slice_in_dim(short_rates, offset, 1, 2)
            return month_step(
                loop_state[0],
                loop_state[1],
                guarantee,
                loop_state[2],
                loop_state[3],
                short_rate,
                lax.dynamic_index_in_dim(net_flow, calendar, 0, False),
                lax.dynamic_index_in_dim(mortality, calendar, 0, False),
                lax.dynamic_index_in_dim(lapse_base, calendar, 0, False),
                fee_rate,
                spread,
            )

        account, surviving, log_discount, present = lax.fori_loop(
            0, PERIOD, advance, (account, surviving, log_discount, present)
        )
        guarantee = anniversary(account, guarantee, ratchet, rollup)
    return (account, surviving, guarantee, present)


def body(
    premium,
    charge,
    mortality,
    lapse_table,
    lapse_index,
    guarantee_type,
    block_index,
    account_start,
    guarantee_start,
    fee_rate,
    first_rates,
    second_rates,
    world_rates,
    spread,
):
    net_flow, mortality_all = sent_together((premium - charge, mortality), "outer", 0, 1)
    tables = jnp.arange(lapse_table.shape[0])
    lapse_hot = (lapse_index[None, :] == tables[:, None]).astype(jnp.float32)
    lapse_base = jnp.dot(lapse_table.T, lapse_hot, precision=lax.Precision.HIGHEST)
    plans = (net_flow, mortality_all, lapse_base)
    ratchet = (guarantee_type == 1).astype(jnp.float32)
    rollup = (guarantee_type == 2).astype(jnp.float32)
    cells_local = account_start.shape[0]
    paths_all = first_rates.shape[1] * lax.axis_size("inner")
    cells_all = cells_local * lax.axis_size("cell")
    spread_one = spread[:, None, None]
    world_three = world_rates[:, None, :]
    year_one = project(
        account_start[None, None, :],
        jnp.ones((1, 1, cells_local), jnp.float32),
        guarantee_start[None, None, :],
        world_three[:, :, :PERIOD],
        0,
        spread_one,
        plans,
        fee_rate,
        ratchet,
        rollup,
    )
    inner_one = project(
        year_one[0],
        year_one[1],
        year_one[2],
        first_rates,
        PERIOD,
        spread_one,
        plans,
        fee_rate,
        ratchet,
        rollup,
    )
    partial_one = jnp.sum(inner_one[3], axis=1) / paths_all
    local_one = jnp.sum(partial_one, axis=1)
    total_one = over_copies(local_one, ("inner", "cell"))
    spread_two = spread_one * (1.0 + jnp.tanh(total_one / cells_all))[:, None, None]
    year_two = project(
        year_one[0],
        year_one[1],
        year_one[2],
        world_three[:, :, PERIOD:],
        PERIOD,
        spread_two,
        plans,
        fee_rate,
        ratchet,
        rollup,
    )
    inner_two = project(
        year_two[0],
        year_two[1],
        year_two[2],
        second_rates,
        2 * PERIOD,
        spread_two,
        plans,
        fee_rate,
        ratchet,
        rollup,
    )
    partial_two = jnp.sum(inner_two[3], axis=1) / paths_all
    local_two = jnp.sum(partial_two, axis=1)
    cell_reserve = sum_at_owner(jnp.stack([partial_one, partial_two]), "inner", 1)
    block_count = 4 * cells_all // BLOCK
    block_hot = (block_index[:, None] == jnp.arange(block_count)[None, :]).astype(jnp.float32)
    kept = cell_reserve.shape[1]
    block_terms = jnp.dot(
        cell_reserve.reshape(2 * kept, cells_local), block_hot, precision=lax.Precision.HIGHEST
    ).reshape(2, kept, block_count)
    block_reserve = sum_at_owner(block_terms, "cell", 2)
    discount = jnp.exp(-jnp.sum(world_rates[:, PERIOD:], axis=1))
    total_two = over_copies(local_two, ("inner", "cell"))
    losses = gather_directly((discount * total_two - total_one) / cells_all, "outer", 0)
    ordered = jnp.sort(losses)
    count_top = ordered.shape[0] // 4
    capital = jnp.mean(ordered[ordered.shape[0] - count_top :]).reshape((1,))
    return (cell_reserve, block_reserve, capital)


def solution(mesh):
    placed = (
        P("outer", "cell"),
        P("outer", "cell"),
        P("outer", "cell"),
        P(),
        P("cell"),
        P("cell"),
        P("cell"),
        P("cell"),
        P("cell"),
        P("cell"),
        P("outer", "inner", None),
        P("outer", "inner", None),
        P("outer", None),
        P("outer"),
    )
    return jax.shard_map(
        body,
        mesh=mesh,
        in_specs=placed,
        out_specs=(P(None, ("outer", "inner"), "cell"), P(None, ("outer", "inner"), "cell"), P()),
        check_vma=False,
    )
```

profile of v0, /device:TPU:1, one launch (start us, length us, event | category | flops | bytes accessed | tf_op | source)
XLA Modules:
  0.0 220.8 jit_solution(8197200616708965889)
XLA Ops:
  2.2 21.2 %all-gather = f32[16,3,4096]{2,1,0:T(4,128)S(1)} all-gather(f32[1,3,4096]{2,1,0:T(4,128)S(1)} %maximum_bitcast_fusion), channel_id=1, replica_groups=mesh['outer'=16,'inner'=4,'cell'=4] {'outer'}, dimensions={0}, use_global_device_ids=true | all-gather | bytes 835584 | tf_op jit(solution)/shard_map/all_gather | solution.py:16
  25.7 2.8 %while.150 = (s32[]{:T(128)}, f32[4,1,2048]{2,1,0:T(1,128)S(1)}, f32[4,1,2048]{2,1,0:T(1,128)S(1)}, f32[48,2048]{1,0:T(8,128)S(1)}, f32[2048]{0:T(1024)S(1)}, /*...) while((s32[]{:T(128)}, f32[4,1,2048]{2,1,0:T(1,128)S(1)}, ...), condition=%wide.region_1.2_spmd.clone, body=%wide.region_0.1_spmd.clone.sunk | while | flops 92175 | bytes 221387 | solution.py:127
  28.9 9.2 %while.151 = (s32[]{:T(128)}, f32[4,16,2048]{2,1,0:T(8,128)S(1)}, f32[4,16,2048]{2,1,0:T(8,128)S(1)}, f32[4,16,1]{1,0,2:T(4,128)S(1)}, f32[4,16,2048]{2,1,0:T(8,...) while((s32[]{:T(128)}, f32[4,16,2048]{2,1,0:T(8,128)S(1)}, ...), condition=%wide.region_3.4_spmd.clone, body=%wide.region_2.3_spmd.clone.sunk | while | flops 2361735 | bytes 4368362 | solution.py:127
  39.6 28.5 %while.146 = (s32[]{:T(128)}, f32[4,16,2048]{2,1,0:T(8,128)S(1)}, f32[4,16,2048]{2,1,0:T(8,128)S(1)}, f32[4,16,1]{1,0,2:T(4,128)S(1)}, f32[4,16,2048]{2,1,0:T(8,...) while((s32[]{:T(128)}, f32[4,16,2048]{2,1,0:T(8,128)S(1)}, ...), condition=%wide.region_5.6_spmd, body=%wide.region_4.5_spmd.sunk | while | flops 2230602 | bytes 5351453 | solution.py:127
  39.6 0.9 constant_dynamic-slice_fusion.33
  42.0 0.9 constant_dynamic-slice_fusion.33
  44.3 0.9 constant_dynamic-slice_fusion.33
  46.7 0.9 constant_dynamic-slice_fusion.33
  49.1 0.9 constant_dynamic-slice_fusion.33
  51.5 0.9 constant_dynamic-slice_fusion.33
  53.8 0.9 constant_dynamic-slice_fusion.33
  56.2 0.9 constant_dynamic-slice_fusion.33
  58.6 0.9 constant_dynamic-slice_fusion.33
  60.9 0.9 constant_dynamic-slice_fusion.33
  63.3 0.9 constant_dynamic-slice_fusion.33
  65.7 0.9 constant_dynamic-slice_fusion.33
  68.1 0.9 fusion.20
  69.0 28.4 %while.147 = (s32[]{:T(128)}, f32[4,16,2048]{2,1,0:T(8,128)S(1)}, f32[4,16,2048]{2,1,0:T(8,128)S(1)}, f32[4,16,1]{1,0,2:T(4,128)S(1)}, f32[4,16,2048]{2,1,0:T(8,...) while((s32[]{:T(128)}, f32[4,16,2048]{2,1,0:T(8,128)S(1)}, ...), condition=%wide.region_7.8_spmd, body=%wide.region_6.7_spmd.sunk | while | flops 2230602 | bytes 5351453 | solution.py:127
  69.0 0.9 constant_dynamic-slice_fusion.35
  76.1 0.9 constant_dynamic-slice_fusion.35
  98.2 13.9 %all-to-all-start = ((f32[16,1,4]{2,1,0:T(1,128)}), f32[16,1,4]{2,1,0:T(1,128)S(1)}, u32[]{:S(2)}, u32[]{:S(2)}) async-start(f32[16,1,4]{2,1,0:T(1,128)} %broadcast_in_dim.205), calls=%async_computation | async-start | bytes 16384 | tf_op jit(solution)/shard_map/all_to_all | solution.py:25
  112.4 6.7 %all-to-all-done = f32[16,1,4]{2,1,0:T(1,128)S(1)} async-done(((f32[16,1,4]{2,1,0:T(1,128)}), f32[16,1,4]{2,1,0:T(1,128)S(1)}, u32[]{:S(2)}, u32[]{:S(2)}) %all-to-all-start) | async-done | bytes 288 | tf_op jit(solution)/shard_map/all_to_all | solution.py:25
  119.2 12.9 %while.148 = (s32[]{:T(128)}, f32[4,1,2048]{2,1,0:T(1,128)S(1)}, f32[4,1,2048]{2,1,0:T(1,128)S(1)}, f32[48,2048]{1,0:T(8,128)S(1)}, f32[2048]{0:T(1024)S(1)}, /*...) while((s32[]{:T(128)}, f32[4,1,2048]{2,1,0:T(1,128)S(1)}, ...), condition=%wide.region_12.13_spmd, body=%wide.region_11.12_spmd.sunk | while | flops 83986 | bytes 246015 | solution.py:127
  119.2 0.9 dynamic-slice_subtract_fusion.4
  120.2 0.9 dynamic-slice_subtract_fusion.4
  121.3 0.9 dynamic-slice_subtract_fusion.4
  122.4 0.9 dynamic-slice_subtract_fusion.4
  123.5 0.9 dynamic-slice_subtract_fusion.4
  124.6 0.9 dynamic-slice_subtract_fusion.4
  125.6 0.9 dynamic-slice_subtract_fusion.4
  126.7 0.9 dynamic-slice_subtract_fusion.4
  127.8 0.9 dynamic-slice_subtract_fusion.4
  128.9 0.9 dynamic-slice_subtract_fusion.4
  129.9 0.9 dynamic-slice_subtract_fusion.4
  131.0 0.9 dynamic-slice_subtract_fusion.4
  132.2 19.2 %while.152 = (s32[]{:T(128)}, f32[4,16,2048]{2,1,0:T(8,128)S(1)}, f32[4,16,2048]{2,1,0:T(8,128)S(1)}, f32[4,16,1]{1,0,2:T(4,128)S(1)}, f32[4,16,2048]{2,1,0:T(8,...) while((s32[]{:T(128)}, f32[4,16,2048]{2,1,0:T(8,128)S(1)}, ...), condition=%wide.region_14.15_spmd.clone, body=%wide.region_13.14_spmd.clone.sunk | while | flops 2361735 | bytes 4368362 | solution.py:127
  143.5 0.9 constant_dynamic-slice_fusion.43
  151.6 20.6 %while.149 = (s32[]{:T(128)}, f32[4,16,2048]{2,1,0:T(8,128)S(1)}, f32[4,16,2048]{2,1,0:T(8,128)S(1)}, f32[4,16,1]{1,0,2:T(4,128)S(1)}, f32[4,16,2048]{2,1,0:T(8,...) while((s32[]{:T(128)}, f32[4,16,2048]{2,1,0:T(8,128)S(1)}, ...), condition=%wide.region_16.17_spmd, body=%wide.region_15.16_spmd.sunk | while | flops 2230601 | bytes 5351433 | solution.py:127
  173.1 4.0 %all-to-all-start.3 = ((f32[16,1,4]{2,1,0:T(1,128)}), f32[16,1,4]{2,1,0:T(1,128)S(1)}, u32[]{:S(2)}, u32[]{:S(2)}) async-start(f32[16,1,4]{2,1,0:T(1,128)} %broadcast_in_dim.212), calls=%async_computation.3 | async-start | bytes 16384 | tf_op jit(solution)/shard_map/all_to_all | solution.py:25
  177.3 6.7 %all-to-all-done.3 = f32[16,1,4]{2,1,0:T(1,128)S(1)} async-done(((f32[16,1,4]{2,1,0:T(1,128)}), f32[16,1,4]{2,1,0:T(1,128)S(1)}, u32[]{:S(2)}, u32[]{:S(2)}) %all-to-all-start.3) | async-done | bytes 288 | tf_op jit(solution)/shard_map/all_to_all | solution.py:25
  184.6 4.5 %all-to-all-start.4 = ((f32[16,1,4]{2,1,0:T(1,128)}), f32[16,1,4]{2,1,0:T(1,128)S(1)}, u32[]{:S(2)}, u32[]{:S(2)}) async-start(f32[16,1,4]{2,1,0:T(1,128)} %broadcast_in_dim.213), calls=%async_computation.4 | async-start | bytes 16384 | tf_op jit(solution)/shard_map/all_to_all | solution.py:25
  189.9 5.7 %all-to-all-done.4 = f32[16,1,4]{2,1,0:T(1,128)S(1)} async-done(((f32[16,1,4]{2,1,0:T(1,128)}), f32[16,1,4]{2,1,0:T(1,128)S(1)}, u32[]{:S(2)}, u32[]{:S(2)}) %all-to-all-start.4) | async-done | bytes 288 | tf_op jit(solution)/shard_map/all_to_all | solution.py:25
  195.5 5.4 %all-to-all-start.1 = ((f32[4,2,1,2048]{3,1,2,0:T(2,128)}), f32[4,2,1,2048]{3,1,2,0:T(2,128)S(1)}, u32[]{:S(2)}, u32[]{:S(2)}) async-start(f32[4,2,1,2048]{3,1,2,0:T(2,128)} %maximum_bitcast_fusion.1), calls=%async_computation.1 | async-start | bytes 131072 | tf_op jit(solution)/shard_map/all_to_all | solution.py:42
  202.2 2.1 sort.15
  204.3 3.8 %all-to-all-done.1 = f32[4,2,1,2048]{3,1,2,0:T(2,128)S(1)} async-done(((f32[4,2,1,2048]{3,1,2,0:T(2,128)}), f32[4,2,1,2048]{3,1,2,0:T(2,128)S(1)}, u32[]{:S(2)}, u32[]{:S(2)}) %all-to-all-start.1) | async-done | bytes 65568 | tf_op jit(solution)/shard_map/all_to_all | solution.py:42
  208.1 1.4 fusion.31
  210.2 3.2 %all-to-all-start.2 = ((f32[4,1,128]{2,1,0:T(1,128)}), f32[4,1,128]{2,1,0:T(1,128)S(1)}, u32[]{:S(2)}, u32[]{:S(2)}) async-start(f32[4,1,128]{2,1,0:T(1,128)} %reshape.339), calls=%async_computation.2 | async-start | bytes 4096 | tf_op jit(solution)/shard_map/all_to_all | solution.py:42
  215.4 2.4 %all-to-all-done.2 = f32[4,1,128]{2,1,0:T(1,128)S(1)} async-done(((f32[4,1,128]{2,1,0:T(1,128)}), f32[4,1,128]{2,1,0:T(1,128)S(1)}, u32[]{:S(2)}, u32[]{:S(2)}) %all-to-all-start.2) | async-done | bytes 2080 | tf_op jit(solution)/shard_map/all_to_all | solution.py:42
  (520 shorter events, 108.6 us)
Async XLA Ops:
  0.6 24.7 %copy-start = (f32[16,48]{1,0:T(8,128)S(1)}, f32[16,48]{1,0:T(8,128)}, u32[]{:S(2)}) copy-start(f32[16,48]{1,0:T(8,128)} %param.31) | copy-start | bytes 9220
  23.8 0.7 copy-start.11
  23.8 1.4 copy-start.10
  23.9 1.4 copy-start.3
  23.9 1.4 copy-start.13
  23.9 1.8 copy-start.14
  23.9 1.8 copy-start.1
  23.9 1.8 copy-start.6
  24.0 4.7 %copy-start.8 = (f32[4,16,36]{2,1,0:T(8,128)S(1)}, f32[4,16,36]{2,1,0:T(8,128)}, u32[]{:S(2)}) copy-start(f32[4,16,36]{2,1,0:T(8,128)} %param.38) | copy-start | bytes 27652
  25.3 14.1 %copy-start.4 = (f32[2048]{0:T(1024)}, f32[2048]{0:T(1024)S(1)}, u32[]{:S(2)}) copy-start(f32[2048]{0:T(1024)S(1)} %get-tuple-element.2887) | copy-start | bytes 24580
  38.0 0.7 copy-start.2
  38.8 0.6 copy-start.7
  69.0 43.2 %copy-start.15 = (f32[4,1,12]{2,0,1:T(4,128)S(1)}, f32[4,1,12]{2,0,1:T(4,128)}, u32[]{:S(2)}) copy-start(f32[4,1,12]{2,0,1:T(4,128)} %get-tuple-element.2889) | copy-start | bytes 580
  69.0 43.3 %copy-start.9 = (f32[4,16,24]{2,1,0:T(8,128)S(1)}, f32[4,16,24]{2,1,0:T(8,128)}, u32[]{:S(2)}) copy-start(f32[4,16,24]{2,1,0:T(8,128)} %param.39) | copy-start | bytes 18436
  97.4 34.6 %copy-start.5 = (f32[2048]{0:T(1024)S(1)}, f32[2048]{0:T(1024)}, u32[]{:S(2)}) copy-start(f32[2048]{0:T(1024)} %copy-done.4) | copy-start | bytes 24580
  98.2 20.9 %all-to-all-start = ((f32[16,1,4]{2,1,0:T(1,128)}), f32[16,1,4]{2,1,0:T(1,128)S(1)}, u32[]{:S(2)}, u32[]{:S(2)}) async-start(f32[16,1,4]{2,1,0:T(1,128)} %broadcast_in_dim.205), calls=%async_computation | async-start | bytes 16384 | tf_op jit(solution)/shard_map/all_to_all | solution.py:25
  151.6 25.4 %copy-start.12 = (f32[4,24]{1,0:T(4,128)S(1)}, f32[4,24]{1,0:T(4,128)}, u32[]{:S(2)}) copy-start(f32[4,24]{1,0:T(4,128)} %param.40) | copy-start | bytes 1156
  172.2 35.9 %copy-start.16 = (s32[2048]{0:T(1024)S(1)}, s32[2048]{0:T(1024)}, u32[]{:S(2)}) copy-start(s32[2048]{0:T(1024)} %param.34) | copy-start | bytes 24580
  173.1 10.9 %all-to-all-start.3 = ((f32[16,1,4]{2,1,0:T(1,128)}), f32[16,1,4]{2,1,0:T(1,128)S(1)}, u32[]{:S(2)}, u32[]{:S(2)}) async-start(f32[16,1,4]{2,1,0:T(1,128)} %broadcast_in_dim.212), calls=%async_computation.3 | async-start | bytes 16384 | tf_op jit(solution)/shard_map/all_to_all | solution.py:25
  184.6 10.9 %all-to-all-start.4 = ((f32[16,1,4]{2,1,0:T(1,128)}), f32[16,1,4]{2,1,0:T(1,128)S(1)}, u32[]{:S(2)}, u32[]{:S(2)}) async-start(f32[16,1,4]{2,1,0:T(1,128)} %broadcast_in_dim.213), calls=%async_computation.4 | async-start | bytes 16384 | tf_op jit(solution)/shard_map/all_to_all | solution.py:25
  195.5 12.5 %all-to-all-start.1 = ((f32[4,2,1,2048]{3,1,2,0:T(2,128)}), f32[4,2,1,2048]{3,1,2,0:T(2,128)S(1)}, u32[]{:S(2)}, u32[]{:S(2)}) async-start(f32[4,2,1,2048]{3,1,2,0:T(2,128)} %maximum_bitcast_fusion.1), calls=%async_computation.1 | async-start | bytes 131072 | tf_op jit(solution)/shard_map/all_to_all | solution.py:42
  210.2 7.6 %all-to-all-start.2 = ((f32[4,1,128]{2,1,0:T(1,128)}), f32[4,1,128]{2,1,0:T(1,128)S(1)}, u32[]{:S(2)}, u32[]{:S(2)}) async-start(f32[4,1,128]{2,1,0:T(1,128)} %reshape.339), calls=%async_computation.2 | async-start | bytes 4096 | tf_op jit(solution)/shard_map/all_to_all | solution.py:42
where the time goes:
time: 225 us; the launch traced here: 221 us
  other arithmetic  83.8 us (37%)
  local copies, waits for them, and re-layouts  50.7 us (23%)
  starting transfers between devices  31 us (14%)
  waiting for transfers between devices  25.3 us (11%)
  blocking collectives  21.2 us (9%)
  loops' own time  4.12 us (2%)
  between operations  2.9 us (1%)
    dynamic_slice x60, local copies, waits for them, and re-layouts, advance(): lax.dynamic_index_in_dim(lapse_base, calendar, 0, False)  41.4 us
    add x60, other arithmetic, month_step(): present = present + jnp.exp(-log_discount) * claims  24.7 us
    all_to_all x3, starting transfers between devices, from_everyone(): lax.all_to_all(jnp.broadcast_to(value[None], (devices, *value.shape)), ax...  22.4 us
    all_gather x1, blocking collectives, sent_together(): lax.all_gather(both, axis, axis=dim, tiled=True)  21.2 us
    mul x60, other arithmetic, month_step(): present = present + jnp.exp(-log_discount) * claims  20.7 us
    all_to_all x3, waiting for transfers between devices, from_everyone(): lax.all_to_all(jnp.broadcast_to(value[None], (devices, *value.shape)), ax...  19.1 us
    mul x84, other arithmetic, month_step(): surviving = surviving * (1.0 - mortality - lapse_rate)  18.3 us
    sub x84, other arithmetic, month_step(): surviving = surviving * (1.0 - mortality - lapse_rate)  10.8 us
  transfers between devices with their start and end apart: 5, of which 5 were waited for; matrix products, arithmetic and copies ran while one was open for 3% of the time, Pallas kernels for 0%

commit v1 on v0

v1 whole, which is shorter than its diff:
```python
import functools

import jax
import jax.numpy as jnp
from jax import lax
from jax.experimental import pallas as pl
from jax.experimental.pallas import tpu as pltpu
from jax.sharding import PartitionSpec as P

PERIOD = 12
LANES = 128
SUBLANES = 8

credit_floor = 0.001
rollup_growth = 0.05
ALL = ("outer", "inner", "cell")

FEE, KEPT, ACCOUNT, GUARANTEE, RATCHET, ROLLUP = range(6)
S_ACCOUNT, S_SURVIVING, S_GUARANTEE = range(3)


def row_of(month, each):
    return month // each, month % each


def world_year(start, each, plan, level, low, high, lapse, cells, state, credit):
    fee, kept = cells[FEE : FEE + 1, :], cells[KEPT : KEPT + 1, :]
    ratchet, rollup = cells[RATCHET : RATCHET + 1, :], cells[ROLLUP : ROLLUP + 1, :]
    account, surviving, guarantee = state
    per_guarantee = 1.0 / guarantee
    for m in range(start, start + PERIOD):
        d, r = row_of(m, each)
        flow = plan[d, r : r + 1, :]
        death = plan[d, each + r : each + r + 1, :]
        account = jnp.maximum(account + flow * per_guarantee, 0.0) * credit(m)
        bounded = jnp.minimum(jnp.maximum(account, low[m : m + 1, :]), high[m : m + 1, :])
        surviving = surviving * (kept - fee * death - lapse[m : m + 1, :] * bounded)
    unit = level[start + PERIOD - 1 : start + PERIOD, :]
    growth = jnp.maximum(ratchet * (account / unit), 1.0 + rollup_growth * rollup)
    account = jnp.where(ratchet > 0.5, jnp.minimum(account, unit), account / growth)
    return account, surviving, guarantee * growth


def inner_paths(
    start, months, each, plan, level, low, high, lapse, cells, rows, credit, discount, kept_accounts, kept_growth, reserve
):
    groups = credit.shape[1] // SUBLANES
    paths = credit.shape[1]
    years = months // PERIOD

    def tile_step(t, total):
        tile = pl.ds(pl.multiple_of(t * LANES, LANES), LANES)

        def spread_out(ref, r):
            return jnp.broadcast_to(ref[pl.ds(r, 1), tile], (SUBLANES, LANES))

        def planned(m, second):
            d, r = row_of(m, each)
            return jnp.broadcast_to(plan[d, pl.ds(r + second * each, 1), tile], (SUBLANES, LANES))

        def group(ref, m, g):
            return ref[m, SUBLANES * g : SUBLANES * (g + 1), :]

        fee, kept = spread_out(cells, FEE), spread_out(cells, KEPT)
        ratchet, rollup = spread_out(cells, RATCHET), spread_out(cells, ROLLUP)
        grown = 1.0 + rollup_growth * rollup
        shrunk = 1.0 / grown
        begin = spread_out(rows, S_ACCOUNT)
        guarantee = spread_out(rows, S_GUARANTEE)
        base = 1.0 / guarantee
        account = [begin] * groups
        per_guarantee = [base] * groups
        for y in range(years):
            for s in range(PERIOD):
                o = y * PERIOD + s
                flow = planned(start + o, 0)
                if y == 0:
                    flow = flow * base
                for g in range(groups):
                    term = flow if y == 0 else flow * per_guarantee[g]
                    account[g] = jnp.maximum(account[g] + term, 0.0) * group(credit, o, g)
                    kept_accounts[o, SUBLANES * g : SUBLANES * (g + 1), :] = account[g]
            if y + 1 < years:
                unit = spread_out(level, start + y * PERIOD + PERIOD - 1)
                per_unit = ratchet / unit
                cap = jnp.where(ratchet > 0.5, unit, 1e30)
                for g in range(groups):
                    growth = jnp.maximum(per_unit * account[g], grown)
                    kept_growth[y, SUBLANES * g : SUBLANES * (g + 1), :] = growth
                    per_guarantee[g] = per_guarantee[g] / growth
                    account[g] = jnp.minimum(account[g], cap) * shrunk
                    kept_growth[years + y, SUBLANES * g : SUBLANES * (g + 1), :] = account[g]
        worth = [None] * groups
        for o in reversed(range(months)):
            m = start + o
            unit, least, most = spread_out(level, m), spread_out(low, m), spread_out(high, m)
            lapsing = spread_out(lapse, m)
            death = planned(m, 1)
            staying = kept - fee * death
            for g in range(groups):
                after = group(kept_accounts, o, g)
                if o == 0:
                    before = begin
                elif o % PERIOD == 0:
                    before = group(kept_growth, years + o // PERIOD - 1, g)
                else:
                    before = group(kept_accounts, o - 1, g)
                value = death * jnp.maximum(unit - after, 0.0) - before
                if worth[g] is not None:
                    later = worth[g]
                    if (o + 1) % PERIOD == 0:
                        later = later * group(kept_growth, o // PERIOD, g)
                    bounded = jnp.minimum(jnp.maximum(after, least), most)
                    value = value + (staying - lapsing * bounded) * later
                worth[g] = value * group(discount, o, g)
        summed = worth[0]
        for g in range(1, groups):
            summed = summed + worth[g]
        scale = guarantee * spread_out(rows, S_SURVIVING) * (1.0 / paths)
        row = jnp.sum(summed * scale, axis=0, keepdims=True)
        reserve[0:1, tile] = row
        return total + row

    tiles = reserve.shape[1] // LANES
    return lax.fori_loop(0, tiles, tile_step, jnp.zeros((1, LANES), jnp.float32))


def first_kernel(
    each, credit_world, spread, plan, level, low, high, lapse, cells, rates,
    reserve, rows, total, credit, discount, kept_accounts, kept_growth,
):
    months = credit.shape[0]
    crediting = 1.0 + jnp.maximum(rates[...] - spread[0], credit_floor)
    discounting = jnp.exp(-rates[...])
    for m in range(months):
        credit[m] = jnp.broadcast_to(crediting[:, m : m + 1], credit.shape[1:])
        discount[m] = jnp.broadcast_to(discounting[:, m : m + 1], credit.shape[1:])
    fee, guarantee = cells[FEE : FEE + 1, :], cells[GUARANTEE : GUARANTEE + 1, :]
    account = fee * cells[ACCOUNT : ACCOUNT + 1, :] / guarantee
    state = (account, jnp.ones_like(account), guarantee)
    state = world_year(0, each, plan, level, low, high, lapse, cells, state, lambda m: credit_world[m])
    for r, value in enumerate(state):
        rows[r : r + 1, :] = value
    total[...] = inner_paths(
        PERIOD, months, each, plan, level, low, high, lapse, cells, rows, credit, discount, kept_accounts, kept_growth, reserve
    )


def second_kernel(
    each, cells_all, block_count, world, spread, place, total_one, next_one, next_two, next_three,
    plan, level, low, high, lapse, cells, rates, rows_one, reserve_one, block_hot,
    reserves, parcel, rows, reserve, credit, discount, kept_accounts, kept_growth, parts,
):
    months = credit.shape[0]
    whole = total_one[...] + next_one[...] + next_two[...] + next_three[...]
    mean = jnp.broadcast_to(jnp.sum(whole, axis=1, keepdims=True), (1, LANES)) / cells_all
    spread_two = (spread[0] * (1.0 + jnp.tanh(mean)))[0, 0]
    crediting = 1.0 + jnp.maximum(rates[...] - spread_two, credit_floor)
    discounting = jnp.exp(-rates[...])
    first = rates.shape[1] - months
    for m in range(months):
        credit[m] = jnp.broadcast_to(crediting[:, first + m : first + m + 1], credit.shape[1:])
        discount[m] = jnp.broadcast_to(discounting[:, first + m : first + m + 1], credit.shape[1:])
    state = tuple(rows_one[r : r + 1, :] for r in range(3))
    state = world_year(
        PERIOD, each, plan, level, low, high, lapse, cells, state,
        lambda m: 1.0 + jnp.maximum(world[m] - spread_two, credit_floor),
    )
    for r, value in enumerate(state):
        rows[r : r + 1, :] = value
    total_two = inner_paths(
        2 * PERIOD, months, each, plan, level, low, high, lapse, cells, rows, credit, discount, kept_accounts, kept_growth, reserve
    )
    parts[...] = jnp.zeros_like(parts)
    for d, source in enumerate((reserve_one, reserve)):
        value = source[0:1, :]
        reserves[d] = value
        for part in range(3):
            rounded = value.astype(jnp.bfloat16).astype(jnp.float32)
            parts[3 * d + part : 3 * d + part + 1, :] = rounded
            value = value - rounded
    sums = jnp.dot(parts[...].astype(jnp.bfloat16), block_hot[...], preferred_element_type=jnp.float32)
    first_sums = sums[0:1, :] + sums[1:2, :] + sums[2:3, :]
    second_sums = sums[3:4, :] + sums[4:5, :] + sums[5:6, :]
    rate_sum = world[PERIOD]
    for m in range(PERIOD + 1, 2 * PERIOD):
        rate_sum = rate_sum + world[m]
    discount_world = jnp.exp(jnp.full((1, LANES), -rate_sum, jnp.float32))
    local = discount_world * total_two - total_one[...]
    loss = jnp.broadcast_to(jnp.sum(local, axis=1, keepdims=True), (1, LANES)) / cells_all
    lane = lax.broadcasted_iota(jnp.int32, (1, LANES), 1)
    loss = jnp.where(lane == place[0], loss, 0.0)
    owners = parcel.shape[1]
    kept = block_count // owners
    for k in range(owners):
        blocks = jnp.concatenate(
            [first_sums[:, kept * k : kept * (k + 1)], second_sums[:, kept * k : kept * (k + 1)]], axis=1
        )
        both = jnp.concatenate([blocks, loss], axis=0)
        parcel[:, k] = jnp.broadcast_to(both[None], (parcel.shape[0], 2, LANES))


def last_kernel(place, received, block_reserve, capital):
    outers, owners = received.shape[0], received.shape[1]
    losses = received[:, 0, 1, :]
    for k in range(1, owners):
        losses = losses + received[:, k, 1, :]
    across = jnp.sum(losses, axis=0, keepdims=True)
    down = jnp.sum(losses, axis=1, keepdims=True)
    lane = lax.broadcasted_iota(jnp.int32, losses.shape, 1)
    place_down = lax.broadcasted_iota(jnp.int32, losses.shape, 0)
    ahead = (across > down) | ((across == down) & (lane < place_down))
    ahead = ahead & (lane < outers)
    rank = jnp.sum(jnp.where(ahead, 1.0, 0.0), axis=1, keepdims=True)
    count_top = outers // 4
    chosen = jnp.where(rank < count_top - 0.5, down, 0.0)
    capital[...] = jnp.broadcast_to(jnp.sum(chosen, axis=0, keepdims=True) / count_top, capital.shape)
    blocks = received[place[0], 0, 0:1, :]
    for k in range(1, owners):
        blocks = blocks + received[place[0], k, 0:1, :]
    kept = block_reserve.shape[2]
    for d in range(2):
        block_reserve[d] = blocks[:, kept * d : kept * (d + 1)]


VMEM = pl.BlockSpec(memory_space=pltpu.VMEM)
SMEM = pl.BlockSpec(memory_space=pltpu.SMEM)
LIMIT = pltpu.CompilerParams(vmem_limit_bytes=48 * 1024 * 1024)


def body(
    premium,
    charge,
    mortality,
    lapse_table,
    lapse_index,
    guarantee_type,
    block_index,
    account_start,
    guarantee_start,
    fee_rate,
    first_rates,
    second_rates,
    world_rates,
    spread,
):
    f32 = jnp.float32
    outer_size, inner_size, cell_size = (lax.axis_size(a) for a in ALL)
    each, local = premium.shape
    months_all = each * outer_size
    inner_at = lax.axis_index("inner")
    place = lax.axis_index("outer") * inner_size + inner_at
    paths = first_rates.shape[1] * inner_size
    months_one, months_two = first_rates.shape[2], second_rates.shape[2]
    cells_all = local * cell_size
    block_count = 4 * cells_all // LANES

    fee = fee_rate[None, :]
    fee_log = jnp.log1p(-fee)

    def scale_of(month):
        return fee * jnp.exp(-(month.astype(f32)[:, None] + 1.0) * fee_log)

    own_months = lax.axis_index("outer") * each + jnp.arange(each)
    flow = (premium - charge) * scale_of(own_months)
    death = mortality * ((1.0 - fee) / fee)
    sent = jnp.concatenate([flow, death], axis=0)
    sent = jnp.broadcast_to(sent[None], (outer_size, *sent.shape))
    plan = lax.all_to_all(sent, "outer", 0, 0, tiled=True)
    rates = lax.all_to_all(jnp.concatenate([first_rates, second_rates], axis=2), "inner", 0, 0, tiled=True)
    rates = rates.reshape(paths, months_one + months_two)

    level = scale_of(jnp.arange(months_all))
    tables = jnp.arange(lapse_table.shape[0])
    lapse_hot = (lapse_index[None, :] == tables[:, None]).astype(f32)
    lapse = jnp.dot(lapse_table.T, lapse_hot, precision=lax.Precision.HIGHEST) * ((1.0 - fee) / level)
    low, high = 0.5 * level, 1.5 * level
    cells = jnp.stack(
        [
            fee_rate,
            1.0 - fee_rate,
            account_start,
            guarantee_start,
            (guarantee_type == 1).astype(f32),
            (guarantee_type == 2).astype(f32),
        ]
    )
    world = lax.dynamic_index_in_dim(world_rates, inner_at, 0, False)
    spread_own = lax.dynamic_slice_in_dim(spread, inner_at, 1, 0)
    credit_world = 1.0 + jnp.maximum(world - spread_own, credit_floor)
    place_own = place.astype(jnp.int32).reshape(1)
    block_hot = (block_index[:, None] == jnp.arange(block_count)[None, :]).astype(jnp.bfloat16)

    row = jax.ShapeDtypeStruct((1, local), f32)

    def inner_scratch(months):
        years = months // PERIOD
        return [
            pltpu.VMEM((months, paths, LANES), f32),
            pltpu.VMEM((months, paths, LANES), f32),
            pltpu.VMEM((months, paths, LANES), f32),
            pltpu.VMEM((2 * years, paths, LANES), f32),
        ]

    reserve_one, rows_one, total_one = pl.pallas_call(
        functools.partial(first_kernel, each),
        out_shape=(row, jax.ShapeDtypeStruct((3, local), f32), jax.ShapeDtypeStruct((1, LANES), f32)),
        in_specs=[SMEM] * 2 + [VMEM] * 7,
        out_specs=[VMEM] * 3,
        scratch_shapes=inner_scratch(months_one),
        compiler_params=LIMIT,
        name="first_date",
    )(credit_world, spread_own, plan, level, low, high, lapse, cells, rates)

    others = [
        lax.ppermute(total_one, "cell", [(k, (k + s) % cell_size) for k in range(cell_size)])
        for s in range(1, cell_size)
    ]

    reserves, parcel = pl.pallas_call(
        functools.partial(second_kernel, each, cells_all, block_count),
        out_shape=(
            jax.ShapeDtypeStruct((2, 1, local), f32),
            jax.ShapeDtypeStruct((outer_size * inner_size, cell_size, 2, LANES), f32),
        ),
        in_specs=[SMEM] * 3 + [VMEM] * 14,
        out_specs=[VMEM] * 2,
        scratch_shapes=[pltpu.VMEM((3, local), f32), pltpu.VMEM((1, local), f32)]
        + inner_scratch(months_two)
        + [pltpu.VMEM((SUBLANES, local), f32)],
        compiler_params=LIMIT,
        name="second_date",
    )(
        world, spread_own, place_own, total_one, *others,
        plan, level, low, high, lapse, cells, rates, rows_one, reserve_one, block_hot,
    )

    received = lax.all_to_all(parcel.reshape(-1, 2, LANES), ALL, 0, 0, tiled=True)
    block_reserve, capital = pl.pallas_call(
        last_kernel,
        out_shape=(
            jax.ShapeDtypeStruct((2, 1, block_count // cell_size), f32),
            jax.ShapeDtypeStruct((1, LANES), f32),
        ),
        in_specs=[SMEM, VMEM],
        out_specs=[VMEM] * 2,
        compiler_params=LIMIT,
        name="last_sums",
    )(place_own, received.reshape(parcel.shape))
    return reserves, block_reserve, capital[0, :1]


def solution(mesh):
    placed = (
        P("outer", "cell"),
        P("outer", "cell"),
        P("outer", "cell"),
        P(),
        P("cell"),
        P("cell"),
        P("cell"),
        P("cell"),
        P("cell"),
        P("cell"),
        P("outer", "inner", None),
        P("outer", "inner", None),
        P("outer", None),
        P("outer"),
    )
    return jax.shard_map(
        body,
        mesh=mesh,
        in_specs=placed,
        out_specs=(P(None, ("outer", "inner"), "cell"), P(None, ("outer", "inner"), "cell"), P()),
        check_vma=False,
    )
```

time: 225 us -> 99.9 us (0.44); the launches traced: 221 us -> 99.2 us
  other arithmetic: 83.8 us -> 5.74 us
  local copies, waits for them, and re-layouts: 50.7 us -> 4.77 us
  Pallas kernels: 0 us -> 21.7 us
  starting transfers between devices: 31 us -> 19.6 us
  waiting for transfers between devices: 25.3 us -> 18.6 us
  blocking collectives: 21.2 us -> 27.7 us
  loops' own time: 4.12 us -> 0 us
    dynamic_slice x144 -> x1, local copies, waits for them, and re-layouts: 42.6 us -> 1.24 us  [body(): spread_own = lax.dynamic_slice_in_dim(spread, inner_at, 1, 0)]
    mul x170 -> x2, other arithmetic: 39.4 us -> 1.08 us  [the longest x1 0.89 us: body(): flow = (premium - charge) * scale_of(own_months)]
    all_to_all x0 -> x1, blocking collectives: none -> 27.7 us  [body(): lax.all_to_all(parcel.reshape(-1, 2, LANES), ALL, 0, 0, tiled=True)]
    add x64 -> x1, other arithmetic: 25.9 us -> 1.34 us  [body(): credit_world = 1.0 + jnp.maximum(world - spread_own, credit_floor)]
    pallas_call x0 -> x3, Pallas kernels: none -> 21.7 us  [the longest x1 11.8 us: body(): pl.pallas_call(functools.partial(first_kernel, each), out_shape=(row, jax...]
    all_gather x1 -> x0, blocking collectives: 21.2 us -> none  [sent_together(): lax.all_gather(both, axis, axis=dim, tiled=True)]
    all_to_all x5 -> x2, starting transfers between devices: 31 us -> 16.9 us  [the longest x1 9.96 us: body(): lax.all_to_all(jnp.concatenate([first_rates, second_rates], axis=2), 'inn...]
    sub x85 -> x1, other arithmetic: 11.6 us -> 0.71 us  [body(): death = mortality * ((1.0 - fee) / fee)]
  transfers between devices with their start and end apart: 5 -> 5, of which waited for: 5 -> 4; matrix products, arithmetic and copies ran while one was open for 3% -> 7% of each run, Pallas kernels for 0% -> 0%
where the time goes in v1:
time: 99.9 us; the launch traced here: 99.2 us
  blocking collectives  27.7 us (28%)
  Pallas kernels  21.7 us (22%)
  starting transfers between devices  19.6 us (20%)
  waiting for transfers between devices  18.6 us (19%)
  other arithmetic  5.74 us (6%)
  local copies, waits for them, and re-layouts  4.77 us (5%)
    all_to_all x1, blocking collectives, body(): lax.all_to_all(parcel.reshape(-1, 2, LANES), ALL, 0, 0, tiled=True)  27.7 us
    all_to_all x1, waiting for transfers between devices, body(): plan = lax.all_to_all(sent, 'outer', 0, 0, tiled=True)  13.4 us
    pallas_call x1, Pallas kernels, body(): pl.pallas_call(functools.partial(first_kernel, each), out_shape=(row, jax...  11.8 us
    all_to_all x1, starting transfers between devices, body(): lax.all_to_all(jnp.concatenate([first_rates, second_rates], axis=2), 'inn...  9.96 us
    pallas_call x1, Pallas kernels, body(): pl.pallas_call(functools.partial(second_kernel, each, cells_all, block_co...  9.08 us
    all_to_all x1, starting transfers between devices, body(): plan = lax.all_to_all(sent, 'outer', 0, 0, tiled=True)  6.9 us
    ppermute x3, waiting for transfers between devices, body(): lax.ppermute(total_one, 'cell', [(k, (k + s) % cell_size) for k in range(...  3.09 us
    ppermute x3, starting transfers between devices, body(): lax.ppermute(total_one, 'cell', [(k, (k + s) % cell_size) for k in range(...  2.74 us
  transfers between devices with their start and end apart: 5, of which 4 were waited for; matrix products, arithmetic and copies ran while one was open for 7% of the time, Pallas kernels for 0%

profile of v1, /device:TPU:1, one launch (start us, length us, event | category | flops | bytes accessed | tf_op | source)
XLA Modules:
  0.0 99.2 jit_solution(11407915404709528364)
XLA Ops:
  0.6 0.0 copy-start
  0.6 0.9 pad_maximum_fusion.1
  1.5 0.7 reshape.52
  2.2 10.0 %all-to-all-start.1 = ((f32[4,1,960]{2,1,0:T(1,128)}), f32[4,1,960]{2,1,0:T(1,128)S(1)}, u32[]{:S(2)}, u32[]{:S(2)}) async-start(f32[4,1,960]{2,1,0:T(1,128)} %reshape.52), calls=%async_computation.1 | async-start | bytes 32768 | tf_op jit(solution)/shard_map/all_to_all | solution.py:270
  12.2 0.7 compare_convert_fusion
  12.9 0.7 broadcast_subtract_fusion
  13.6 1.2 %dynamic_slice.8.spread = f32[1]{0:T(128)} dynamic-slice(f32[4]{0:T(128)} %param.27, s32[]{:T(128)S(6)} %select_n.5), dynamic_slice_sizes={1} | dynamic-slice | bytes 12 | tf_op jit(solution)/shard_map/dynamic_slice | solution.py:289
  14.8 0.9 multiply_multiply_fusion
  15.8 1.3 %maximum_add_fusion = (f32[24]{0:T(128)S(1)}, f32[24]{0:T(128)S(1)}) fusion(f32[]{:T(128)} %bitcast.2, f32[4,24]{1,0:T(4,128)} %param.26, s32[]{:T(128)S(6)} %select_n.5), kind=kLoop, calls=%fused_computation.20 | loop fusion | flops 72 | bytes 296 | tf_op jit(solution)/shard_map/add | solution.py:290
  17.1 2.1 %all-to-all-done.1 = f32[4,1,960]{2,1,0:T(1,128)S(1)} async-done(((f32[4,1,960]{2,1,0:T(1,128)}), f32[4,1,960]{2,1,0:T(1,128)S(1)}, u32[]{:S(2)}, u32[]{:S(2)}) %all-to-all-start.1) | async-done | bytes 15392 | tf_op jit(solution)/shard_map/all_to_all | solution.py:270
  19.2 1.1 %broadcast_in_dim.4 = f32[16,6,2048]{2,1,0:T(8,128)} broadcast(f32[6,2048]{1,0:T(8,128)S(1)} %pad_maximum_fusion), dimensions={1,2} | broadcast | bytes 835584 | tf_op jit(solution)/shard_map/broadcast_in_dim | solution.py:268
  20.3 0.0 copy-start.3
  20.3 0.0 copy-start.5
  20.3 0.0 copy-start.6
  20.3 0.0 copy-start.7
  20.3 6.9 %all-to-all-start = ((f32[16,6,2048]{2,1,0:T(8,128)}), f32[16,6,2048]{2,1,0:T(8,128)S(1)}, u32[]{:S(2)}, u32[]{:S(2)}) async-start(f32[16,6,2048]{2,1,0:T(8,128)} %broadcast_in_dim.4), calls=%async_computation | async-start | bytes 2097152 | tf_op jit(solution)/shard_map/all_to_all | solution.py:269
  27.2 0.0 copy-done.3
  27.2 0.0 copy-done.5
  27.3 0.0 copy-done.6
  27.3 0.1 stack.32.cells
  27.4 0.0 copy-done
  27.4 0.0 copy-done.7
  27.4 0.4 fusion.lapse
  27.8 0.0 copy-start.1
  27.8 0.2 fusion.2
  28.0 0.5 broadcast.44
  28.5 0.7 reduce
  29.2 0.1 reshape.53
  29.3 13.4 %all-to-all-done.plan = f32[16,6,2048]{2,1,0:T(8,128)S(1)} async-done(((f32[16,6,2048]{2,1,0:T(8,128)}), f32[16,6,2048]{2,1,0:T(8,128)S(1)}, u32[]{:S(2)}, u32[]{:S(2)}) %all-to-all-start) | async-done | bytes 786464 | tf_op jit(solution)/shard_map/all_to_all | solution.py:269
  42.7 0.0 copy-start.4
  42.7 11.8 %first_date.1 = (f32[1,2048]{1,0:T(1,128)S(1)}, f32[3,2048]{1,0:T(4,128)S(1)}, f32[1,128]{1,0:T(1,128)S(1)}) custom-call(f32[24]{0:T(128)S(1)} %get-tuple-element.17.credit_world, f32[1]{0:T(128)} %dynamic_slice.8.spread, f32[16,6,2048]{2,1,0:T(8,128)S(1)} %all-to-all-done.plan, f32[48,2048]{1,0:T(8,128)S(1)} %get-tuple-element.21.level, ...), custom_call_target="tpu_custom_call" | custom-call | tf_op jit(solution)/shard_map/first_date/pallas_call | solution.py:305
  54.5 0.0 copy-done.1
  54.5 1.7 %collective-permute-start.2 = (f32[1,128]{1,0:T(1,128)S(1)}, f32[1,128]{1,0:T(1,128)S(1)}, u32[]{:S(2)}, u32[]{:S(2)}) collective-permute-start(f32[1,128]{1,0:T(1,128)S(1)} %get-tuple-element.10.total_one), channel_id=1, source_target_pairs={{0,3},{1,0},{2,1},{3,2},{4,7},{5,4},{6,5},{7,6},{8,11},{9,8},{10,9... | collective-permute-start | bytes 1544 | tf_op jit(solution)/shard_map/ppermute | solution.py:316
  56.2 0.3 collective-permute-start.1
  56.5 0.7 collective-permute-start
  57.3 0.0 copy-done.4
  57.3 0.3 fusion.1.block_hot
  57.6 0.0 collective-permute-done.2.next_three
  57.6 1.9 %collective-permute-done.1.next_two = f32[1,128]{1,0:T(1,128)S(1)} collective-permute-done((f32[1,128]{1,0:T(1,128)S(1)}, f32[1,128]{1,0:T(1,128)S(1)}, u32[]{:S(2)}, u32[]{:S(2)}) %collective-permute-start.1) | collective-permute-done | bytes 544 | tf_op jit(solution)/shard_map/ppermute | solution.py:316
  59.5 1.2 %collective-permute-done.next_one = f32[1,128]{1,0:T(1,128)S(1)} collective-permute-done((f32[1,128]{1,0:T(1,128)S(1)}, f32[1,128]{1,0:T(1,128)S(1)}, u32[]{:S(2)}, u32[]{:S(2)}) %collective-permute-start) | collective-permute-done | bytes 544 | tf_op jit(solution)/shard_map/ppermute | solution.py:316
  60.7 0.0 copy-start.2
  60.7 1.0 %copy-done.2 = f32[48,2048]{1,0:T(8,128)S(1)} copy-done((f32[48,2048]{1,0:T(8,128)S(1)}, f32[48,2048]{1,0:T(8,128)}, u32[]{:S(2)}) %copy-start.2) | copy-done | bytes 393240
  61.7 9.1 %second_date.1 = (f32[2,1,2048]{2,1,0:T(1,128)}, f32[64,4,2,128]{3,2,1,0:T(2,128)S(1)}) custom-call(f32[24]{0:T(128)S(1)} %get-tuple-element.18.world, f32[1]{0:T(128)} %dynamic_slice.8.spread, s32[1]{0:T(128)} %bitcast.1.place, f32[1,128]{1,0:T(1,128)S(1)} %get-tuple-element.10.total_one, f32[1,128]{1,0:T(1,128)S(1)} %collective-permute-done.next_one, ...), custom_call_target="tpu_custom_call" | custom-call | tf_op jit(solution)/shard_map/second_date/pallas_call | solution.py:320
  70.8 27.7 %all_to_all.15 = f32[256,2,128]{2,1,0:T(2,128)S(1)} all-to-all(f32[256,2,128]{2,1,0:T(2,128)S(1)} %bitcast.24), channel_id=1, replica_groups=mesh['outer'=16,'inner'=4,'cell'=4] {'outer','inner','cell'}, dimensions={0} | all-to-all | bytes 524288 | tf_op jit(solution)/shard_map/all_to_all | solution.py:338
  98.4 0.8 last_sums.1
  (3 shorter events, 0.0 us)
Async XLA Ops:
  0.6 26.7 %copy-start = (f32[16,48]{1,0:T(8,128)S(1)}, f32[16,48]{1,0:T(8,128)}, u32[]{:S(2)}) copy-start(f32[16,48]{1,0:T(8,128)} %param.17) | copy-start | bytes 9220
  2.2 17.0 %all-to-all-start.1 = ((f32[4,1,960]{2,1,0:T(1,128)}), f32[4,1,960]{2,1,0:T(1,128)S(1)}, u32[]{:S(2)}, u32[]{:S(2)}) async-start(f32[4,1,960]{2,1,0:T(1,128)} %reshape.52), calls=%async_computation.1 | async-start | bytes 32768 | tf_op jit(solution)/shard_map/all_to_all | solution.py:270
  20.3 6.9 %copy-start.3 = (f32[2048]{0:T(1024)S(1)}, f32[2048]{0:T(1024)}, u32[]{:S(2)}) copy-start(f32[2048]{0:T(1024)} %param.23) | copy-start | bytes 24580
  20.3 6.9 %copy-start.5 = (f32[2048]{0:T(1024)S(1)}, f32[2048]{0:T(1024)}, u32[]{:S(2)}) copy-start(f32[2048]{0:T(1024)} %param.21) | copy-start | bytes 24580
  20.3 6.9 %copy-start.6 = (f32[2048]{0:T(1024)S(1)}, f32[2048]{0:T(1024)}, u32[]{:S(2)}) copy-start(f32[2048]{0:T(1024)} %param.22) | copy-start | bytes 24580
  20.3 7.1 %copy-start.7 = (s32[2048]{0:T(1024)S(1)}, s32[2048]{0:T(1024)}, u32[]{:S(2)}) copy-start(s32[2048]{0:T(1024)} %param.18) | copy-start | bytes 24580
  20.3 22.3 %all-to-all-start = ((f32[16,6,2048]{2,1,0:T(8,128)}), f32[16,6,2048]{2,1,0:T(8,128)S(1)}, u32[]{:S(2)}, u32[]{:S(2)}) async-start(f32[16,6,2048]{2,1,0:T(8,128)} %broadcast_in_dim.4), calls=%async_computation | async-start | bytes 2097152 | tf_op jit(solution)/shard_map/all_to_all | solution.py:269
  27.8 26.7 %copy-start.1 = (f32[48,2048]{1,0:T(8,128)}, f32[48,2048]{1,0:T(8,128)S(1)}, u32[]{:S(2)}) copy-start(f32[48,2048]{1,0:T(8,128)S(1)} %fusion.lapse) | copy-start | bytes 1179652
  42.7 14.6 %copy-start.4 = (s32[2048]{0:T(1024)S(1)}, s32[2048]{0:T(1024)}, u32[]{:S(2)}) copy-start(s32[2048]{0:T(1024)} %param.20) | copy-start | bytes 24580
  54.5 3.1 %collective-permute-start.2 = (f32[1,128]{1,0:T(1,128)S(1)}, f32[1,128]{1,0:T(1,128)S(1)}, u32[]{:S(2)}, u32[]{:S(2)}) collective-permute-start(f32[1,128]{1,0:T(1,128)S(1)} %get-tuple-element.10.total_one), channel_id=1, source_target_pairs={{0,3},{1,0},{2,1},{3,2},{4,7},{5,4},{6,5},{7,6},{8,11},{9,8},{10,9... | collective-permute-start | bytes 1544 | tf_op jit(solution)/shard_map/ppermute | solution.py:316
  56.2 3.3 %collective-permute-start.1 = (f32[1,128]{1,0:T(1,128)S(1)}, f32[1,128]{1,0:T(1,128)S(1)}, u32[]{:S(2)}, u32[]{:S(2)}) collective-permute-start(f32[1,128]{1,0:T(1,128)S(1)} %get-tuple-element.10.total_one), channel_id=1, source_target_pairs={{0,2},{1,3},{2,0},{3,1},{4,6},{5,7},{6,4},{7,5},{8,10},{9,11},{10,... | collective-permute-start | bytes 1544 | tf_op jit(solution)/shard_map/ppermute | solution.py:316
  56.5 4.2 %collective-permute-start = (f32[1,128]{1,0:T(1,128)S(1)}, f32[1,128]{1,0:T(1,128)S(1)}, u32[]{:S(2)}, u32[]{:S(2)}) collective-permute-start(f32[1,128]{1,0:T(1,128)S(1)} %get-tuple-element.10.total_one), channel_id=1, source_target_pairs={{0,1},{1,2},{2,3},{3,0},{4,5},{5,6},{6,7},{7,4},{8,9},{9,10},{10,1... | collective-permute-start | bytes 1544 | tf_op jit(solution)/shard_map/ppermute | solution.py:316
  60.7 1.0 %copy-start.2 = (f32[48,2048]{1,0:T(8,128)S(1)}, f32[48,2048]{1,0:T(8,128)}, u32[]{:S(2)}) copy-start(f32[48,2048]{1,0:T(8,128)} %copy-done.1) | copy-start | bytes 1179652

commit v2 on v1

v2 whole, which is shorter than its diff:
```python
import functools

import jax
import jax.numpy as jnp
from jax import lax
from jax.experimental import pallas as pl
from jax.experimental.pallas import tpu as pltpu
from jax.sharding import PartitionSpec as P

PERIOD = 12
LANES = 128
SUBLANES = 8

credit_floor = 0.001
rollup_growth = 0.05
ALL = ("outer", "inner", "cell")

FEE, ACCOUNT, GUARANTEE, RATCHET, ROLLUP = range(5)
S_ACCOUNT, S_SURVIVING, S_GUARANTEE = range(3)


def lines_of(month, count):
    return slice(month * count, (month + 1) * count)


def parcel_kernel(first_month, premium, charge, mortality, fee_rate, sent, fees, received, scratch, in_sems, out_sems):
    each, count = received.shape[1], fees.shape[0]
    copies = [pltpu.make_async_copy(fee_rate, fees, in_sems.at[0])]
    for i, source in enumerate((premium, charge, mortality)):
        copies.append(pltpu.make_async_copy(source, received.at[i], in_sems.at[i + 1]))
    for copy in copies:
        copy.start()
    for copy in copies:
        copy.wait()
    fee = fees[...]
    grow = jnp.log1p(-fee)
    per_fee = (1.0 - fee) / fee
    for r in range(each):
        for t in range(count):
            at = slice(t * LANES, (t + 1) * LANES)
            row = r * count + t
            scratch[row : row + 1, :] = received[0, r : r + 1, at] - received[1, r : r + 1, at]
            row = (each + r) * count + t
            scratch[row : row + 1, :] = received[2, r : r + 1, at]
    for r in range(each):
        at, then = lines_of(r, count), lines_of(each + r, count)
        month = (first_month[0] + r).astype(jnp.float32)
        scratch[at, :] = scratch[at, :] * (fee * jnp.exp(-(month + 1.0) * grow))
        scratch[then, :] = scratch[then, :] * per_fee
    copies = [pltpu.make_async_copy(scratch, sent.at[i], out_sems.at[i]) for i in range(sent.shape[0])]
    for copy in copies:
        copy.start()
    for copy in copies:
        copy.wait()


def prepare_kernel(lapse_table, lapse_index, fee_rate, level, low, high, lapse):
    fee, index = fee_rate[...], lapse_index[...]
    count = fee.shape[0]
    grow = jnp.log1p(-fee)
    per_fee = (1.0 - fee) / fee
    tables, months = lapse_table.shape

    def one_month(m, carry):
        at = pl.ds(pl.multiple_of(m * count, count), count)
        growth = jnp.exp(-(m.astype(jnp.float32) + 1.0) * grow)
        value = fee * growth
        level[at, :] = value
        low[at, :] = 0.5 * value
        high[at, :] = 1.5 * value
        base = jnp.full(fee.shape, lapse_table[0, m], jnp.float32)
        for k in range(1, tables):
            base = jnp.where(index == k, lapse_table[k, m], base)
        lapse[at, :] = base * (per_fee / growth)
        return carry

    lax.fori_loop(0, months, one_month, 0)


def world_year(start, plan, level, low, high, lapse, cells, state, credit):
    count = cells.shape[1]
    each = plan.shape[1] // (2 * count)
    fee, ratchet, rollup = cells[FEE], cells[RATCHET], cells[ROLLUP]
    kept = 1.0 - fee
    account, surviving, guarantee = state
    per_guarantee = 1.0 / guarantee
    for m in range(start, start + PERIOD):
        d, r = m // each, m % each
        at = lines_of(m, count)
        flow = plan[d, lines_of(r, count), :]
        death = plan[d, lines_of(each + r, count), :]
        account = jnp.maximum(account + flow * per_guarantee, 0.0) * credit(m)
        bounded = jnp.minimum(jnp.maximum(account, low[at, :]), high[at, :])
        surviving = surviving * (kept - fee * death - lapse[at, :] * bounded)
    unit = level[lines_of(start + PERIOD - 1, count), :]
    growth = jnp.maximum(ratchet * (account / unit), 1.0 + rollup_growth * rollup)
    account = jnp.where(ratchet > 0.5, jnp.minimum(account, unit), account / growth)
    return account, surviving, guarantee * growth


def inner_paths(
    start, months, plan, level, low, high, lapse, cells, rows, credit, discount, kept_accounts, kept_growth, reserve
):
    count = cells.shape[1]
    each = plan.shape[1] // (2 * count)
    paths = credit.shape[1]
    groups = paths // SUBLANES
    years = months // PERIOD
    full = (SUBLANES, LANES)

    def tile_step(t, total):
        def spread_out(ref, m):
            return jnp.broadcast_to(ref[pl.ds(m * count + t, 1), :], full)

        def of_cell(ref, r):
            return jnp.broadcast_to(ref[r, pl.ds(t, 1), :], full)

        def planned(m, second):
            d, r = m // each, m % each
            return jnp.broadcast_to(plan[d, pl.ds((r + second * each) * count + t, 1), :], full)

        def group(ref, m, g):
            return ref[m, SUBLANES * g : SUBLANES * (g + 1), :]

        fee = of_cell(cells, FEE)
        kept = 1.0 - fee
        ratchet, rollup = of_cell(cells, RATCHET), of_cell(cells, ROLLUP)
        grown = 1.0 + rollup_growth * rollup
        shrunk = 1.0 / grown
        begin = of_cell(rows, S_ACCOUNT)
        guarantee = of_cell(rows, S_GUARANTEE)
        base = 1.0 / guarantee
        account = [begin] * groups
        per_guarantee = [base] * groups
        for y in range(years):
            for s in range(PERIOD):
                o = y * PERIOD + s
                flow = planned(start + o, 0)
                if y == 0:
                    flow = flow * base
                for g in range(groups):
                    term = flow if y == 0 else flow * per_guarantee[g]
                    account[g] = jnp.maximum(account[g] + term, 0.0) * group(credit, o, g)
                    kept_accounts[o, SUBLANES * g : SUBLANES * (g + 1), :] = account[g]
            if y + 1 < years:
                unit = spread_out(level, start + y * PERIOD + PERIOD - 1)
                per_unit = ratchet / unit
                cap = jnp.where(ratchet > 0.5, unit, 1e30)
                for g in range(groups):
                    growth = jnp.maximum(per_unit * account[g], grown)
                    kept_growth[y, SUBLANES * g : SUBLANES * (g + 1), :] = growth
                    per_guarantee[g] = per_guarantee[g] / growth
                    account[g] = jnp.minimum(account[g], cap) * shrunk
                    kept_growth[years + y, SUBLANES * g : SUBLANES * (g + 1), :] = account[g]
        worth = [None] * groups
        for o in reversed(range(months)):
            m = start + o
            unit, least, most = spread_out(level, m), spread_out(low, m), spread_out(high, m)
            lapsing = spread_out(lapse, m)
            death = planned(m, 1)
            staying = kept - fee * death
            for g in range(groups):
                after = group(kept_accounts, o, g)
                if o == 0:
                    before = begin
                elif o % PERIOD == 0:
                    before = group(kept_growth, years + o // PERIOD - 1, g)
                else:
                    before = group(kept_accounts, o - 1, g)
                value = death * jnp.maximum(unit - after, 0.0) - before
                if worth[g] is not None:
                    later = worth[g]
                    if (o + 1) % PERIOD == 0:
                        later = later * group(kept_growth, o // PERIOD, g)
                    bounded = jnp.minimum(jnp.maximum(after, least), most)
                    value = value + (staying - lapsing * bounded) * later
                worth[g] = value * group(discount, o, g)
        summed = worth[0]
        for g in range(1, groups):
            summed = summed + worth[g]
        scale = guarantee * of_cell(rows, S_SURVIVING) * (1.0 / paths)
        row = jnp.sum(summed * scale, axis=0, keepdims=True)
        reserve[0:1, pl.ds(pl.multiple_of(t * LANES, LANES), LANES)] = row
        return total + row

    return lax.fori_loop(0, count, tile_step, jnp.zeros((1, LANES), jnp.float32))


def fill_tables(first, months, spread, sources, credit, discount):
    for part, source in enumerate(sources):
        rates = source[...]
        lines = rates.shape[0]
        crediting = 1.0 + jnp.maximum(rates - spread, credit_floor)
        discounting = jnp.exp(-rates)
        for m in range(months):
            at = slice(part * lines, (part + 1) * lines)
            credit[m, at, :] = jnp.broadcast_to(crediting[:, first + m : first + m + 1], (lines, LANES))
            discount[m, at, :] = jnp.broadcast_to(discounting[:, first + m : first + m + 1], (lines, LANES))


def block_sums(value, parts, block_hot):
    parts[...] = jnp.zeros_like(parts)
    for part in range(3):
        rounded = value.astype(jnp.bfloat16).astype(jnp.float32)
        parts[part : part + 1, :] = rounded
        value = value - rounded
    sums = jnp.dot(parts[...].astype(jnp.bfloat16), block_hot[...], preferred_element_type=jnp.float32)
    return sums[0:1, :] + sums[1:2, :] + sums[2:3, :]


def first_kernel(
    owners, months, cell_at, world, spread, plan, level, low, high, lapse, cells, own, near, far, across, block_hot,
    reserve, rows, kept_here, next_one, next_two, next_three, credit, discount, kept_accounts, kept_growth, parts, shares,
):
    fill_tables(0, months, spread[0], (own, near, far, across), credit, discount)
    fee, guarantee = cells[FEE], cells[GUARANTEE]
    account = fee * cells[ACCOUNT] / guarantee
    state = (account, jnp.ones_like(account), guarantee)
    state = world_year(
        0, plan, level, low, high, lapse, cells, state, lambda m: 1.0 + jnp.maximum(world[m] - spread[0], credit_floor)
    )
    for r, value in enumerate(state):
        rows[r] = value
    total = inner_paths(
        PERIOD, months, plan, level, low, high, lapse, cells, rows, credit, discount, kept_accounts, kept_growth, reserve
    )
    half = LANES // 2
    sums = block_sums(reserve[...], parts, block_hot)
    total = jnp.broadcast_to(jnp.sum(total, axis=1, keepdims=True), (1, half))
    for k in range(owners):
        shares[k : k + 1, :] = jnp.concatenate([sums[:, half * k : half * (k + 1)], total], axis=1)
    for s, target in enumerate((kept_here, next_one, next_two, next_three)):
        target[...] = shares[pl.ds(lax.rem(cell_at[0] + s, owners), 1), :]


def second_kernel(
    cells_all, months, world, spread, place, kept_here, next_one, next_two, next_three,
    plan, level, low, high, lapse, cells, own, near, far, across, rows_one, reserve_one, block_hot,
    reserves, parcel, blocks_one, rows, reserve, credit, discount, kept_accounts, kept_growth, parts,
):
    half = LANES // 2
    whole = kept_here[...] + next_one[...] + next_two[...] + next_three[...]
    blocks_one[...] = whole
    spread_two = (spread[0] * (1.0 + jnp.tanh(whole / cells_all)))[0, half]
    fill_tables(own.shape[1] - months, months, spread_two, (own, near, far, across), credit, discount)
    state = tuple(rows_one[r] for r in range(3))
    state = world_year(
        PERIOD, plan, level, low, high, lapse, cells, state,
        lambda m: 1.0 + jnp.maximum(world[m] - spread_two, credit_floor),
    )
    for r, value in enumerate(state):
        rows[r] = value
    total = inner_paths(
        2 * PERIOD, months, plan, level, low, high, lapse, cells, rows, credit, discount, kept_accounts, kept_growth, reserve
    )
    reserves[0] = reserve_one[...]
    reserves[1] = reserve[...]
    sums = block_sums(reserve[...], parts, block_hot)
    rate_sum = world[PERIOD]
    for m in range(PERIOD + 1, 2 * PERIOD):
        rate_sum = rate_sum + world[m]
    discount_world = jnp.exp(jnp.full((1, LANES), -rate_sum, jnp.float32))
    total_two = jnp.broadcast_to(jnp.sum(total, axis=1, keepdims=True), (1, LANES))
    loss = (discount_world * total_two - kept_here[...]) / cells_all
    lane = lax.broadcasted_iota(jnp.int32, (1, LANES), 1)
    loss = jnp.where(lane == half + place[0], loss, 0.0)
    for k in range(parcel.shape[1]):
        line = jnp.concatenate([sums[:, half * k : half * (k + 1)], loss[:, half:]], axis=1)
        parcel[:, k] = jnp.broadcast_to(line[None], (parcel.shape[0], 1, LANES))


def last_kernel(place, received, blocks_one, block_reserve, capital):
    outers, owners = received.shape[0], received.shape[1]
    half = LANES // 2
    losses = received[:, 0, 0, :]
    for k in range(1, owners):
        losses = losses + received[:, k, 0, :]
    lane = lax.broadcasted_iota(jnp.int32, losses.shape, 1) - half
    losses = jnp.where(lane >= 0, losses, 0.0)
    across = jnp.sum(losses, axis=0, keepdims=True)
    down = jnp.sum(losses, axis=1, keepdims=True)
    place_down = lax.broadcasted_iota(jnp.int32, losses.shape, 0)
    ahead = (across > down) | ((across == down) & (lane < place_down))
    ahead = ahead & (lane >= 0)
    rank = jnp.sum(jnp.where(ahead, 1.0, 0.0), axis=1, keepdims=True)
    count_top = outers // 4
    chosen = jnp.where(rank < count_top - 0.5, down, 0.0)
    capital[...] = jnp.broadcast_to(jnp.sum(chosen, axis=0, keepdims=True) / count_top, capital.shape)
    blocks = received[place[0], 0]
    for k in range(1, owners):
        blocks = blocks + received[place[0], k]
    block_reserve[0] = blocks_one[:, :half]
    block_reserve[1] = blocks[:, :half]


VMEM = pl.BlockSpec(memory_space=pltpu.VMEM)
SMEM = pl.BlockSpec(memory_space=pltpu.SMEM)
HBM = pl.BlockSpec(memory_space=pltpu.HBM)
MEBI = 1024 * 1024


def body(
    premium,
    charge,
    mortality,
    lapse_table,
    lapse_index,
    guarantee_type,
    block_index,
    account_start,
    guarantee_start,
    fee_rate,
    first_rates,
    second_rates,
    world_rates,
    spread,
):
    f32 = jnp.float32
    outer_size, inner_size, cell_size = (lax.axis_size(a) for a in ALL)
    each, local = premium.shape
    months_all = each * outer_size
    inner_at = lax.axis_index("inner")
    place = lax.axis_index("outer") * inner_size + inner_at
    paths = first_rates.shape[1] * inner_size
    months_one, months_two = first_rates.shape[2], second_rates.shape[2]
    cells_all = local * cell_size
    block_count = 4 * cells_all // LANES

    count = local // LANES
    fee = fee_rate.reshape(count, LANES)

    def call(kernel, name, outs, specs, scratch=(), out_space=VMEM, limit=16):
        return pl.pallas_call(
            kernel,
            out_shape=outs,
            in_specs=specs,
            out_specs=jax.tree.map(lambda _: out_space, outs),
            scratch_shapes=list(scratch),
            compiler_params=pltpu.CompilerParams(vmem_limit_bytes=limit * MEBI),
            name=name,
        )

    def floats(*lengths):
        return jax.ShapeDtypeStruct(lengths, f32)

    def held(*lengths):
        return pltpu.VMEM(lengths, f32)

    first_month = (lax.axis_index("outer") * each).astype(jnp.int32).reshape(1)
    sent = call(
        parcel_kernel,
        "parcel",
        floats(outer_size, 2 * each * count, LANES),
        [SMEM] + [HBM] * 4,
        [
            held(count, LANES),
            held(3, each, local),
            held(2 * each * count, LANES),
            pltpu.SemaphoreType.DMA((4,)),
            pltpu.SemaphoreType.DMA((outer_size,)),
        ],
        HBM,
        60,
    )(first_month, premium, charge, mortality, fee)
    sent, first_rates, second_rates = lax.optimization_barrier((sent, first_rates, second_rates))
    rates = jnp.concatenate([first_rates, second_rates], axis=2)
    plan = lax.all_to_all(sent, "outer", 0, 0, tiled=True)
    shares = [
        lax.dynamic_index_in_dim(rates, jnp.bitwise_xor(inner_at, s), 0, False) for s in range(inner_size)
    ]
    shares[1:] = [
        lax.ppermute(shares[s], "inner", [(j, j ^ s) for j in range(inner_size)]) for s in range(1, inner_size)
    ]
    shaped = [floats(months_all * count, LANES)] * 4
    level, low, high, lapse = call(prepare_kernel, "prepare", shaped, [SMEM] + [VMEM] * 2)(
        lapse_table, lapse_index.reshape(count, LANES), fee
    )
    cells = jnp.stack(
        [
            fee_rate,
            account_start,
            guarantee_start,
            (guarantee_type == 1).astype(f32),
            (guarantee_type == 2).astype(f32),
        ]
    ).reshape(-1, count, LANES)
    world = lax.dynamic_index_in_dim(world_rates, inner_at, 0, False)
    spread_own = lax.dynamic_slice_in_dim(spread, inner_at, 1, 0)
    cell_at = lax.axis_index("cell").astype(jnp.int32).reshape(1)
    place_own = place.astype(jnp.int32).reshape(1)
    block_hot = (block_index[:, None] == jnp.arange(block_count)[None, :]).astype(jnp.bfloat16)

    def inner_scratch(months):
        years = months // PERIOD
        return [
            held(months, paths, LANES),
            held(months, paths, LANES),
            held(months, paths, LANES),
            held(2 * years, paths, LANES),
        ]

    line = floats(1, LANES)
    state = floats(3, count, LANES)
    reserve_one, rows_one, kept_here, *others = call(
        functools.partial(first_kernel, cell_size, months_one),
        "first_date",
        [floats(1, local), state, line, line, line, line],
        [SMEM] * 3 + [VMEM] * 11,
        inner_scratch(months_one) + [held(SUBLANES, local), held(cell_size, LANES)],
    )(cell_at, world, spread_own, plan, level, low, high, lapse, cells, *shares, block_hot)

    others = [
        lax.ppermute(others[s - 1], "cell", [(k, (k + s) % cell_size) for k in range(cell_size)])
        for s in range(1, cell_size)
    ]

    reserves, parcel, blocks_one = call(
        functools.partial(second_kernel, cells_all, months_two),
        "second_date",
        [floats(2, 1, local), floats(outer_size * inner_size, cell_size, 1, LANES), line],
        [SMEM] * 3 + [VMEM] * 17,
        [held(3, count, LANES), held(1, local)] + inner_scratch(months_two) + [held(SUBLANES, local)],
    )(
        world, spread_own, place_own, kept_here, *others,
        plan, level, low, high, lapse, cells, *shares, rows_one, reserve_one, block_hot,
    )

    received = lax.all_to_all(parcel.reshape(-1, 1, LANES), ALL, 0, 0, tiled=True)
    block_reserve, capital = call(
        last_kernel, "last_sums", [floats(2, 1, block_count // cell_size), line], [SMEM] + [VMEM] * 2
    )(place_own, received.reshape(parcel.shape), blocks_one)
    return reserves, block_reserve, capital[0, :1]


def solution(mesh):
    placed = (
        P("outer", "cell"),
        P("outer", "cell"),
        P("outer", "cell"),
        P(),
        P("cell"),
        P("cell"),
        P("cell"),
        P("cell"),
        P("cell"),
        P("cell"),
        P("outer", "inner", None),
        P("outer", "inner", None),
        P("outer", None),
        P("outer"),
    )
    return jax.shard_map(
        body,
        mesh=mesh,
        in_specs=placed,
        out_specs=(P(None, ("outer", "inner"), "cell"), P(None, ("outer", "inner"), "cell"), P()),
        check_vma=False,
    )
```

time: 99.9 us -> 78.9 us (0.79)
  waiting for transfers between devices: 18.6 us -> 5.41 us
  other arithmetic: 5.74 us -> 0.43 us
  Pallas kernels: 21.7 us -> 26 us
  local copies, waits for them, and re-layouts: 4.77 us -> 0.67 us
  blocking collectives: 27.7 us -> 25.9 us
    all_to_all x1, waiting for transfers between devices: 13.4 us -> 0.01 us  [body(): plan = lax.all_to_all(sent, 'outer', 0, 0, tiled=True)]
    all_to_all x1 -> x0, starting transfers between devices: 9.96 us -> none  [body(): lax.all_to_all(jnp.concatenate([first_rates, second_rates], axis=2), 'inn...]
    ppermute x3 -> x6, starting transfers between devices: 2.74 us -> 11.6 us  [the longest x3 8.07 us: body(): lax.ppermute(shares[s], 'inner', [(j, j ^ s) for j in range(inner_size)])]
    pallas_call x3 -> x5, Pallas kernels: 21.7 us -> 26 us  [the longest x1 12.4 us: body(): call(functools.partial(first_kernel, cell_size, months_one), 'first_date'...]
    ppermute x3 -> x6, waiting for transfers between devices: 3.09 us -> 5.41 us  [the longest x3 3.74 us: body(): lax.ppermute(shares[s], 'inner', [(j, j ^ s) for j in range(inner_size)])]
    all_to_all x1 -> x0, waiting for transfers between devices: 2.11 us -> none  [body(): lax.all_to_all(jnp.concatenate([first_rates, second_rates], axis=2), 'inn...]
    all_to_all x1, blocking collectives: 27.7 us -> 25.9 us  [body(): lax.all_to_all(parcel.reshape(-1, 1, LANES), ALL, 0, 0, tiled=True)]
    unnamed x18 -> x25, local copies, waits for them, and re-layouts: 1.83 us -> 0.07 us
  transfers between devices with their start and end apart: 5 -> 7, of which waited for: 4 -> 3; matrix products, arithmetic and copies ran while one was open for 7% -> 1% of each run, Pallas kernels for 0% -> 2%
where the time goes in v2:
time: 78.9 us; the launch traced here: 78.6 us
  Pallas kernels  26 us (33%)
  blocking collectives  25.9 us (33%)
  starting transfers between devices  19.3 us (24%)
  waiting for transfers between devices  5.41 us (7%)
  between operations  0.89 us (1%)
    all_to_all x1, blocking collectives, body(): lax.all_to_all(parcel.reshape(-1, 1, LANES), ALL, 0, 0, tiled=True)  25.9 us
    pallas_call x1, Pallas kernels, body(): call(functools.partial(first_kernel, cell_size, months_one), 'first_date'...  12.4 us
    pallas_call x1, Pallas kernels, body(): call(functools.partial(second_kernel, cells_all, months_two), 'second_dat...  9.32 us
    ppermute x3, starting transfers between devices, body(): lax.ppermute(shares[s], 'inner', [(j, j ^ s) for j in range(inner_size)])  8.07 us
    all_to_all x1, starting transfers between devices, body(): plan = lax.all_to_all(sent, 'outer', 0, 0, tiled=True)  7.73 us
    ppermute x3, waiting for transfers between devices, body(): lax.ppermute(shares[s], 'inner', [(j, j ^ s) for j in range(inner_size)])  3.74 us
    ppermute x3, starting transfers between devices, body(): lax.ppermute(others[s - 1], 'cell', [(k, (k + s) % cell_size) for k in ra...  3.49 us
    pallas_call x1, Pallas kernels, body(): call(parcel_kernel, 'parcel', floats(outer_size, 2 * each * count, LANES)...  1.94 us
  transfers between devices with their start and end apart: 7, of which 3 were waited for; matrix products, arithmetic and copies ran while one was open for 1% of the time, Pallas kernels for 2%

profile of v2, /device:TPU:1, one launch (start us, length us, event | category | flops | bytes accessed | tf_op | source)
XLA Modules:
  0.0 78.6 jit_solution(10238969650211824291)
XLA Ops:
  0.6 0.0 copy-start
  0.7 0.0 copy-start.4
  0.7 0.0 copy-start.5
  0.7 1.9 %parcel.1 = f32[16,96,128]{2,1,0:T(8,128)} custom-call(s32[1]{0:T(128)} %bitcast.3.first_month, f32[3,2048]{1,0:T(4,128)} %premium.1, f32[3,2048]{1,0:T(4,128)} %charge.1, f32[3,2048]{1,0:T(4,128)} %mortality.1, f32[16,128]{1,0:T(8,128)} %bitcast.33), custom_call_target="tpu_custom_call" | custom-call | tf_op jit(solution)/shard_map/parcel/pallas_call | solution.py:350
  2.6 0.0 copy-start.1
  2.6 0.0 copy-start.8
  2.6 0.0 copy-start.9
  2.7 0.0 copy-start.6
  2.7 0.0 copy-start.7
  2.7 0.0 copy-start.10
  2.7 0.0 copy-start.2
  2.7 0.0 copy-start.3
  2.7 7.7 %all-to-all-start = ((f32[16,96,128]{2,1,0:T(8,128)}), f32[16,96,128]{2,1,0:T(8,128)S(1)}, u32[]{:S(2)}, u32[]{:S(2)}) async-start(f32[16,96,128]{2,1,0:T(8,128)} %parcel.1), calls=%async_computation | async-start | bytes 1572864 | tf_op jit(solution)/shard_map/all_to_all | solution.py:367
  10.5 0.0 copy-done.4
  10.5 0.0 copy-done.5
  10.5 0.1 fusion.2
  10.6 7.8 %collective-permute-start.2 = (f32[16,60]{1,0:T(8,128)S(1)}, f32[16,60]{1,0:T(8,128)S(1)}, u32[]{:S(2)}, u32[]{:S(2)}) collective-permute-start(f32[16,60]{1,0:T(8,128)S(1)} %get-tuple-element.39), channel_id=1, source_target_pairs={{0,12},{4,8},{8,4},{12,0},{1,13},{5,9},{9,5},{13,1},{2,14},{6,10},... | collective-permute-start | bytes 11528 | tf_op jit(solution)/shard_map/ppermute | solution.py:372
  18.4 0.0 collective-permute-start
  18.4 0.2 collective-permute-start.1
  18.6 0.0 copy-done.1
  18.7 0.0 copy-done.8
  18.7 0.0 copy-done.9
  18.7 0.0 copy-done.6
  18.7 0.0 copy-done.7
  18.7 0.3 fusion.block_hot
  19.1 0.0 copy-done
  19.1 0.0 copy-done.10
  19.1 0.6 dynamic_slice.21.spread
  19.7 0.0 copy-done.2
  19.7 0.0 copy-done.3
  19.7 1.7 %prepare.1 = (f32[768,128]{1,0:T(8,128)S(1)}, f32[768,128]{1,0:T(8,128)S(1)}, f32[768,128]{1,0:T(8,128)S(1)}, f32[768,128]{1,0:T(8,128)S(1)}) custom-call(f32[16,48]{1,0:T(8,128)S(1)} %copy-done.2, s32[16,128]{1,0:T(8,128)S(1)} %bitcast.35, f32[16,128]{1,0:T(8,128)S(1)} %bitcast.34), custom_call_target="tpu_custom_call" | custom-call | tf_op jit(solution)/shard_map/prepare/pallas_call | solution.py:375
  21.4 0.0 collective-permute-done.2.across
  21.4 0.0 collective-permute-done.near
  21.4 3.7 %collective-permute-done.1.far = f32[16,60]{1,0:T(8,128)S(1)} collective-permute-done((f32[16,60]{1,0:T(8,128)S(1)}, f32[16,60]{1,0:T(8,128)S(1)}, u32[]{:S(2)}, u32[]{:S(2)}) %collective-permute-start.1) | collective-permute-done | bytes 3872 | tf_op jit(solution)/shard_map/ppermute | solution.py:372
  25.1 0.0 all-to-all-done.plan
  25.1 12.4 %first_date.1 = (f32[1,2048]{1,0:T(1,128)S(1)}, f32[3,16,128]{2,1,0:T(8,128)S(1)}, f32[1,128]{1,0:T(1,128)S(1)}, f32[1,128]{1,0:T(1,128)S(1)}, f32[1,128]{1,0:T(1,128)S(1)}, /*index=5*/f32[1,128]{1,0:T(1,128)S(1)}) custom-call(s32[1]{0:T(128)} %bitcast.2.cell_at, f32[24]{0:T(128)S(1)} %fusion.9.world, f32[1]{0:T(128)} %dynamic_slice.21.spread, ...), custom_call_target="tpu_custom_call" | custom-call | tf_op jit(solution)/shard_map/first_date/pallas_call | solution.py:404
  37.5 0.8 collective-permute-start.3
  38.3 2.0 %collective-permute-start.4 = (f32[1,128]{1,0:T(1,128)S(1)}, f32[1,128]{1,0:T(1,128)S(1)}, u32[]{:S(2)}, u32[]{:S(2)}) collective-permute-start(f32[1,128]{1,0:T(1,128)S(1)} %get-tuple-element.30), channel_id=1, source_target_pairs={{0,2},{1,3},{2,0},{3,1},{4,6},{5,7},{6,4},{7,5},{8,10},{9,11},{10,... | collective-permute-start | bytes 1544 | tf_op jit(solution)/shard_map/ppermute | solution.py:413
  40.3 0.7 collective-permute-start.5
  41.0 0.7 collective-permute-done.3.next_one
  41.8 0.0 collective-permute-done.4.next_two
  41.8 0.9 %collective-permute-done.5.next_three = f32[1,128]{1,0:T(1,128)S(1)} collective-permute-done((f32[1,128]{1,0:T(1,128)S(1)}, f32[1,128]{1,0:T(1,128)S(1)}, u32[]{:S(2)}, u32[]{:S(2)}) %collective-permute-start.5) | collective-permute-done | bytes 544 | tf_op jit(solution)/shard_map/ppermute | solution.py:413
  42.7 9.3 %second_date.1 = (f32[2,1,2048]{2,1,0:T(1,128)}, f32[64,4,1,128]{3,2,1,0:T(1,128)S(1)}, f32[1,128]{1,0:T(1,128)S(1)}) custom-call(f32[24]{0:T(128)S(1)} %fusion.9.world, f32[1]{0:T(128)} %dynamic_slice.21.spread, s32[1]{0:T(128)} %bitcast.1.place, f32[1,128]{1,0:T(1,128)S(1)} %get-tuple-element.28.kept_here, f32[1,128]{1,0:T(1,128)S(1)} %collective-permute-done.3.next_one, ...), custom_call_target="tpu_custom_call" | custom-call | tf_op jit(solution)/shard_map/second_date/pallas_call | solution.py:417
  52.0 25.9 %all_to_all.10 = f32[256,1,128]{2,1,0:T(1,128)S(1)} all-to-all(f32[256,1,128]{2,1,0:T(1,128)S(1)} %bitcast.32), channel_id=1, replica_groups=mesh['outer'=16,'inner'=4,'cell'=4] {'outer','inner','cell'}, dimensions={0} | all-to-all | bytes 262144 | tf_op jit(solution)/shard_map/all_to_all | solution.py:428
  77.9 0.7 last_sums.1
  (6 shorter events, 0.0 us)
Async XLA Ops:
  0.6 18.4 %copy-start = (f32[4,24]{1,0:T(4,128)S(1)}, f32[4,24]{1,0:T(4,128)}, u32[]{:S(2)}) copy-start(f32[4,24]{1,0:T(4,128)} %param.26) | copy-start | bytes 1156
  0.7 9.8 %copy-start.4 = (f32[4,16,36]{2,1,0:T(8,128)S(1)}, f32[4,16,36]{2,1,0:T(8,128)}, u32[]{:S(2)}) copy-start(f32[4,16,36]{2,1,0:T(8,128)} %param.24) | copy-start | bytes 27652
  0.7 9.8 %copy-start.5 = (f32[4,16,24]{2,1,0:T(8,128)S(1)}, f32[4,16,24]{2,1,0:T(8,128)}, u32[]{:S(2)}) copy-start(f32[4,16,24]{2,1,0:T(8,128)} %param.25) | copy-start | bytes 18436
  2.6 16.0 %copy-start.1 = (f32[2048]{0:T(1024)S(1)}, f32[2048]{0:T(1024)}, u32[]{:S(2)}) copy-start(f32[2048]{0:T(1024)} %param.23) | copy-start | bytes 24580
  2.6 16.0 %copy-start.8 = (f32[2048]{0:T(1024)S(1)}, f32[2048]{0:T(1024)}, u32[]{:S(2)}) copy-start(f32[2048]{0:T(1024)} %param.21) | copy-start | bytes 24580
  2.6 16.0 %copy-start.9 = (f32[2048]{0:T(1024)S(1)}, f32[2048]{0:T(1024)}, u32[]{:S(2)}) copy-start(f32[2048]{0:T(1024)} %param.22) | copy-start | bytes 24580
  2.7 16.0 %copy-start.6 = (s32[2048]{0:T(1024)S(1)}, s32[2048]{0:T(1024)}, u32[]{:S(2)}) copy-start(s32[2048]{0:T(1024)} %param.19) | copy-start | bytes 24580
  2.7 16.0 %copy-start.7 = (s32[2048]{0:T(1024)S(1)}, s32[2048]{0:T(1024)}, u32[]{:S(2)}) copy-start(s32[2048]{0:T(1024)} %param.20) | copy-start | bytes 24580
  2.7 16.4 %copy-start.10 = (f32[4]{0:T(128)S(1)}, f32[4]{0:T(128)}, u32[]{:S(2)}) copy-start(f32[4]{0:T(128)} %param.27) | copy-start | bytes 52
  2.7 17.0 %copy-start.2 = (f32[16,48]{1,0:T(8,128)S(1)}, f32[16,48]{1,0:T(8,128)}, u32[]{:S(2)}) copy-start(f32[16,48]{1,0:T(8,128)} %lapse_table.1) | copy-start | bytes 9220
  2.7 17.0 %copy-start.3 = (s32[2048]{0:T(1024)S(1)}, s32[2048]{0:T(1024)}, u32[]{:S(2)}) copy-start(s32[2048]{0:T(1024)} %param.18) | copy-start | bytes 24580
  2.7 22.4 %all-to-all-start = ((f32[16,96,128]{2,1,0:T(8,128)}), f32[16,96,128]{2,1,0:T(8,128)S(1)}, u32[]{:S(2)}, u32[]{:S(2)}) async-start(f32[16,96,128]{2,1,0:T(8,128)} %parcel.1), calls=%async_computation | async-start | bytes 1572864 | tf_op jit(solution)/shard_map/all_to_all | solution.py:367
  10.6 10.8 %collective-permute-start.2 = (f32[16,60]{1,0:T(8,128)S(1)}, f32[16,60]{1,0:T(8,128)S(1)}, u32[]{:S(2)}, u32[]{:S(2)}) collective-permute-start(f32[16,60]{1,0:T(8,128)S(1)} %get-tuple-element.39), channel_id=1, source_target_pairs={{0,12},{4,8},{8,4},{12,0},{1,13},{5,9},{9,5},{13,1},{2,14},{6,10},... | collective-permute-start | bytes 11528 | tf_op jit(solution)/shard_map/ppermute | solution.py:372
  18.4 3.0 %collective-permute-start = (f32[16,60]{1,0:T(8,128)S(1)}, f32[16,60]{1,0:T(8,128)S(1)}, u32[]{:S(2)}, u32[]{:S(2)}) collective-permute-start(f32[16,60]{1,0:T(8,128)S(1)} %get-tuple-element.41), channel_id=1, source_target_pairs={{0,4},{4,0},{8,12},{12,8},{1,5},{5,1},{9,13},{13,9},{2,6},{6,2},{1... | collective-permute-start | bytes 11528 | tf_op jit(solution)/shard_map/ppermute | solution.py:372
  18.4 6.7 %collective-permute-start.1 = (f32[16,60]{1,0:T(8,128)S(1)}, f32[16,60]{1,0:T(8,128)S(1)}, u32[]{:S(2)}, u32[]{:S(2)}) collective-permute-start(f32[16,60]{1,0:T(8,128)S(1)} %get-tuple-element.42), channel_id=1, source_target_pairs={{0,8},{4,12},{8,0},{12,4},{1,9},{5,13},{9,1},{13,5},{2,10},{6,14},... | collective-permute-start | bytes 11528 | tf_op jit(solution)/shard_map/ppermute | solution.py:372
  37.5 4.2 %collective-permute-start.3 = (f32[1,128]{1,0:T(1,128)S(1)}, f32[1,128]{1,0:T(1,128)S(1)}, u32[]{:S(2)}, u32[]{:S(2)}) collective-permute-start(f32[1,128]{1,0:T(1,128)S(1)} %get-tuple-element.29), channel_id=1, source_target_pairs={{0,1},{1,2},{2,3},{3,0},{4,5},{5,6},{6,7},{7,4},{8,9},{9,10},{10,1... | collective-permute-start | bytes 1544 | tf_op jit(solution)/shard_map/ppermute | solution.py:413
  38.3 3.5 %collective-permute-start.4 = (f32[1,128]{1,0:T(1,128)S(1)}, f32[1,128]{1,0:T(1,128)S(1)}, u32[]{:S(2)}, u32[]{:S(2)}) collective-permute-start(f32[1,128]{1,0:T(1,128)S(1)} %get-tuple-element.30), channel_id=1, source_target_pairs={{0,2},{1,3},{2,0},{3,1},{4,6},{5,7},{6,4},{7,5},{8,10},{9,11},{10,... | collective-permute-start | bytes 1544 | tf_op jit(solution)/shard_map/ppermute | solution.py:413
  40.3 2.4 %collective-permute-start.5 = (f32[1,128]{1,0:T(1,128)S(1)}, f32[1,128]{1,0:T(1,128)S(1)}, u32[]{:S(2)}, u32[]{:S(2)}) collective-permute-start(f32[1,128]{1,0:T(1,128)S(1)} %get-tuple-element.31), channel_id=1, source_target_pairs={{0,3},{1,0},{2,1},{3,2},{4,7},{5,4},{6,5},{7,6},{8,11},{9,8},{10,9... | collective-permute-start | bytes 1544 | tf_op jit(solution)/shard_map/ppermute | solution.py:413

commit v3 on v2

v3 whole, which is shorter than its diff:
```python
import functools

import jax
import jax.numpy as jnp
from jax import lax
from jax.experimental import pallas as pl
from jax.experimental.pallas import tpu as pltpu
from jax.sharding import PartitionSpec as P

PERIOD = 12
LANES = 128
SUBLANES = 8
TOGETHER = 2
CORES = 2

credit_floor = 0.001
rollup_growth = 0.05
ALL = ("outer", "inner", "cell")

FEE, ACCOUNT, GUARANTEE, RATCHET, ROLLUP = range(5)
S_ACCOUNT, S_SURVIVING, S_GUARANTEE = range(3)


def lines_of(month, count):
    return slice(month * count, (month + 1) * count)


def parcel_kernel(outer_at, inner_at, premium, charge, mortality, fee_rate, sent, fees, received, scratch, in_sems, out_sems):
    each, wide = received.shape[1:]
    count = fees.shape[0]
    half = lax.rem(inner_at[0], CORES)
    copies = [pltpu.make_async_copy(fee_rate.at[half], fees, in_sems.at[0])]
    columns = pl.ds(pl.multiple_of(half * wide, wide), wide)
    for i, source in enumerate((premium, charge, mortality)):
        copies.append(pltpu.make_async_copy(source.at[:, columns], received.at[i], in_sems.at[i + 1]))
    for copy in copies:
        copy.start()
    for copy in copies:
        copy.wait()
    fee = fees[...]
    grow = jnp.log1p(-fee)
    per_fee = (1.0 - fee) / fee
    for r in range(each):
        for t in range(count):
            at = slice(t * LANES, (t + 1) * LANES)
            row = r * count + t
            scratch[row : row + 1, :] = received[0, r : r + 1, at] - received[1, r : r + 1, at]
            row = (each + r) * count + t
            scratch[row : row + 1, :] = received[2, r : r + 1, at]
    for r in range(each):
        at, then = lines_of(r, count), lines_of(each + r, count)
        month = (outer_at[0] * each + r).astype(jnp.float32)
        scratch[at, :] = scratch[at, :] * (fee * jnp.exp(-(month + 1.0) * grow))
        scratch[then, :] = scratch[then, :] * per_fee
    copies = [pltpu.make_async_copy(scratch, sent.at[i], out_sems.at[i]) for i in range(sent.shape[0])]
    for copy in copies:
        copy.start()
    for copy in copies:
        copy.wait()


def prepare_kernel(
    inner_at, lapse_table, lapse_index, kind, account, guarantee, fee_rate, cells, level, low, high, lapse, indices
):
    half = lax.rem(inner_at[0], CORES)
    for part, source in enumerate((half, 1 - half)):
        at = lines_of(part, kind.shape[1])
        cells[FEE, at, :] = fee_rate[source]
        cells[ACCOUNT, at, :] = account[source]
        cells[GUARANTEE, at, :] = guarantee[source]
        cells[RATCHET, at, :] = jnp.where(kind[source] == 1, 1.0, 0.0)
        cells[ROLLUP, at, :] = jnp.where(kind[source] == 2, 1.0, 0.0)
        indices[at, :] = lapse_index[source]
    fee, index = cells[FEE], indices[...]
    count = fee.shape[0]
    grow = jnp.log1p(-fee)
    per_fee = (1.0 - fee) / fee
    tables, months = lapse_table.shape

    def one_month(m, carry):
        at = pl.ds(pl.multiple_of(m * count, count), count)
        growth = jnp.exp(-(m.astype(jnp.float32) + 1.0) * grow)
        value = fee * growth
        level[at, :] = value
        low[at, :] = 0.5 * value
        high[at, :] = 1.5 * value
        base = jnp.full(fee.shape, lapse_table[0, m], jnp.float32)
        for k in range(1, tables):
            base = jnp.where(index == k, lapse_table[k, m], base)
        lapse[at, :] = base * (per_fee / growth)
        return carry

    lax.fori_loop(0, months, one_month, 0)


def fill_first_tables(inner_at, spread, own, near, far, across, credit, discount):
    lines = own.shape[0]
    for part, rates in enumerate((own[...], near[...], far[:lines, :], across[lines:, :])):
        at = slice(part * lines, (part + 1) * lines)
        crediting = 1.0 + jnp.maximum(rates - spread[inner_at[0]], credit_floor)
        discounting = jnp.exp(-rates)
        for m in range(credit.shape[0]):
            credit[m, at, :] = jnp.broadcast_to(crediting[:, m : m + 1], (lines, LANES))
            discount[m, at, :] = jnp.broadcast_to(discounting[:, m : m + 1], (lines, LANES))


def second_table_kernel(own, near, far, across, rate, discount):
    first = own.shape[1] - rate.shape[0]
    lines = own.shape[0]
    for part, rates in enumerate((own[...], near[...], far[:lines, :], across[lines:, :])):
        at = slice(part * lines, (part + 1) * lines)
        discounting = jnp.exp(-rates)
        for m in range(rate.shape[0]):
            rate[m, at, :] = jnp.broadcast_to(rates[:, first + m : first + m + 1], (lines, LANES))
            discount[m, at, :] = jnp.broadcast_to(discounting[:, first + m : first + m + 1], (lines, LANES))


def world_year(start, part, plan, level, low, high, lapse, cells, state, credit):
    count = cells.shape[1]
    own = count // CORES
    each = plan.shape[1] // (2 * own)
    here = lines_of(part, own)
    fee, ratchet, rollup = cells[FEE, here, :], cells[RATCHET, here, :], cells[ROLLUP, here, :]
    kept = 1.0 - fee
    account, surviving, guarantee = state
    per_guarantee = 1.0 / guarantee
    for m in range(start, start + PERIOD):
        d, r = m // each, m % each
        at = slice(m * count + part * own, m * count + (part + 1) * own)
        flow = plan[d, lines_of(r, own), :]
        death = plan[d, lines_of(each + r, own), :]
        account = jnp.maximum(account + flow * per_guarantee, 0.0) * credit(m)
        bounded = jnp.minimum(jnp.maximum(account, low[at, :]), high[at, :])
        surviving = surviving * (kept - fee * death - lapse[at, :] * bounded)
        unit = level[at, :]
    growth = jnp.maximum(ratchet * (account / unit), 1.0 + rollup_growth * rollup)
    account = jnp.where(ratchet > 0.5, jnp.minimum(account, unit), account / growth)
    return account, surviving, guarantee * growth


def inner_paths(
    start, part, target, plan, level, low, high, lapse, cells, rows, credit, discount, kept_accounts, kept_growth, reserve
):
    count = cells.shape[1]
    own = count // CORES
    each = plan.shape[1] // (2 * own)
    months, paths = credit.shape[:2]
    groups = paths // SUBLANES
    years = months // PERIOD
    full = (SUBLANES, LANES)

    def group(ref, m, g):
        return ref[m, SUBLANES * g : SUBLANES * (g + 1), :]

    def tiles_step(step, total):
        def spread_out(ref, i, m):
            return jnp.broadcast_to(ref[pl.ds(m * count + part * own + step * TOGETHER + i, 1), :], full)

        def of_cell(i, r):
            return jnp.broadcast_to(cells[r, pl.ds(part * own + step * TOGETHER + i, 1), :], full)

        def of_state(i, r):
            return jnp.broadcast_to(rows[r, pl.ds(step * TOGETHER + i, 1), :], full)

        def planned(i, m, second):
            d, r = m // each, m % each
            return jnp.broadcast_to(plan[d, pl.ds((r + second * each) * own + step * TOGETHER + i, 1), :], full)

        def of_tile(ref, i, m, g):
            return ref[i, m, SUBLANES * g : SUBLANES * (g + 1), :]

        def keep(ref, i, m, g, value):
            ref[i, m, SUBLANES * g : SUBLANES * (g + 1), :] = value

        tiles = range(TOGETHER)
        begin = [of_state(i, S_ACCOUNT) for i in tiles]
        base = [1.0 / of_state(i, S_GUARANTEE) for i in tiles]
        account = [[begin[i]] * groups for i in tiles]
        per_guarantee = [[base[i]] * groups for i in tiles]
        for o in range(months):
            flow = [planned(i, start + o, 0) for i in tiles]
            if o < PERIOD:
                flow = [flow[i] * base[i] for i in tiles]
            for g in range(groups):
                crediting = group(credit, o, g)
                for i in tiles:
                    term = flow[i] if o < PERIOD else flow[i] * per_guarantee[i][g]
                    account[i][g] = jnp.maximum(account[i][g] + term, 0.0) * crediting
                    keep(kept_accounts, i, o, g, account[i][g])
            if (o + 1) % PERIOD == 0 and o + 1 < months:
                y = o // PERIOD
                for i in tiles:
                    ratchet = of_cell(i, RATCHET)
                    grown = 1.0 + rollup_growth * of_cell(i, ROLLUP)
                    shrunk = 1.0 / grown
                    unit = spread_out(level, i, start + o)
                    per_unit = ratchet / unit
                    cap = jnp.where(ratchet > 0.5, unit, 1e30)
                    for g in range(groups):
                        growth = jnp.maximum(per_unit * account[i][g], grown)
                        keep(kept_growth, i, y, g, growth)
                        per_guarantee[i][g] = per_guarantee[i][g] / growth
                        account[i][g] = jnp.minimum(account[i][g], cap) * shrunk
                        keep(kept_growth, i, years + y, g, account[i][g])
        fee = [of_cell(i, FEE) for i in tiles]
        worth = [[None] * groups for i in tiles]
        for o in reversed(range(months)):
            m = start + o
            for i in tiles:
                unit, least, most = spread_out(level, i, m), spread_out(low, i, m), spread_out(high, i, m)
                lapsing = spread_out(lapse, i, m)
                death = planned(i, m, 1)
                staying = (1.0 - fee[i]) - fee[i] * death
                for g in range(groups):
                    after = of_tile(kept_accounts, i, o, g)
                    if o == 0:
                        before = begin[i]
                    elif o % PERIOD == 0:
                        before = of_tile(kept_growth, i, years + o // PERIOD - 1, g)
                    else:
                        before = of_tile(kept_accounts, i, o - 1, g)
                    value = death * jnp.maximum(unit - after, 0.0) - before
                    if worth[i][g] is not None:
                        later = worth[i][g]
                        if (o + 1) % PERIOD == 0:
                            later = later * of_tile(kept_growth, i, o // PERIOD, g)
                        bounded = jnp.minimum(jnp.maximum(after, least), most)
                        value = value + (staying - lapsing * bounded) * later
                    worth[i][g] = value * group(discount, o, g)
        for i in tiles:
            summed = worth[i][0]
            for g in range(1, groups):
                summed = summed + worth[i][g]
            scale = of_state(i, S_GUARANTEE) * of_state(i, S_SURVIVING) * (1.0 / paths)
            row = jnp.sum(summed * scale, axis=0, keepdims=True)
            at = pl.multiple_of((target + step * TOGETHER + i) * LANES, LANES)
            reserve[0:1, pl.ds(at, LANES)] = row
            total = total + row
        return total

    return lax.fori_loop(0, own // TOGETHER, tiles_step, jnp.zeros((1, LANES), jnp.float32))


def block_sums(value, parts, block_hot):
    parts[...] = jnp.zeros_like(parts)
    for part in range(3):
        rounded = value.astype(jnp.bfloat16).astype(jnp.float32)
        parts[part : part + 1, :] = rounded
        value = value - rounded
    sums = jnp.dot(parts[...].astype(jnp.bfloat16), block_hot[...], preferred_element_type=jnp.float32)
    return sums[0:1, :] + sums[1:2, :] + sums[2:3, :]


def first_half(part, inner_at, world, spread, plan, level, low, high, lapse, cells, credit, discount, reserve, rows, kept_accounts, kept_growth):
    own = cells.shape[1] // CORES
    at, here = inner_at[0], lines_of(part, own)
    half = lax.rem(at, CORES)
    fee, guarantee = cells[FEE, here, :], cells[GUARANTEE, here, :]
    account = fee * cells[ACCOUNT, here, :] / guarantee
    state = (account, jnp.ones_like(account), guarantee)
    state = world_year(
        0, part, plan, level, low, high, lapse, cells, state,
        lambda m: 1.0 + jnp.maximum(world[at, m] - spread[at], credit_floor),
    )
    for r, value in enumerate(state):
        rows[r] = value
    target = (half if part == 0 else 1 - half) * own
    return inner_paths(
        PERIOD, part, target, plan, level, low, high, lapse, cells, rows, credit, discount, kept_accounts, kept_growth, reserve
    )


def first_own_kernel(
    inner_at, world, spread, plan, level, low, high, lapse, cells, own_rates, near_rates, far_rates, across_rates,
    reserve, rows, total, credit, discount, kept_accounts, kept_growth,
):
    fill_first_tables(inner_at, spread, own_rates, near_rates, far_rates, across_rates, credit, discount)
    total[...] = first_half(
        0, inner_at, world, spread, plan, level, low, high, lapse, cells, credit, discount, reserve, rows, kept_accounts, kept_growth
    )


def first_other_kernel(
    owners, inner_at, cell_at, world, spread, plan, level, low, high, lapse, cells, credit, discount,
    reserve_own, total_own, block_hot,
    reserve, rows, kept_here, next_one, next_two, next_three, kept_accounts, kept_growth, parts, shares,
):
    reserve[...] = reserve_own[...]
    total = total_own[...] + first_half(
        1, inner_at, world, spread, plan, level, low, high, lapse, cells, credit, discount, reserve, rows, kept_accounts, kept_growth
    )
    half = LANES // 2
    sums = block_sums(reserve[...], parts, block_hot)
    total = jnp.broadcast_to(jnp.sum(total, axis=1, keepdims=True), (1, half))
    for k in range(owners):
        shares[k : k + 1, :] = jnp.concatenate([sums[:, half * k : half * (k + 1)], total], axis=1)
    for s, target in enumerate((kept_here, next_one, next_two, next_three)):
        target[...] = shares[pl.ds(lax.rem(cell_at[0] + s, owners), 1), :]


def second_kernel(
    cells_all, inner_at, world, spread, place, kept_here, next_one, next_two, next_three,
    plan_own, plan_other, level, low, high, lapse, cells, rate, discount, rows_own, rows_other, reserve_one, block_hot,
    reserves, parcel, blocks_one, rows, reserve, credit, kept_accounts, kept_growth, parts,
):
    half = LANES // 2
    at = inner_at[0]
    own = cells.shape[1] // CORES
    whole = kept_here[...] + next_one[...] + next_two[...] + next_three[...]
    blocks_one[...] = whole
    spread_two = (spread[at] * (1.0 + jnp.tanh(whole / cells_all)))[0, half]
    for m in range(credit.shape[0]):
        credit[m] = 1.0 + jnp.maximum(rate[m] - spread_two, credit_floor)
    core = lax.rem(at, CORES)
    total = jnp.zeros((1, LANES), jnp.float32)
    for part, (plan, source) in enumerate(((plan_own, rows_own), (plan_other, rows_other))):
        state = world_year(
            PERIOD, part, plan, level, low, high, lapse, cells, tuple(source[r] for r in range(3)),
            lambda m: 1.0 + jnp.maximum(world[at, m] - spread_two, credit_floor),
        )
        for r, value in enumerate(state):
            rows[part, r] = value
    for part, plan in enumerate((plan_own, plan_other)):
        total = total + inner_paths(
            2 * PERIOD, part, (core if part == 0 else 1 - core) * own,
            plan, level, low, high, lapse, cells, rows.at[part], credit, discount, kept_accounts, kept_growth, reserve,
        )
    reserves[0] = reserve_one[...]
    reserves[1] = reserve[...]
    sums = block_sums(reserve[...], parts, block_hot)
    rate_sum = world[at, PERIOD]
    for m in range(PERIOD + 1, 2 * PERIOD):
        rate_sum = rate_sum + world[at, m]
    discount_world = jnp.exp(jnp.full((1, LANES), -rate_sum, jnp.float32))
    total_two = jnp.broadcast_to(jnp.sum(total, axis=1, keepdims=True), (1, LANES))
    loss = (discount_world * total_two - kept_here[...]) / cells_all
    lane = lax.broadcasted_iota(jnp.int32, (1, LANES), 1)
    loss = jnp.where(lane == half + place[0], loss, 0.0)
    for k in range(parcel.shape[1]):
        line = jnp.concatenate([sums[:, half * k : half * (k + 1)], loss[:, half:]], axis=1)
        parcel[:, k] = jnp.broadcast_to(line[None], (parcel.shape[0], 1, LANES))


def last_kernel(place, received, blocks_one, block_reserve, capital):
    outers, owners = received.shape[0], received.shape[1]
    half = LANES // 2
    losses = received[:, 0, 0, :]
    for k in range(1, owners):
        losses = losses + received[:, k, 0, :]
    lane = lax.broadcasted_iota(jnp.int32, losses.shape, 1) - half
    losses = jnp.where(lane >= 0, losses, 0.0)
    across = jnp.sum(losses, axis=0, keepdims=True)
    down = jnp.sum(losses, axis=1, keepdims=True)
    place_down = lax.broadcasted_iota(jnp.int32, losses.shape, 0)
    ahead = (across > down) | ((across == down) & (lane < place_down))
    ahead = ahead & (lane >= 0)
    rank = jnp.sum(jnp.where(ahead, 1.0, 0.0), axis=1, keepdims=True)
    count_top = outers // 4
    chosen = jnp.where(rank < count_top - 0.5, down, 0.0)
    capital[...] = jnp.broadcast_to(jnp.sum(chosen, axis=0, keepdims=True) / count_top, capital.shape)
    blocks = received[place[0], 0]
    for k in range(1, owners):
        blocks = blocks + received[place[0], k]
    block_reserve[0] = blocks_one[:, :half]
    block_reserve[1] = blocks[:, :half]


VMEM = pl.BlockSpec(memory_space=pltpu.VMEM)
SMEM = pl.BlockSpec(memory_space=pltpu.SMEM)
HBM = pl.BlockSpec(memory_space=pltpu.HBM)
MEBI = 1024 * 1024


def call(kernel, name, outs, specs, scratch=(), out_space=VMEM, limit=16, read=0):
    return pl.pallas_call(
        kernel,
        out_shape=outs,
        in_specs=specs,
        out_specs=jax.tree.map(lambda _: out_space, outs),
        scratch_shapes=list(scratch),
        compiler_params=pltpu.CompilerParams(vmem_limit_bytes=limit * MEBI),
        name=name,
        cost_estimate=pl.CostEstimate(flops=4000 * read, bytes_accessed=read, transcendentals=0),
    )


def floats(*lengths):
    return jax.ShapeDtypeStruct(lengths, jnp.float32)


def held(*lengths):
    return pltpu.VMEM(lengths, jnp.float32)


def body(
    premium,
    charge,
    mortality,
    lapse_table,
    lapse_index,
    guarantee_type,
    block_index,
    account_start,
    guarantee_start,
    fee_rate,
    first_rates,
    second_rates,
    world_rates,
    spread,
):
    outer_size, inner_size, cell_size = (lax.axis_size(a) for a in ALL)
    each, local = premium.shape
    months_all = each * outer_size
    paths = first_rates.shape[1] * inner_size
    months_one, months_two = first_rates.shape[2], second_rates.shape[2]
    cells_all = local * cell_size
    block_count = 4 * cells_all // LANES
    count = local // LANES
    own = count // CORES

    outer_at, inner_at, cell_at = (lax.axis_index(a).astype(jnp.int32) for a in ALL)
    place = (outer_at * inner_size + inner_at).reshape(1)
    outer_at, inner_one, cell_at = outer_at.reshape(1), inner_at.reshape(1), cell_at.reshape(1)

    def halves(value):
        return value.reshape(CORES, own, LANES)

    sent = call(
        parcel_kernel,
        "parcel",
        floats(outer_size, 2 * each * own, LANES),
        [SMEM] * 2 + [HBM] * 4,
        [
            held(own, LANES),
            held(3, each, own * LANES),
            held(2 * each * own, LANES),
            pltpu.SemaphoreType.DMA((4,)),
            pltpu.SemaphoreType.DMA((outer_size,)),
        ],
        HBM,
        60,
    )(outer_at, inner_one, premium, charge, mortality, halves(fee_rate))
    sent, first_rates, second_rates = lax.optimization_barrier((sent, first_rates, second_rates))
    rates = jnp.concatenate([first_rates, second_rates], axis=2)
    plan_own = lax.all_to_all(sent, "outer", 0, 0, tiled=True)
    own_rates, near_rates, far_rates, across_rates = (
        lax.dynamic_index_in_dim(rates, jnp.bitwise_xor(inner_at, s), 0, False) for s in range(inner_size)
    )
    far_rates = jnp.concatenate([far_rates, across_rates], axis=0)

    def swapped(value, s):
        return lax.ppermute(value, "inner", [(j, j ^ s) for j in range(inner_size)])

    far_rates = swapped(far_rates, CORES)
    near_rates = swapped(near_rates, 1)
    across_rates = swapped(far_rates, 1)
    shares = [own_rates, near_rates, far_rates, across_rates]
    coefs = [floats(5, count, LANES)] + [floats(months_all * count, LANES)] * 4
    cells, *coefs = call(prepare_kernel, "prepare", coefs, [SMEM] * 2 + [VMEM] * 5, [pltpu.VMEM((count, LANES), jnp.int32)], read=4 * MEBI)(
        inner_one,
        lapse_table,
        *(halves(a) for a in (lapse_index, guarantee_type, account_start, guarantee_start, fee_rate)),
    )
    block_hot = (block_index[:, None] == jnp.arange(block_count)[None, :]).astype(jnp.bfloat16)

    plan_other = swapped(plan_own, 1)

    def inner_scratch(months):
        return [
            held(TOGETHER, months, paths, LANES),
            held(TOGETHER, 2 * (months // PERIOD), paths, LANES),
        ]

    line = floats(1, LANES)
    state = floats(3, own, LANES)
    table = floats(months_one, paths, LANES)
    reserve_own, rows_own, total_own, credit_one, discount_one = call(
        first_own_kernel,
        "first_date_own",
        [floats(1, local), state, line, table, table],
        [SMEM] * 3 + [VMEM] * 10,
        inner_scratch(months_one),
        read=20 * MEBI,
    )(inner_one, world_rates, spread, plan_own, *coefs, cells, *shares)
    reserve_one, rows_other, kept_here, *others = call(
        functools.partial(first_other_kernel, cell_size),
        "first_date_other",
        [floats(1, local), state, line, line, line, line],
        [SMEM] * 4 + [VMEM] * 11,
        inner_scratch(months_one) + [held(SUBLANES, local), held(cell_size, LANES)],
    )(
        inner_one, cell_at, world_rates, spread, plan_other, *coefs, cells, credit_one, discount_one,
        reserve_own, total_own, block_hot,
    )

    others = [
        lax.ppermute(others[s - 1], "cell", [(k, (k + s) % cell_size) for k in range(cell_size)])
        for s in range(1, cell_size)
    ]
    reserve_one, *shares = lax.optimization_barrier((reserve_one, *shares))
    rate_two, discount_two = call(
        second_table_kernel, "second_tables", [floats(months_two, paths, LANES)] * 2, [VMEM] * 4
    )(*shares)

    reserves, parcel, blocks_one = call(
        functools.partial(second_kernel, cells_all),
        "second_date",
        [floats(2, 1, local), floats(outer_size * inner_size, cell_size, 1, LANES), line],
        [SMEM] * 4 + [VMEM] * 17,
        [held(CORES, 3, own, LANES), held(1, local), held(months_two, paths, LANES)]
        + inner_scratch(months_two)
        + [held(SUBLANES, local)],
    )(
        inner_one, world_rates, spread, place, kept_here, *others,
        plan_own, plan_other, *coefs, cells, rate_two, discount_two, rows_own, rows_other, reserve_one, block_hot,
    )

    received = lax.all_to_all(parcel.reshape(-1, 1, LANES), ALL, 0, 0, tiled=True)
    block_reserve, capital = call(
        last_kernel, "last_sums", [floats(2, 1, block_count // cell_size), line], [SMEM] + [VMEM] * 2
    )(place, received.reshape(parcel.shape), blocks_one)
    return reserves, block_reserve, capital[0, :1]


def solution(mesh):
    placed = (
        P("outer", "cell"),
        P("outer", "cell"),
        P("outer", "cell"),
        P(),
        P("cell"),
        P("cell"),
        P("cell"),
        P("cell"),
        P("cell"),
        P("cell"),
        P("outer", "inner", None),
        P("outer", "inner", None),
        P("outer", None),
        P("outer"),
    )
    return jax.shard_map(
        body,
        mesh=mesh,
        in_specs=placed,
        out_specs=(P(None, ("outer", "inner"), "cell"), P(None, ("outer", "inner"), "cell"), P()),
        check_vma=False,
    )
```

time: 78.9 us -> 74.9 us (0.949)
  waiting for transfers between devices: 5.41 us -> 1.28 us
  starting transfers between devices: 19.3 us -> 21.3 us
  Pallas kernels: 26 us -> 24.9 us
    ppermute x3 -> x4, waiting for transfers between devices: 3.74 us -> 0.24 us  [swapped(): return lax.ppermute(value, 'inner', [(j, j ^ s) for j in range(inner_size)])]
    ppermute x3, starting transfers between devices: 3.49 us -> 5.04 us  [body(): lax.ppermute(others[s - 1], 'cell', [(k, (k + s) % cell_size) for k in ra...]
    pallas_call x4 -> x6, Pallas kernels: 25.3 us -> 24.2 us  [the longest x1 7.94 us: body(): call(functools.partial(second_kernel, cells_all), 'second_date', [floats(...]
    ppermute x3 -> x4, starting transfers between devices: 8.07 us -> 8.66 us  [swapped(): return lax.ppermute(value, 'inner', [(j, j ^ s) for j in range(inner_size)])]
  transfers between devices with their start and end apart: 7 -> 8, of which waited for: 3 -> 2; matrix products, arithmetic and copies ran while one was open for 1% -> 1% of each run, Pallas kernels for 2% -> 11%
where the time goes in v3:
time: 74.9 us; the launch traced here: 74.6 us
  blocking collectives  25.8 us (34%)
  Pallas kernels  24.9 us (33%)
  starting transfers between devices  21.3 us (28%)
  waiting for transfers between devices  1.28 us (2%)
  between operations  0.88 us (1%)
    all_to_all x1, blocking collectives, body(): lax.all_to_all(parcel.reshape(-1, 1, LANES), ALL, 0, 0, tiled=True)  25.8 us
    ppermute x4, starting transfers between devices, swapped(): return lax.ppermute(value, 'inner', [(j, j ^ s) for j in range(inner_size)])  8.66 us
    pallas_call x1, Pallas kernels, body(): call(functools.partial(second_kernel, cells_all), 'second_date', [floats(...  7.94 us
    all_to_all x1, starting transfers between devices, body(): plan_own = lax.all_to_all(sent, 'outer', 0, 0, tiled=True)  7.6 us
    pallas_call x1, Pallas kernels, body(): call(first_own_kernel, 'first_date_own', [floats(1, local), state, line,...  6.29 us
    pallas_call x1, Pallas kernels, body(): call(functools.partial(first_other_kernel, cell_size), 'first_date_other'...  5.84 us
    ppermute x3, starting transfers between devices, body(): lax.ppermute(others[s - 1], 'cell', [(k, (k + s) % cell_size) for k in ra...  5.04 us
    pallas_call x1, Pallas kernels, body(): call(parcel_kernel, 'parcel', floats(outer_size, 2 * each * own, LANES),...  1.81 us
  transfers between devices with their start and end apart: 8, of which 2 were waited for; matrix products, arithmetic and copies ran while one was open for 1% of the time, Pallas kernels for 11%

profile of v3, /device:TPU:1, one launch (start us, length us, event | category | flops | bytes accessed | tf_op | source)
XLA Modules:
  0.0 74.6 jit_solution(2739524021082246658)
XLA Ops:
  0.6 0.0 copy-start.1
  0.6 0.0 copy-start.9
  0.7 0.0 copy-start.8
  0.7 0.0 copy-start.7
  0.7 0.0 copy-start.6
  0.7 0.0 copy-start.5
  0.7 0.0 copy-start.4
  0.7 0.0 copy-start.3
  0.7 1.8 %parcel.1 = f32[16,48,128]{2,1,0:T(8,128)} custom-call(s32[1]{0:T(128)} %bitcast.3.outer_at, s32[1]{0:T(128)} %bitcast.inner_at, f32[3,2048]{1,0:T(4,128)} %premium.1, f32[3,2048]{1,0:T(4,128)} %charge.1, f32[3,2048]{1,0:T(4,128)} %mortality.1, f32[2,8,128]{2,1,0:T(8,128)} %bitcast.25), custom_call_target="tpu_custom_call" | custom-call | tf_op jit(solution)/shard_map/parcel/pallas_call | solution.py:428
  2.5 7.6 %all-to-all-start = ((f32[16,48,128]{2,1,0:T(8,128)}), f32[16,48,128]{2,1,0:T(8,128)S(1)}, u32[]{:S(2)}, u32[]{:S(2)}) async-start(f32[16,48,128]{2,1,0:T(8,128)} %parcel.1), calls=%async_computation | async-start | bytes 786432 | tf_op jit(solution)/shard_map/all_to_all | solution.py:445
  10.2 0.0 copy-done.9
  10.2 0.0 copy-done.8
  10.2 0.1 fusion.8
  10.3 1.0 %collective-permute-start.1 = (f32[16,60]{1,0:T(8,128)S(1)}, f32[16,60]{1,0:T(8,128)S(1)}, u32[]{:S(2)}, u32[]{:S(2)}) collective-permute-start(f32[16,60]{1,0:T(8,128)S(1)} %get-tuple-element.67), channel_id=1, source_target_pairs={{0,4},{4,0},{8,12},{12,8},{1,5},{5,1},{9,13},{13,9},{2,6},{6,2},{1... | collective-permute-start | bytes 11528 | tf_op jit(solution)/shard_map/ppermute | solution.py:452
  11.3 6.9 %collective-permute-start.2 = (f32[32,60]{1,0:T(8,128)S(1)}, f32[32,60]{1,0:T(8,128)S(1)}, u32[]{:S(2)}, u32[]{:S(2)}) collective-permute-start(f32[32,60]{1,0:T(8,128)S(1)} %pad_maximum_fusion), channel_id=1, source_target_pairs={{0,8},{4,12},{8,0},{12,4},{1,9},{5,13},{9,1},{13,5},{2,10},{6,14},... | collective-permute-start | bytes 23048 | tf_op jit(solution)/shard_map/ppermute | solution.py:452
  18.2 0.0 copy-done.1
  18.3 0.0 copy-done.7
  18.3 0.0 copy-done.6
  18.3 0.0 copy-done.5
  18.3 0.0 copy-done.4
  18.3 0.0 copy-done.3
  18.3 0.0 copy-start.10
  18.3 0.0 copy-start
  18.3 0.0 copy-start.2
  18.3 1.7 %prepare.1 = (f32[5,16,128]{2,1,0:T(8,128)S(1)}, f32[768,128]{1,0:T(8,128)S(1)}, f32[768,128]{1,0:T(8,128)S(1)}, f32[768,128]{1,0:T(8,128)S(1)}, f32[768,128]{1,0:T(8,128)S(1)}) custom-call(s32[1]{0:T(128)} %bitcast.inner_at, f32[16,48]{1,0:T(8,128)S(1)} %copy-done.3, s32[2,8,128]{2,1,0:T(8,128)S(1)} %bitcast.27, s32[2,8,128]{2,1,0:T(8,128)S(1)} %bitcast.28, ...), custom_call_target="tpu_custom_call" | custom-call | flops 16777216000 | bytes 4194304 | tf_op jit(solution)/shard_map/prepare/pallas_call | solution.py:459
  20.0 0.0 collective-permute-done.2.far_rates.far
  20.0 0.4 collective-permute-start.3
  20.5 0.0 copy-done.10
  20.5 0.3 fusion.block_hot
  20.8 0.0 all-to-all-done.plan.plan_own
  20.8 0.2 collective-permute-start
  21.1 0.0 collective-permute-done.1.near_rates.near
  21.1 0.2 collective-permute-done.3.across_rates.across
  21.3 0.0 copy-done
  21.3 0.0 copy-done.2
  21.3 6.3 %first_date_own.1 = (f32[1,2048]{1,0:T(1,128)S(1)}, f32[3,8,128]{2,1,0:T(8,128)S(1)}, f32[1,128]{1,0:T(1,128)S(1)}, f32[36,64,128]{2,1,0:T(8,128)S(1)}, f32[36,64,128]{2,1,0:T(8,128)S(1)}) custom-call(s32[1]{0:T(128)} %bitcast.inner_at, f32[4,24]{1,0:T(4,128)S(1)} %copy-done, f32[4]{0:T(128)S(1)} %copy-done.2, ...), custom_call_target="tpu_custom_call" | custom-call | flops 83886080000 | bytes 20971520 | tf_op jit(solution)/shard_map/first_date_own/pallas_call | solution.py:477
  27.6 0.0 collective-permute-done.plan.plan_other
  27.6 5.8 %first_date_other.1 = (f32[1,2048]{1,0:T(1,128)S(1)}, f32[3,8,128]{2,1,0:T(8,128)S(1)}, f32[1,128]{1,0:T(1,128)S(1)}, f32[1,128]{1,0:T(1,128)S(1)}, f32[1,128]{1,0:T(1,128)S(1)}, /*index=5*/f32[1,128]{1,0:T(1,128)S(1)}) custom-call(s32[1]{0:T(128)} %bitcast.inner_at, s32[1]{0:T(128)} %bitcast.2.cell_at, f32[4,24]{1,0:T(4,128)S(1)} %copy-done, ...), custom_call_target="tpu_custom_call" | custom-call | tf_op jit(solution)/shard_map/first_date_other/pallas_call | solution.py:485
  33.4 1.3 %collective-permute-start.4 = (f32[1,128]{1,0:T(1,128)S(1)}, f32[1,128]{1,0:T(1,128)S(1)}, u32[]{:S(2)}, u32[]{:S(2)}) collective-permute-start(f32[1,128]{1,0:T(1,128)S(1)} %get-tuple-element.47), channel_id=1, source_target_pairs={{0,1},{1,2},{2,3},{3,0},{4,5},{5,6},{6,7},{7,4},{8,9},{9,10},{10,1... | collective-permute-start | bytes 1544 | tf_op jit(solution)/shard_map/ppermute | solution.py:497
  34.8 3.0 %collective-permute-start.5 = (f32[1,128]{1,0:T(1,128)S(1)}, f32[1,128]{1,0:T(1,128)S(1)}, u32[]{:S(2)}, u32[]{:S(2)}) collective-permute-start(f32[1,128]{1,0:T(1,128)S(1)} %get-tuple-element.48), channel_id=1, source_target_pairs={{0,2},{1,3},{2,0},{3,1},{4,6},{5,7},{6,4},{7,5},{8,10},{9,11},{10,... | collective-permute-start | bytes 1544 | tf_op jit(solution)/shard_map/ppermute | solution.py:497
  37.7 0.7 collective-permute-start.6
  38.5 0.6 second_tables.1
  39.1 0.0 collective-permute-done.4.next_one
  39.1 0.0 collective-permute-done.5.next_two
  39.1 1.0 %collective-permute-done.6.next_three = f32[1,128]{1,0:T(1,128)S(1)} collective-permute-done((f32[1,128]{1,0:T(1,128)S(1)}, f32[1,128]{1,0:T(1,128)S(1)}, u32[]{:S(2)}, u32[]{:S(2)}) %collective-permute-start.6) | collective-permute-done | bytes 544 | tf_op jit(solution)/shard_map/ppermute | solution.py:497
  40.1 7.9 %second_date.1 = (f32[2,1,2048]{2,1,0:T(1,128)}, f32[64,4,1,128]{3,2,1,0:T(1,128)S(1)}, f32[1,128]{1,0:T(1,128)S(1)}) custom-call(s32[1]{0:T(128)} %bitcast.inner_at, f32[4,24]{1,0:T(4,128)S(1)} %copy-done, f32[4]{0:T(128)S(1)} %copy-done.2, s32[1]{0:T(128)} %bitcast.1.place, f32[1,128]{1,0:T(1,128)S(1)} %get-tuple-element.46.kept_here, ...), custom_call_target="tpu_custom_call" | custom-call | tf_op jit(solution)/shard_map/second_date/pallas_call | solution.py:505
  48.1 25.8 %all_to_all.10 = f32[256,1,128]{2,1,0:T(1,128)S(1)} all-to-all(f32[256,1,128]{2,1,0:T(1,128)S(1)} %bitcast.24), channel_id=1, replica_groups=mesh['outer'=16,'inner'=4,'cell'=4] {'outer','inner','cell'}, dimensions={0} | all-to-all | bytes 262144 | tf_op jit(solution)/shard_map/all_to_all | solution.py:518
  73.9 0.7 last_sums.1
  (1 shorter events, 0.0 us)
Async XLA Ops:
  0.6 17.6 %copy-start.1 = (f32[2048]{0:T(1024)S(1)}, f32[2048]{0:T(1024)}, u32[]{:S(2)}) copy-start(f32[2048]{0:T(1024)} %param.23) | copy-start | bytes 24580
  0.6 9.5 %copy-start.9 = (f32[4,16,24]{2,1,0:T(8,128)S(1)}, f32[4,16,24]{2,1,0:T(8,128)}, u32[]{:S(2)}) copy-start(f32[4,16,24]{2,1,0:T(8,128)} %param.25) | copy-start | bytes 18436
  0.7 9.5 %copy-start.8 = (f32[4,16,36]{2,1,0:T(8,128)S(1)}, f32[4,16,36]{2,1,0:T(8,128)}, u32[]{:S(2)}) copy-start(f32[4,16,36]{2,1,0:T(8,128)} %param.24) | copy-start | bytes 27652
  0.7 17.6 %copy-start.7 = (f32[2048]{0:T(1024)S(1)}, f32[2048]{0:T(1024)}, u32[]{:S(2)}) copy-start(f32[2048]{0:T(1024)} %param.22) | copy-start | bytes 24580
  0.7 17.6 %copy-start.6 = (f32[2048]{0:T(1024)S(1)}, f32[2048]{0:T(1024)}, u32[]{:S(2)}) copy-start(f32[2048]{0:T(1024)} %param.21) | copy-start | bytes 24580
  0.7 17.6 %copy-start.5 = (s32[2048]{0:T(1024)S(1)}, s32[2048]{0:T(1024)}, u32[]{:S(2)}) copy-start(s32[2048]{0:T(1024)} %param.19) | copy-start | bytes 24580
  0.7 17.6 %copy-start.4 = (s32[2048]{0:T(1024)S(1)}, s32[2048]{0:T(1024)}, u32[]{:S(2)}) copy-start(s32[2048]{0:T(1024)} %param.18) | copy-start | bytes 24580
  0.7 17.6 %copy-start.3 = (f32[16,48]{1,0:T(8,128)S(1)}, f32[16,48]{1,0:T(8,128)}, u32[]{:S(2)}) copy-start(f32[16,48]{1,0:T(8,128)} %lapse_table.1) | copy-start | bytes 9220
  2.5 18.3 %all-to-all-start = ((f32[16,48,128]{2,1,0:T(8,128)}), f32[16,48,128]{2,1,0:T(8,128)S(1)}, u32[]{:S(2)}, u32[]{:S(2)}) async-start(f32[16,48,128]{2,1,0:T(8,128)} %parcel.1), calls=%async_computation | async-start | bytes 786432 | tf_op jit(solution)/shard_map/all_to_all | solution.py:445
  10.3 10.8 %collective-permute-start.1 = (f32[16,60]{1,0:T(8,128)S(1)}, f32[16,60]{1,0:T(8,128)S(1)}, u32[]{:S(2)}, u32[]{:S(2)}) collective-permute-start(f32[16,60]{1,0:T(8,128)S(1)} %get-tuple-element.67), channel_id=1, source_target_pairs={{0,4},{4,0},{8,12},{12,8},{1,5},{5,1},{9,13},{13,9},{2,6},{6,2},{1... | collective-permute-start | bytes 11528 | tf_op jit(solution)/shard_map/ppermute | solution.py:452
  11.3 8.7 %collective-permute-start.2 = (f32[32,60]{1,0:T(8,128)S(1)}, f32[32,60]{1,0:T(8,128)S(1)}, u32[]{:S(2)}, u32[]{:S(2)}) collective-permute-start(f32[32,60]{1,0:T(8,128)S(1)} %pad_maximum_fusion), channel_id=1, source_target_pairs={{0,8},{4,12},{8,0},{12,4},{1,9},{5,13},{9,1},{13,5},{2,10},{6,14},... | collective-permute-start | bytes 23048 | tf_op jit(solution)/shard_map/ppermute | solution.py:452
  18.3 2.2 %copy-start.10 = (s32[2048]{0:T(1024)S(1)}, s32[2048]{0:T(1024)}, u32[]{:S(2)}) copy-start(s32[2048]{0:T(1024)} %param.20) | copy-start | bytes 24580
  18.3 3.0 %copy-start = (f32[4,24]{1,0:T(4,128)S(1)}, f32[4,24]{1,0:T(4,128)}, u32[]{:S(2)}) copy-start(f32[4,24]{1,0:T(4,128)} %world.5) | copy-start | bytes 1156
  18.3 3.0 %copy-start.2 = (f32[4]{0:T(128)S(1)}, f32[4]{0:T(128)}, u32[]{:S(2)}) copy-start(f32[4]{0:T(128)} %spread.5) | copy-start | bytes 52
  20.0 1.3 %collective-permute-start.3 = (f32[32,60]{1,0:T(8,128)S(1)}, f32[32,60]{1,0:T(8,128)S(1)}, u32[]{:S(2)}, u32[]{:S(2)}) collective-permute-start(f32[32,60]{1,0:T(8,128)S(1)} %collective-permute-done.2.far_rates.far), channel_id=1, source_target_pairs={{0,4},{4,0},{8,12},{12,8},{1,5},{5,1},{9,13},{13,9},{2,6},{6,2},{1... | collective-permute-start | bytes 23048 | tf_op jit(solution)/shard_map/ppermute | solution.py:452
  20.8 6.8 %collective-permute-start = (f32[16,48,128]{2,1,0:T(8,128)S(1)}, f32[16,48,128]{2,1,0:T(8,128)S(1)}, u32[]{:S(2)}, u32[]{:S(2)}) collective-permute-start(f32[16,48,128]{2,1,0:T(8,128)S(1)} %all-to-all-done.plan.plan_own), channel_id=1, source_target_pairs={{0,4},{4,0},{8,12},{12,8},{1,5},{5,1},{9,13},{13,9},{2,6},{6,2},{1... | collective-permute-start | bytes 1179656 | tf_op jit(solution)/shard_map/ppermute | solution.py:452
  33.4 5.7 %collective-permute-start.4 = (f32[1,128]{1,0:T(1,128)S(1)}, f32[1,128]{1,0:T(1,128)S(1)}, u32[]{:S(2)}, u32[]{:S(2)}) collective-permute-start(f32[1,128]{1,0:T(1,128)S(1)} %get-tuple-element.47), channel_id=1, source_target_pairs={{0,1},{1,2},{2,3},{3,0},{4,5},{5,6},{6,7},{7,4},{8,9},{9,10},{10,1... | collective-permute-start | bytes 1544 | tf_op jit(solution)/shard_map/ppermute | solution.py:497
  34.8 4.3 %collective-permute-start.5 = (f32[1,128]{1,0:T(1,128)S(1)}, f32[1,128]{1,0:T(1,128)S(1)}, u32[]{:S(2)}, u32[]{:S(2)}) collective-permute-start(f32[1,128]{1,0:T(1,128)S(1)} %get-tuple-element.48), channel_id=1, source_target_pairs={{0,2},{1,3},{2,0},{3,1},{4,6},{5,7},{6,4},{7,5},{8,10},{9,11},{10,... | collective-permute-start | bytes 1544 | tf_op jit(solution)/shard_map/ppermute | solution.py:497
  37.7 2.4 %collective-permute-start.6 = (f32[1,128]{1,0:T(1,128)S(1)}, f32[1,128]{1,0:T(1,128)S(1)}, u32[]{:S(2)}, u32[]{:S(2)}) collective-permute-start(f32[1,128]{1,0:T(1,128)S(1)} %get-tuple-element.49), channel_id=1, source_target_pairs={{0,3},{1,0},{2,1},{3,2},{4,7},{5,4},{6,5},{7,6},{8,11},{9,8},{10,9... | collective-permute-start | bytes 1544 | tf_op jit(solution)/shard_map/ppermute | solution.py:497

commit v4 on v3

--- a/solution.py
+++ b/solution.py
@@ -93,17 +93,6 @@
     lax.fori_loop(0, months, one_month, 0)
 
 
-def fill_first_tables(inner_at, spread, own, near, far, across, credit, discount):
-    lines = own.shape[0]
-    for part, rates in enumerate((own[...], near[...], far[:lines, :], across[lines:, :])):
-        at = slice(part * lines, (part + 1) * lines)
-        crediting = 1.0 + jnp.maximum(rates - spread[inner_at[0]], credit_floor)
-        discounting = jnp.exp(-rates)
-        for m in range(credit.shape[0]):
-            credit[m, at, :] = jnp.broadcast_to(crediting[:, m : m + 1], (lines, LANES))
-            discount[m, at, :] = jnp.broadcast_to(discounting[:, m : m + 1], (lines, LANES))
-
-
 def second_table_kernel(own, near, far, across, rate, discount):
     first = own.shape[1] - rate.shape[0]
     lines = own.shape[0]
@@ -139,7 +128,8 @@
 
 
 def inner_paths(
-    start, part, target, plan, level, low, high, lapse, cells, rows, credit, discount, kept_accounts, kept_growth, reserve
+    start, part, target, plan, level, low, high, lapse, cells, rows, credit, discount, kept_accounts, kept_growth, reserve,
+    narrow=None,
 ):
     count = cells.shape[1]
     own = count // CORES
@@ -152,7 +142,14 @@
     def group(ref, m, g):
         return ref[m, SUBLANES * g : SUBLANES * (g + 1), :]
 
-    def tiles_step(step, total):
+    def tiles_step(step, total, narrow=None):
+        def of_paths(table, which, o, g):
+            if narrow is None:
+                return group(table, o, g)
+            value = jnp.broadcast_to(narrow[which, SUBLANES * g : SUBLANES * (g + 1), o : o + 1], full)
+            table[o, SUBLANES * g : SUBLANES * (g + 1), :] = value
+            return value
+
         def spread_out(ref, i, m):
             return jnp.broadcast_to(ref[pl.ds(m * count + part * own + step * TOGETHER + i, 1), :], full)
 
@@ -182,7 +179,7 @@
             if o < PERIOD:
                 flow = [flow[i] * base[i] for i in tiles]
             for g in range(groups):
-                crediting = group(credit, o, g)
+                crediting = of_paths(credit, 0, o, g)
                 for i in tiles:
                     term = flow[i] if o < PERIOD else flow[i] * per_guarantee[i][g]
                     account[i][g] = jnp.maximum(account[i][g] + term, 0.0) * crediting
@@ -206,6 +203,7 @@
         worth = [[None] * groups for i in tiles]
         for o in reversed(range(months)):
             m = start + o
+            discounting = [None] * groups
             for i in tiles:
                 unit, least, most = spread_out(level, i, m), spread_out(low, i, m), spread_out(high, i, m)
                 lapsing = spread_out(lapse, i, m)
@@ -226,7 +224,9 @@
                             later = later * of_tile(kept_growth, i, o // PERIOD, g)
                         bounded = jnp.minimum(jnp.maximum(after, least), most)
                         value = value + (staying - lapsing * bounded) * later
-                    worth[i][g] = value * group(discount, o, g)
+                    if i == 0:
+                        discounting[g] = of_paths(discount, 1, o, g)
+                    worth[i][g] = value * discounting[g]
         for i in tiles:
             summed = worth[i][0]
             for g in range(1, groups):
@@ -238,7 +238,10 @@
             total = total + row
         return total
 
-    return lax.fori_loop(0, own // TOGETHER, tiles_step, jnp.zeros((1, LANES), jnp.float32))
+    total = jnp.zeros((1, LANES), jnp.float32)
+    if narrow is not None:
+        total = tiles_step(0, total, narrow)
+    return lax.fori_loop(0 if narrow is None else 1, own // TOGETHER, tiles_step, total)
 
 
 def block_sums(value, parts, block_hot):
@@ -251,7 +254,7 @@
     return sums[0:1, :] + sums[1:2, :] + sums[2:3, :]
 
 
-def first_half(part, inner_at, world, spread, plan, level, low, high, lapse, cells, credit, discount, reserve, rows, kept_accounts, kept_growth):
+def first_half(part, inner_at, world, spread, plan, level, low, high, lapse, cells, credit, discount, reserve, rows, kept_accounts, kept_growth, narrow=None):
     own = cells.shape[1] // CORES
     at, here = inner_at[0], lines_of(part, own)
     half = lax.rem(at, CORES)
@@ -266,17 +269,21 @@
         rows[r] = value
     target = (half if part == 0 else 1 - half) * own
     return inner_paths(
-        PERIOD, part, target, plan, level, low, high, lapse, cells, rows, credit, discount, kept_accounts, kept_growth, reserve
+        PERIOD, part, target, plan, level, low, high, lapse, cells, rows, credit, discount, kept_accounts, kept_growth, reserve, narrow
     )
 
 
 def first_own_kernel(
     inner_at, world, spread, plan, level, low, high, lapse, cells, own_rates, near_rates, far_rates, across_rates,
-    reserve, rows, total, credit, discount, kept_accounts, kept_growth,
+    reserve, rows, total, credit, discount, kept_accounts, kept_growth, narrow,
 ):
-    fill_first_tables(inner_at, spread, own_rates, near_rates, far_rates, across_rates, credit, discount)
+    lines = own_rates.shape[0]
+    for part, rates in enumerate((own_rates[...], near_rates[...], far_rates[:lines, :], across_rates[lines:, :])):
+        at = slice(part * lines, (part + 1) * lines)
+        narrow[0, at, :] = 1.0 + jnp.maximum(rates - spread[inner_at[0]], credit_floor)
+        narrow[1, at, :] = jnp.exp(-rates)
     total[...] = first_half(
-        0, inner_at, world, spread, plan, level, low, high, lapse, cells, credit, discount, reserve, rows, kept_accounts, kept_growth
+        0, inner_at, world, spread, plan, level, low, high, lapse, cells, credit, discount, reserve, rows, kept_accounts, kept_growth, narrow
     )
 
 
@@ -479,7 +486,7 @@
         "first_date_own",
         [floats(1, local), state, line, table, table],
         [SMEM] * 3 + [VMEM] * 10,
-        inner_scratch(months_one),
+        inner_scratch(months_one) + [held(2, paths, months_one + months_two)],
         read=20 * MEBI,
     )(inner_one, world_rates, spread, plan_own, *coefs, cells, *shares)
     reserve_one, rows_other, kept_here, *others = call(

time: 74.9 us -> 74.4 us (level)
  no operation moved by 1% of the time
where the time goes in v4:
time: 74.4 us; the launch traced here: 74.1 us
  blocking collectives  25.8 us (35%)
  Pallas kernels  24.3 us (33%)
  starting transfers between devices  21.3 us (29%)
  waiting for transfers between devices  1.28 us (2%)
  between operations  0.88 us (1%)
    all_to_all x1, blocking collectives, body(): lax.all_to_all(parcel.reshape(-1, 1, LANES), ALL, 0, 0, tiled=True)  25.8 us
    ppermute x4, starting transfers between devices, swapped(): return lax.ppermute(value, 'inner', [(j, j ^ s) for j in range(inner_size)])  8.66 us
    pallas_call x1, Pallas kernels, body(): call(functools.partial(second_kernel, cells_all), 'second_date', [floats(...  7.94 us
    all_to_all x1, starting transfers between devices, body(): plan_own = lax.all_to_all(sent, 'outer', 0, 0, tiled=True)  7.6 us
    pallas_call x1, Pallas kernels, body(): call(functools.partial(first_other_kernel, cell_size), 'first_date_other'...  5.84 us
    pallas_call x1, Pallas kernels, body(): call(first_own_kernel, 'first_date_own', [floats(1, local), state, line,...  5.75 us
    ppermute x3, starting transfers between devices, body(): lax.ppermute(others[s - 1], 'cell', [(k, (k + s) % cell_size) for k in ra...  5.04 us
    pallas_call x1, Pallas kernels, body(): call(parcel_kernel, 'parcel', floats(outer_size, 2 * each * own, LANES),...  1.81 us
  transfers between devices with their start and end apart: 8, of which 2 were waited for; matrix products, arithmetic and copies ran while one was open for 1% of the time, Pallas kernels for 11%

profile of v4, /device:TPU:1, one launch (start us, length us, event | category | flops | bytes accessed | tf_op | source)
XLA Modules:
  0.0 74.1 jit_solution(15525085419587421305)
XLA Ops:
  0.6 0.0 copy-start.1
  0.6 0.0 copy-start.9
  0.7 0.0 copy-start.8
  0.7 0.0 copy-start.7
  0.7 0.0 copy-start.6
  0.7 0.0 copy-start.5
  0.7 0.0 copy-start.4
  0.7 0.0 copy-start.3
  0.7 1.8 %parcel.1 = f32[16,48,128]{2,1,0:T(8,128)} custom-call(s32[1]{0:T(128)} %bitcast.3.outer_at, s32[1]{0:T(128)} %bitcast.inner_at, f32[3,2048]{1,0:T(4,128)} %premium.1, f32[3,2048]{1,0:T(4,128)} %charge.1, f32[3,2048]{1,0:T(4,128)} %mortality.1, f32[2,8,128]{2,1,0:T(8,128)} %bitcast.25), custom_call_target="tpu_custom_call" | custom-call | tf_op jit(solution)/shard_map/parcel/pallas_call | solution.py:435
  2.5 7.6 %all-to-all-start = ((f32[16,48,128]{2,1,0:T(8,128)}), f32[16,48,128]{2,1,0:T(8,128)S(1)}, u32[]{:S(2)}, u32[]{:S(2)}) async-start(f32[16,48,128]{2,1,0:T(8,128)} %parcel.1), calls=%async_computation | async-start | bytes 786432 | tf_op jit(solution)/shard_map/all_to_all | solution.py:452
  10.2 0.0 copy-done.9
  10.2 0.0 copy-done.8
  10.2 0.1 fusion.8
  10.3 1.0 %collective-permute-start.1 = (f32[16,60]{1,0:T(8,128)S(1)}, f32[16,60]{1,0:T(8,128)S(1)}, u32[]{:S(2)}, u32[]{:S(2)}) collective-permute-start(f32[16,60]{1,0:T(8,128)S(1)} %get-tuple-element.67), channel_id=1, source_target_pairs={{0,4},{4,0},{8,12},{12,8},{1,5},{5,1},{9,13},{13,9},{2,6},{6,2},{1... | collective-permute-start | bytes 11528 | tf_op jit(solution)/shard_map/ppermute | solution.py:459
  11.3 6.9 %collective-permute-start.2 = (f32[32,60]{1,0:T(8,128)S(1)}, f32[32,60]{1,0:T(8,128)S(1)}, u32[]{:S(2)}, u32[]{:S(2)}) collective-permute-start(f32[32,60]{1,0:T(8,128)S(1)} %pad_maximum_fusion), channel_id=1, source_target_pairs={{0,8},{4,12},{8,0},{12,4},{1,9},{5,13},{9,1},{13,5},{2,10},{6,14},... | collective-permute-start | bytes 23048 | tf_op jit(solution)/shard_map/ppermute | solution.py:459
  18.2 0.0 copy-done.1
  18.3 0.0 copy-done.7
  18.3 0.0 copy-done.6
  18.3 0.0 copy-done.5
  18.3 0.0 copy-done.4
  18.3 0.0 copy-done.3
  18.3 0.0 copy-start.10
  18.3 0.0 copy-start
  18.3 0.0 copy-start.2
  18.3 1.7 %prepare.1 = (f32[5,16,128]{2,1,0:T(8,128)S(1)}, f32[768,128]{1,0:T(8,128)S(1)}, f32[768,128]{1,0:T(8,128)S(1)}, f32[768,128]{1,0:T(8,128)S(1)}, f32[768,128]{1,0:T(8,128)S(1)}) custom-call(s32[1]{0:T(128)} %bitcast.inner_at, f32[16,48]{1,0:T(8,128)S(1)} %copy-done.3, s32[2,8,128]{2,1,0:T(8,128)S(1)} %bitcast.27, s32[2,8,128]{2,1,0:T(8,128)S(1)} %bitcast.28, ...), custom_call_target="tpu_custom_call" | custom-call | flops 16777216000 | bytes 4194304 | tf_op jit(solution)/shard_map/prepare/pallas_call | solution.py:466
  20.0 0.0 collective-permute-done.2.far_rates.far
  20.0 0.4 collective-permute-start.3
  20.5 0.0 copy-done.10
  20.5 0.3 fusion.block_hot
  20.8 0.0 all-to-all-done.plan.plan_own
  20.8 0.2 collective-permute-start
  21.1 0.0 collective-permute-done.1.near_rates.near
  21.1 0.2 collective-permute-done.3.across_rates.across
  21.3 0.0 copy-done
  21.3 0.0 copy-done.2
  21.3 5.7 %first_date_own.1 = (f32[1,2048]{1,0:T(1,128)S(1)}, f32[3,8,128]{2,1,0:T(8,128)S(1)}, f32[1,128]{1,0:T(1,128)S(1)}, f32[36,64,128]{2,1,0:T(8,128)S(1)}, f32[36,64,128]{2,1,0:T(8,128)S(1)}) custom-call(s32[1]{0:T(128)} %bitcast.inner_at, f32[4,24]{1,0:T(4,128)S(1)} %copy-done, f32[4]{0:T(128)S(1)} %copy-done.2, ...), custom_call_target="tpu_custom_call" | custom-call | flops 83886080000 | bytes 20971520 | tf_op jit(solution)/shard_map/first_date_own/pallas_call | solution.py:484
  27.1 0.0 collective-permute-done.plan.plan_other
  27.1 5.8 %first_date_other.1 = (f32[1,2048]{1,0:T(1,128)S(1)}, f32[3,8,128]{2,1,0:T(8,128)S(1)}, f32[1,128]{1,0:T(1,128)S(1)}, f32[1,128]{1,0:T(1,128)S(1)}, f32[1,128]{1,0:T(1,128)S(1)}, /*index=5*/f32[1,128]{1,0:T(1,128)S(1)}) custom-call(s32[1]{0:T(128)} %bitcast.inner_at, s32[1]{0:T(128)} %bitcast.2.cell_at, f32[4,24]{1,0:T(4,128)S(1)} %copy-done, ...), custom_call_target="tpu_custom_call" | custom-call | tf_op jit(solution)/shard_map/first_date_other/pallas_call | solution.py:492
  32.9 1.3 %collective-permute-start.4 = (f32[1,128]{1,0:T(1,128)S(1)}, f32[1,128]{1,0:T(1,128)S(1)}, u32[]{:S(2)}, u32[]{:S(2)}) collective-permute-start(f32[1,128]{1,0:T(1,128)S(1)} %get-tuple-element.47), channel_id=1, source_target_pairs={{0,1},{1,2},{2,3},{3,0},{4,5},{5,6},{6,7},{7,4},{8,9},{9,10},{10,1... | collective-permute-start | bytes 1544 | tf_op jit(solution)/shard_map/ppermute | solution.py:504
  34.2 3.0 %collective-permute-start.5 = (f32[1,128]{1,0:T(1,128)S(1)}, f32[1,128]{1,0:T(1,128)S(1)}, u32[]{:S(2)}, u32[]{:S(2)}) collective-permute-start(f32[1,128]{1,0:T(1,128)S(1)} %get-tuple-element.48), channel_id=1, source_target_pairs={{0,2},{1,3},{2,0},{3,1},{4,6},{5,7},{6,4},{7,5},{8,10},{9,11},{10,... | collective-permute-start | bytes 1544 | tf_op jit(solution)/shard_map/ppermute | solution.py:504
  37.2 0.7 collective-permute-start.6
  37.9 0.6 second_tables.1
  38.6 0.0 collective-permute-done.4.next_one
  38.6 0.0 collective-permute-done.5.next_two
  38.6 1.0 %collective-permute-done.6.next_three = f32[1,128]{1,0:T(1,128)S(1)} collective-permute-done((f32[1,128]{1,0:T(1,128)S(1)}, f32[1,128]{1,0:T(1,128)S(1)}, u32[]{:S(2)}, u32[]{:S(2)}) %collective-permute-start.6) | collective-permute-done | bytes 544 | tf_op jit(solution)/shard_map/ppermute | solution.py:504
  39.6 7.9 %second_date.1 = (f32[2,1,2048]{2,1,0:T(1,128)}, f32[64,4,1,128]{3,2,1,0:T(1,128)S(1)}, f32[1,128]{1,0:T(1,128)S(1)}) custom-call(s32[1]{0:T(128)} %bitcast.inner_at, f32[4,24]{1,0:T(4,128)S(1)} %copy-done, f32[4]{0:T(128)S(1)} %copy-done.2, s32[1]{0:T(128)} %bitcast.1.place, f32[1,128]{1,0:T(1,128)S(1)} %get-tuple-element.46.kept_here, ...), custom_call_target="tpu_custom_call" | custom-call | tf_op jit(solution)/shard_map/second_date/pallas_call | solution.py:512
  47.5 25.8 %all_to_all.10 = f32[256,1,128]{2,1,0:T(1,128)S(1)} all-to-all(f32[256,1,128]{2,1,0:T(1,128)S(1)} %bitcast.24), channel_id=1, replica_groups=mesh['outer'=16,'inner'=4,'cell'=4] {'outer','inner','cell'}, dimensions={0} | all-to-all | bytes 262144 | tf_op jit(solution)/shard_map/all_to_all | solution.py:525
  73.4 0.7 last_sums.1
  (1 shorter events, 0.0 us)
Async XLA Ops:
  0.6 17.6 %copy-start.1 = (f32[2048]{0:T(1024)S(1)}, f32[2048]{0:T(1024)}, u32[]{:S(2)}) copy-start(f32[2048]{0:T(1024)} %param.23) | copy-start | bytes 24580
  0.6 9.5 %copy-start.9 = (f32[4,16,24]{2,1,0:T(8,128)S(1)}, f32[4,16,24]{2,1,0:T(8,128)}, u32[]{:S(2)}) copy-start(f32[4,16,24]{2,1,0:T(8,128)} %param.25) | copy-start | bytes 18436
  0.7 9.5 %copy-start.8 = (f32[4,16,36]{2,1,0:T(8,128)S(1)}, f32[4,16,36]{2,1,0:T(8,128)}, u32[]{:S(2)}) copy-start(f32[4,16,36]{2,1,0:T(8,128)} %param.24) | copy-start | bytes 27652
  0.7 17.6 %copy-start.7 = (f32[2048]{0:T(1024)S(1)}, f32[2048]{0:T(1024)}, u32[]{:S(2)}) copy-start(f32[2048]{0:T(1024)} %param.22) | copy-start | bytes 24580
  0.7 17.6 %copy-start.6 = (f32[2048]{0:T(1024)S(1)}, f32[2048]{0:T(1024)}, u32[]{:S(2)}) copy-start(f32[2048]{0:T(1024)} %param.21) | copy-start | bytes 24580
  0.7 17.6 %copy-start.5 = (s32[2048]{0:T(1024)S(1)}, s32[2048]{0:T(1024)}, u32[]{:S(2)}) copy-start(s32[2048]{0:T(1024)} %param.19) | copy-start | bytes 24580
  0.7 17.6 %copy-start.4 = (s32[2048]{0:T(1024)S(1)}, s32[2048]{0:T(1024)}, u32[]{:S(2)}) copy-start(s32[2048]{0:T(1024)} %param.18) | copy-start | bytes 24580
  0.7 17.6 %copy-start.3 = (f32[16,48]{1,0:T(8,128)S(1)}, f32[16,48]{1,0:T(8,128)}, u32[]{:S(2)}) copy-start(f32[16,48]{1,0:T(8,128)} %lapse_table.1) | copy-start | bytes 9220
  2.5 18.3 %all-to-all-start = ((f32[16,48,128]{2,1,0:T(8,128)}), f32[16,48,128]{2,1,0:T(8,128)S(1)}, u32[]{:S(2)}, u32[]{:S(2)}) async-start(f32[16,48,128]{2,1,0:T(8,128)} %parcel.1), calls=%async_computation | async-start | bytes 786432 | tf_op jit(solution)/shard_map/all_to_all | solution.py:452
  10.3 10.8 %collective-permute-start.1 = (f32[16,60]{1,0:T(8,128)S(1)}, f32[16,60]{1,0:T(8,128)S(1)}, u32[]{:S(2)}, u32[]{:S(2)}) collective-permute-start(f32[16,60]{1,0:T(8,128)S(1)} %get-tuple-element.67), channel_id=1, source_target_pairs={{0,4},{4,0},{8,12},{12,8},{1,5},{5,1},{9,13},{13,9},{2,6},{6,2},{1... | collective-permute-start | bytes 11528 | tf_op jit(solution)/shard_map/ppermute | solution.py:459
  11.3 8.7 %collective-permute-start.2 = (f32[32,60]{1,0:T(8,128)S(1)}, f32[32,60]{1,0:T(8,128)S(1)}, u32[]{:S(2)}, u32[]{:S(2)}) collective-permute-start(f32[32,60]{1,0:T(8,128)S(1)} %pad_maximum_fusion), channel_id=1, source_target_pairs={{0,8},{4,12},{8,0},{12,4},{1,9},{5,13},{9,1},{13,5},{2,10},{6,14},... | collective-permute-start | bytes 23048 | tf_op jit(solution)/shard_map/ppermute | solution.py:459
  18.3 2.2 %copy-start.10 = (s32[2048]{0:T(1024)S(1)}, s32[2048]{0:T(1024)}, u32[]{:S(2)}) copy-start(s32[2048]{0:T(1024)} %param.20) | copy-start | bytes 24580
  18.3 3.0 %copy-start = (f32[4,24]{1,0:T(4,128)S(1)}, f32[4,24]{1,0:T(4,128)}, u32[]{:S(2)}) copy-start(f32[4,24]{1,0:T(4,128)} %world.5) | copy-start | bytes 1156
  18.3 3.0 %copy-start.2 = (f32[4]{0:T(128)S(1)}, f32[4]{0:T(128)}, u32[]{:S(2)}) copy-start(f32[4]{0:T(128)} %spread.5) | copy-start | bytes 52
  20.0 1.3 %collective-permute-start.3 = (f32[32,60]{1,0:T(8,128)S(1)}, f32[32,60]{1,0:T(8,128)S(1)}, u32[]{:S(2)}, u32[]{:S(2)}) collective-permute-start(f32[32,60]{1,0:T(8,128)S(1)} %collective-permute-done.2.far_rates.far), channel_id=1, source_target_pairs={{0,4},{4,0},{8,12},{12,8},{1,5},{5,1},{9,13},{13,9},{2,6},{6,2},{1... | collective-permute-start | bytes 23048 | tf_op jit(solution)/shard_map/ppermute | solution.py:459
  20.8 6.2 %collective-permute-start = (f32[16,48,128]{2,1,0:T(8,128)S(1)}, f32[16,48,128]{2,1,0:T(8,128)S(1)}, u32[]{:S(2)}, u32[]{:S(2)}) collective-permute-start(f32[16,48,128]{2,1,0:T(8,128)S(1)} %all-to-all-done.plan.plan_own), channel_id=1, source_target_pairs={{0,4},{4,0},{8,12},{12,8},{1,5},{5,1},{9,13},{13,9},{2,6},{6,2},{1... | collective-permute-start | bytes 1179656 | tf_op jit(solution)/shard_map/ppermute | solution.py:459
  32.9 5.7 %collective-permute-start.4 = (f32[1,128]{1,0:T(1,128)S(1)}, f32[1,128]{1,0:T(1,128)S(1)}, u32[]{:S(2)}, u32[]{:S(2)}) collective-permute-start(f32[1,128]{1,0:T(1,128)S(1)} %get-tuple-element.47), channel_id=1, source_target_pairs={{0,1},{1,2},{2,3},{3,0},{4,5},{5,6},{6,7},{7,4},{8,9},{9,10},{10,1... | collective-permute-start | bytes 1544 | tf_op jit(solution)/shard_map/ppermute | solution.py:504
  34.2 4.3 %collective-permute-start.5 = (f32[1,128]{1,0:T(1,128)S(1)}, f32[1,128]{1,0:T(1,128)S(1)}, u32[]{:S(2)}, u32[]{:S(2)}) collective-permute-start(f32[1,128]{1,0:T(1,128)S(1)} %get-tuple-element.48), channel_id=1, source_target_pairs={{0,2},{1,3},{2,0},{3,1},{4,6},{5,7},{6,4},{7,5},{8,10},{9,11},{10,... | collective-permute-start | bytes 1544 | tf_op jit(solution)/shard_map/ppermute | solution.py:504
  37.2 2.4 %collective-permute-start.6 = (f32[1,128]{1,0:T(1,128)S(1)}, f32[1,128]{1,0:T(1,128)S(1)}, u32[]{:S(2)}, u32[]{:S(2)}) collective-permute-start(f32[1,128]{1,0:T(1,128)S(1)} %get-tuple-element.49), channel_id=1, source_target_pairs={{0,3},{1,0},{2,1},{3,2},{4,7},{5,4},{6,5},{7,6},{8,11},{9,8},{10,9... | collective-permute-start | bytes 1544 | tf_op jit(solution)/shard_map/ppermute | solution.py:504

commit v5 on v4

--- a/solution.py
+++ b/solution.py
@@ -60,8 +60,10 @@
 
 
 def prepare_kernel(
-    inner_at, lapse_table, lapse_index, kind, account, guarantee, fee_rate, cells, level, low, high, lapse, indices
+    inner_at, lapse_table, lapse_index, kind, account, guarantee, fee_rate, rates,
+    cells, level, low, high, lapse, rates_after, indices,
 ):
+    rates_after[...] = rates[...]
     half = lax.rem(inner_at[0], CORES)
     for part, source in enumerate((half, 1 - half)):
         at = lines_of(part, kind.shape[1])
@@ -343,17 +345,20 @@
     loss = (discount_world * total_two - kept_here[...]) / cells_all
     lane = lax.broadcasted_iota(jnp.int32, (1, LANES), 1)
     loss = jnp.where(lane == half + place[0], loss, 0.0)
-    for k in range(parcel.shape[1]):
-        line = jnp.concatenate([sums[:, half * k : half * (k + 1)], loss[:, half:]], axis=1)
-        parcel[:, k] = jnp.broadcast_to(line[None], (parcel.shape[0], 1, LANES))
-
-
-def last_kernel(place, received, blocks_one, block_reserve, capital):
-    outers, owners = received.shape[0], received.shape[1]
+    lines = [
+        jnp.concatenate([sums[:, half * k : half * (k + 1)], loss[:, half:]], axis=1) for k in range(sums.shape[1] // half)
+    ]
+    lines = jnp.concatenate(lines * (SUBLANES // len(lines)), axis=0)
+    for at in range(0, parcel.shape[0], SUBLANES):
+        parcel[at : at + SUBLANES, :] = lines
+
+
+def last_kernel(owners, place, received, blocks_one, block_reserve, capital):
     half = LANES // 2
-    losses = received[:, 0, 0, :]
+    outers = received.shape[0] // owners
+    losses = received[pl.ds(0, outers, stride=owners), :]
     for k in range(1, owners):
-        losses = losses + received[:, k, 0, :]
+        losses = losses + received[pl.ds(k, outers, stride=owners), :]
     lane = lax.broadcasted_iota(jnp.int32, losses.shape, 1) - half
     losses = jnp.where(lane >= 0, losses, 0.0)
     across = jnp.sum(losses, axis=0, keepdims=True)
@@ -365,9 +370,9 @@
     count_top = outers // 4
     chosen = jnp.where(rank < count_top - 0.5, down, 0.0)
     capital[...] = jnp.broadcast_to(jnp.sum(chosen, axis=0, keepdims=True) / count_top, capital.shape)
-    blocks = received[place[0], 0]
+    blocks = received[pl.ds(place[0] * owners, 1), :]
     for k in range(1, owners):
-        blocks = blocks + received[place[0], k]
+        blocks = blocks + received[pl.ds(place[0] * owners + k, 1), :]
     block_reserve[0] = blocks_one[:, :half]
     block_reserve[1] = blocks[:, :half]
 
@@ -459,15 +464,17 @@
         return lax.ppermute(value, "inner", [(j, j ^ s) for j in range(inner_size)])
 
     far_rates = swapped(far_rates, CORES)
-    near_rates = swapped(near_rates, 1)
     across_rates = swapped(far_rates, 1)
-    shares = [own_rates, near_rates, far_rates, across_rates]
     coefs = [floats(5, count, LANES)] + [floats(months_all * count, LANES)] * 4
-    cells, *coefs = call(prepare_kernel, "prepare", coefs, [SMEM] * 2 + [VMEM] * 5, [pltpu.VMEM((count, LANES), jnp.int32)], read=4 * MEBI)(
+    coefs += [floats(*near_rates.shape)]
+    cells, *coefs, near_rates = call(prepare_kernel, "prepare", coefs, [SMEM] * 2 + [VMEM] * 6, [pltpu.VMEM((count, LANES), jnp.int32)], read=4 * MEBI)(
         inner_one,
         lapse_table,
         *(halves(a) for a in (lapse_index, guarantee_type, account_start, guarantee_start, fee_rate)),
-    )
+        near_rates,
+    )
+    near_rates = swapped(near_rates, 1)
+    shares = [own_rates, near_rates, far_rates, across_rates]
     block_hot = (block_index[:, None] == jnp.arange(block_count)[None, :]).astype(jnp.bfloat16)
 
     plan_other = swapped(plan_own, 1)
@@ -512,7 +519,7 @@
     reserves, parcel, blocks_one = call(
         functools.partial(second_kernel, cells_all),
         "second_date",
-        [floats(2, 1, local), floats(outer_size * inner_size, cell_size, 1, LANES), line],
+        [floats(2, 1, local), floats(outer_size * inner_size * cell_size, LANES), line],
         [SMEM] * 4 + [VMEM] * 17,
         [held(CORES, 3, own, LANES), held(1, local), held(months_two, paths, LANES)]
         + inner_scratch(months_two)
@@ -522,10 +529,10 @@
         plan_own, plan_other, *coefs, cells, rate_two, discount_two, rows_own, rows_other, reserve_one, block_hot,
     )
 
-    received = lax.all_to_all(parcel.reshape(-1, 1, LANES), ALL, 0, 0, tiled=True)
+    received = lax.all_to_all(parcel, ALL, 0, 0, tiled=True)
     block_reserve, capital = call(
-        last_kernel, "last_sums", [floats(2, 1, block_count // cell_size), line], [SMEM] + [VMEM] * 2
-    )(place, received.reshape(parcel.shape), blocks_one)
+        functools.partial(last_kernel, cell_size), "last_sums", [floats(2, 1, block_count // cell_size), line], [SMEM] + [VMEM] * 2
+    )(place, received, blocks_one)
     return reserves, block_reserve, capital[0, :1]
 
 

time: 74.4 us -> 74.3 us (level)
  no operation moved by 1% of the time
where the time goes in v5:
time: 74.3 us; the launch traced here: 74 us
  blocking collectives  25.7 us (35%)
  Pallas kernels  24.3 us (33%)
  starting transfers between devices  21.3 us (29%)
  waiting for transfers between devices  1.26 us (2%)
  between operations  0.88 us (1%)
    all_to_all x1, blocking collectives, body(): received = lax.all_to_all(parcel, ALL, 0, 0, tiled=True)  25.7 us
    ppermute x4, starting transfers between devices, swapped(): return lax.ppermute(value, 'inner', [(j, j ^ s) for j in range(inner_size)])  8.92 us
    pallas_call x1, Pallas kernels, body(): call(functools.partial(second_kernel, cells_all), 'second_date', [floats(...  7.97 us
    all_to_all x1, starting transfers between devices, body(): plan_own = lax.all_to_all(sent, 'outer', 0, 0, tiled=True)  7.6 us
    pallas_call x1, Pallas kernels, body(): call(functools.partial(first_other_kernel, cell_size), 'first_date_other'...  5.83 us
    pallas_call x1, Pallas kernels, body(): call(first_own_kernel, 'first_date_own', [floats(1, local), state, line,...  5.75 us
    ppermute x3, starting transfers between devices, body(): lax.ppermute(others[s - 1], 'cell', [(k, (k + s) % cell_size) for k in ra...  4.8 us
    pallas_call x1, Pallas kernels, body(): call(parcel_kernel, 'parcel', floats(outer_size, 2 * each * own, LANES),...  1.81 us
  transfers between devices with their start and end apart: 8, of which 2 were waited for; matrix products, arithmetic and copies ran while one was open for 1% of the time, Pallas kernels for 11%

profile of v5, /device:TPU:1, one launch (start us, length us, event | category | flops | bytes accessed | tf_op | source)
XLA Modules:
  0.0 74.0 jit_solution(2003599529188634517)
XLA Ops:
  0.6 0.0 copy-start.1
  0.6 0.0 copy-start.9
  0.7 0.0 copy-start.8
  0.7 0.0 copy-start.7
  0.7 0.0 copy-start.6
  0.7 0.0 copy-start.5
  0.7 0.0 copy-start.4
  0.7 0.0 copy-start.3
  0.7 1.8 %parcel.1 = f32[16,48,128]{2,1,0:T(8,128)} custom-call(s32[1]{0:T(128)} %bitcast.3.outer_at, s32[1]{0:T(128)} %bitcast.inner_at, f32[3,2048]{1,0:T(4,128)} %premium.1, f32[3,2048]{1,0:T(4,128)} %charge.1, f32[3,2048]{1,0:T(4,128)} %mortality.1, f32[2,8,128]{2,1,0:T(8,128)} %bitcast.25), custom_call_target="tpu_custom_call" | custom-call | tf_op jit(solution)/shard_map/parcel/pallas_call | solution.py:440
  2.5 7.6 %all-to-all-start = ((f32[16,48,128]{2,1,0:T(8,128)}), f32[16,48,128]{2,1,0:T(8,128)S(1)}, u32[]{:S(2)}, u32[]{:S(2)}) async-start(f32[16,48,128]{2,1,0:T(8,128)} %parcel.1), calls=%async_computation | async-start | bytes 786432 | tf_op jit(solution)/shard_map/all_to_all | solution.py:457
  10.2 0.0 copy-done.9
  10.2 0.0 copy-done.8
  10.2 0.1 fusion.8
  10.3 7.0 %collective-permute-start.2 = (f32[32,60]{1,0:T(8,128)S(1)}, f32[32,60]{1,0:T(8,128)S(1)}, u32[]{:S(2)}, u32[]{:S(2)}) collective-permute-start(f32[32,60]{1,0:T(8,128)S(1)} %pad_maximum_fusion), channel_id=1, source_target_pairs={{0,8},{4,12},{8,0},{12,4},{1,9},{5,13},{9,1},{13,5},{2,10},{6,14},... | collective-permute-start | bytes 23048 | tf_op jit(solution)/shard_map/ppermute | solution.py:464
  17.3 0.0 copy-done.1
  17.3 0.0 copy-done.7
  17.3 0.0 copy-done.6
  17.3 0.0 copy-done.5
  17.3 0.0 copy-done.4
  17.3 0.0 copy-done.3
  17.3 0.0 copy-start.10
  17.3 0.0 copy-start
  17.3 0.0 copy-start.2
  17.3 1.7 %prepare.1 = (f32[5,16,128]{2,1,0:T(8,128)S(1)}, f32[768,128]{1,0:T(8,128)S(1)}, f32[768,128]{1,0:T(8,128)S(1)}, f32[768,128]{1,0:T(8,128)S(1)}, f32[768,128]{1,0:T(8,128)S(1)}, /*index=5*/f32[16,60]{1,0:T(8,128)S(1)}) custom-call(s32[1]{0:T(128)} %bitcast.inner_at, f32[16,48]{1,0:T(8,128)S(1)} %copy-done.3, s32[2,8,128]{2,1,0:T(8,128)S(1)} %bitcast.27, ...), custom_call_target="tpu_custom_call" | custom-call | flops 16777216000 | bytes 4194304 | tf_op jit(solution)/shard_map/prepare/pallas_call | solution.py:470
  19.0 1.3 %collective-permute-start.1 = (f32[16,60]{1,0:T(8,128)S(1)}, f32[16,60]{1,0:T(8,128)S(1)}, u32[]{:S(2)}, u32[]{:S(2)}) collective-permute-start(f32[16,60]{1,0:T(8,128)S(1)} %get-tuple-element.43), channel_id=1, source_target_pairs={{0,4},{4,0},{8,12},{12,8},{1,5},{5,1},{9,13},{13,9},{2,6},{6,2},{1... | collective-permute-start | bytes 11528 | tf_op jit(solution)/shard_map/ppermute | solution.py:464
  20.3 0.0 collective-permute-done.2.far_rates.far
  20.3 0.1 collective-permute-start.3
  20.5 0.0 copy-done.10
  20.5 0.3 fusion.block_hot
  20.8 0.0 all-to-all-done.plan.plan_own
  20.8 0.5 collective-permute-start
  21.3 0.0 collective-permute-done.1.near_rates.near
  21.3 0.2 collective-permute-done.3.across_rates.across
  21.5 0.0 copy-done
  21.5 0.0 copy-done.2
  21.5 5.7 %first_date_own.1 = (f32[1,2048]{1,0:T(1,128)S(1)}, f32[3,8,128]{2,1,0:T(8,128)S(1)}, f32[1,128]{1,0:T(1,128)S(1)}, f32[36,64,128]{2,1,0:T(8,128)S(1)}, f32[36,64,128]{2,1,0:T(8,128)S(1)}) custom-call(s32[1]{0:T(128)} %bitcast.inner_at, f32[4,24]{1,0:T(4,128)S(1)} %copy-done, f32[4]{0:T(128)S(1)} %copy-done.2, ...), custom_call_target="tpu_custom_call" | custom-call | flops 83886080000 | bytes 20971520 | tf_op jit(solution)/shard_map/first_date_own/pallas_call | solution.py:491
  27.3 0.0 collective-permute-done.plan.plan_other
  27.3 5.8 %first_date_other.1 = (f32[1,2048]{1,0:T(1,128)S(1)}, f32[3,8,128]{2,1,0:T(8,128)S(1)}, f32[1,128]{1,0:T(1,128)S(1)}, f32[1,128]{1,0:T(1,128)S(1)}, f32[1,128]{1,0:T(1,128)S(1)}, /*index=5*/f32[1,128]{1,0:T(1,128)S(1)}) custom-call(s32[1]{0:T(128)} %bitcast.inner_at, s32[1]{0:T(128)} %bitcast.2.cell_at, f32[4,24]{1,0:T(4,128)S(1)} %copy-done, ...), custom_call_target="tpu_custom_call" | custom-call | tf_op jit(solution)/shard_map/first_date_other/pallas_call | solution.py:499
  33.1 1.1 %collective-permute-start.4 = (f32[1,128]{1,0:T(1,128)S(1)}, f32[1,128]{1,0:T(1,128)S(1)}, u32[]{:S(2)}, u32[]{:S(2)}) collective-permute-start(f32[1,128]{1,0:T(1,128)S(1)} %get-tuple-element.49), channel_id=1, source_target_pairs={{0,1},{1,2},{2,3},{3,0},{4,5},{5,6},{6,7},{7,4},{8,9},{9,10},{10,1... | collective-permute-start | bytes 1544 | tf_op jit(solution)/shard_map/ppermute | solution.py:511
  34.2 3.0 %collective-permute-start.5 = (f32[1,128]{1,0:T(1,128)S(1)}, f32[1,128]{1,0:T(1,128)S(1)}, u32[]{:S(2)}, u32[]{:S(2)}) collective-permute-start(f32[1,128]{1,0:T(1,128)S(1)} %get-tuple-element.50), channel_id=1, source_target_pairs={{0,2},{1,3},{2,0},{3,1},{4,6},{5,7},{6,4},{7,5},{8,10},{9,11},{10,... | collective-permute-start | bytes 1544 | tf_op jit(solution)/shard_map/ppermute | solution.py:511
  37.2 0.7 collective-permute-start.6
  37.9 0.6 second_tables.1
  38.6 0.0 collective-permute-done.4.next_one
  38.6 0.0 collective-permute-done.5.next_two
  38.6 1.0 %collective-permute-done.6.next_three = f32[1,128]{1,0:T(1,128)S(1)} collective-permute-done((f32[1,128]{1,0:T(1,128)S(1)}, f32[1,128]{1,0:T(1,128)S(1)}, u32[]{:S(2)}, u32[]{:S(2)}) %collective-permute-start.6) | collective-permute-done | bytes 544 | tf_op jit(solution)/shard_map/ppermute | solution.py:511
  39.6 8.0 %second_date.1 = (f32[2,1,2048]{2,1,0:T(1,128)}, f32[256,128]{1,0:T(8,128)S(1)}, f32[1,128]{1,0:T(1,128)S(1)}) custom-call(s32[1]{0:T(128)} %bitcast.inner_at, f32[4,24]{1,0:T(4,128)S(1)} %copy-done, f32[4]{0:T(128)S(1)} %copy-done.2, s32[1]{0:T(128)} %bitcast.1.place, f32[1,128]{1,0:T(1,128)S(1)} %get-tuple-element.48.kept_here, ...), custom_call_target="tpu_custom_call" | custom-call | tf_op jit(solution)/shard_map/second_date/pallas_call | solution.py:519
  47.6 25.7 %all_to_all.16 = f32[256,1,128]{2,1,0:T(1,128)S(1)} all-to-all(f32[256,1,128]{2,1,0:T(1,128)S(1)} %bitcast.24), channel_id=1, replica_groups=mesh['outer'=16,'inner'=4,'cell'=4] {'outer','inner','cell'}, dimensions={0} | all-to-all | bytes 262144 | tf_op jit(solution)/shard_map/all_to_all | solution.py:532
  73.3 0.7 last_sums.1
  (1 shorter events, 0.0 us)
Async XLA Ops:
  0.6 16.6 %copy-start.1 = (f32[2048]{0:T(1024)S(1)}, f32[2048]{0:T(1024)}, u32[]{:S(2)}) copy-start(f32[2048]{0:T(1024)} %param.23) | copy-start | bytes 24580
  0.6 9.5 %copy-start.9 = (f32[4,16,24]{2,1,0:T(8,128)S(1)}, f32[4,16,24]{2,1,0:T(8,128)}, u32[]{:S(2)}) copy-start(f32[4,16,24]{2,1,0:T(8,128)} %param.25) | copy-start | bytes 18436
  0.7 9.5 %copy-start.8 = (f32[4,16,36]{2,1,0:T(8,128)S(1)}, f32[4,16,36]{2,1,0:T(8,128)}, u32[]{:S(2)}) copy-start(f32[4,16,36]{2,1,0:T(8,128)} %param.24) | copy-start | bytes 27652
  0.7 16.6 %copy-start.7 = (f32[2048]{0:T(1024)S(1)}, f32[2048]{0:T(1024)}, u32[]{:S(2)}) copy-start(f32[2048]{0:T(1024)} %param.22) | copy-start | bytes 24580
  0.7 16.6 %copy-start.6 = (f32[2048]{0:T(1024)S(1)}, f32[2048]{0:T(1024)}, u32[]{:S(2)}) copy-start(f32[2048]{0:T(1024)} %param.21) | copy-start | bytes 24580
  0.7 16.6 %copy-start.5 = (s32[2048]{0:T(1024)S(1)}, s32[2048]{0:T(1024)}, u32[]{:S(2)}) copy-start(s32[2048]{0:T(1024)} %param.19) | copy-start | bytes 24580
  0.7 16.6 %copy-start.4 = (s32[2048]{0:T(1024)S(1)}, s32[2048]{0:T(1024)}, u32[]{:S(2)}) copy-start(s32[2048]{0:T(1024)} %param.18) | copy-start | bytes 24580
  0.7 16.6 %copy-start.3 = (f32[16,48]{1,0:T(8,128)S(1)}, f32[16,48]{1,0:T(8,128)}, u32[]{:S(2)}) copy-start(f32[16,48]{1,0:T(8,128)} %lapse_table.1) | copy-start | bytes 9220
  2.5 18.3 %all-to-all-start = ((f32[16,48,128]{2,1,0:T(8,128)}), f32[16,48,128]{2,1,0:T(8,128)S(1)}, u32[]{:S(2)}, u32[]{:S(2)}) async-start(f32[16,48,128]{2,1,0:T(8,128)} %parcel.1), calls=%async_computation | async-start | bytes 786432 | tf_op jit(solution)/shard_map/all_to_all | solution.py:457
  10.3 10.1 %collective-permute-start.2 = (f32[32,60]{1,0:T(8,128)S(1)}, f32[32,60]{1,0:T(8,128)S(1)}, u32[]{:S(2)}, u32[]{:S(2)}) collective-permute-start(f32[32,60]{1,0:T(8,128)S(1)} %pad_maximum_fusion), channel_id=1, source_target_pairs={{0,8},{4,12},{8,0},{12,4},{1,9},{5,13},{9,1},{13,5},{2,10},{6,14},... | collective-permute-start | bytes 23048 | tf_op jit(solution)/shard_map/ppermute | solution.py:464
  17.3 3.1 %copy-start.10 = (s32[2048]{0:T(1024)S(1)}, s32[2048]{0:T(1024)}, u32[]{:S(2)}) copy-start(s32[2048]{0:T(1024)} %param.20) | copy-start | bytes 24580
  17.3 4.2 %copy-start = (f32[4,24]{1,0:T(4,128)S(1)}, f32[4,24]{1,0:T(4,128)}, u32[]{:S(2)}) copy-start(f32[4,24]{1,0:T(4,128)} %world.5) | copy-start | bytes 1156
  17.3 4.2 %copy-start.2 = (f32[4]{0:T(128)S(1)}, f32[4]{0:T(128)}, u32[]{:S(2)}) copy-start(f32[4]{0:T(128)} %spread.5) | copy-start | bytes 52
  19.0 2.3 %collective-permute-start.1 = (f32[16,60]{1,0:T(8,128)S(1)}, f32[16,60]{1,0:T(8,128)S(1)}, u32[]{:S(2)}, u32[]{:S(2)}) collective-permute-start(f32[16,60]{1,0:T(8,128)S(1)} %get-tuple-element.43), channel_id=1, source_target_pairs={{0,4},{4,0},{8,12},{12,8},{1,5},{5,1},{9,13},{13,9},{2,6},{6,2},{1... | collective-permute-start | bytes 11528 | tf_op jit(solution)/shard_map/ppermute | solution.py:464
  20.3 1.2 %collective-permute-start.3 = (f32[32,60]{1,0:T(8,128)S(1)}, f32[32,60]{1,0:T(8,128)S(1)}, u32[]{:S(2)}, u32[]{:S(2)}) collective-permute-start(f32[32,60]{1,0:T(8,128)S(1)} %collective-permute-done.2.far_rates.far), channel_id=1, source_target_pairs={{0,4},{4,0},{8,12},{12,8},{1,5},{5,1},{9,13},{13,9},{2,6},{6,2},{1... | collective-permute-start | bytes 23048 | tf_op jit(solution)/shard_map/ppermute | solution.py:464
  20.8 6.5 %collective-permute-start = (f32[16,48,128]{2,1,0:T(8,128)S(1)}, f32[16,48,128]{2,1,0:T(8,128)S(1)}, u32[]{:S(2)}, u32[]{:S(2)}) collective-permute-start(f32[16,48,128]{2,1,0:T(8,128)S(1)} %all-to-all-done.plan.plan_own), channel_id=1, source_target_pairs={{0,4},{4,0},{8,12},{12,8},{1,5},{5,1},{9,13},{13,9},{2,6},{6,2},{1... | collective-permute-start | bytes 1179656 | tf_op jit(solution)/shard_map/ppermute | solution.py:464
  33.1 5.4 %collective-permute-start.4 = (f32[1,128]{1,0:T(1,128)S(1)}, f32[1,128]{1,0:T(1,128)S(1)}, u32[]{:S(2)}, u32[]{:S(2)}) collective-permute-start(f32[1,128]{1,0:T(1,128)S(1)} %get-tuple-element.49), channel_id=1, source_target_pairs={{0,1},{1,2},{2,3},{3,0},{4,5},{5,6},{6,7},{7,4},{8,9},{9,10},{10,1... | collective-permute-start | bytes 1544 | tf_op jit(solution)/shard_map/ppermute | solution.py:511
  34.2 4.3 %collective-permute-start.5 = (f32[1,128]{1,0:T(1,128)S(1)}, f32[1,128]{1,0:T(1,128)S(1)}, u32[]{:S(2)}, u32[]{:S(2)}) collective-permute-start(f32[1,128]{1,0:T(1,128)S(1)} %get-tuple-element.50), channel_id=1, source_target_pairs={{0,2},{1,3},{2,0},{3,1},{4,6},{5,7},{6,4},{7,5},{8,10},{9,11},{10,... | collective-permute-start | bytes 1544 | tf_op jit(solution)/shard_map/ppermute | solution.py:511
  37.2 2.4 %collective-permute-start.6 = (f32[1,128]{1,0:T(1,128)S(1)}, f32[1,128]{1,0:T(1,128)S(1)}, u32[]{:S(2)}, u32[]{:S(2)}) collective-permute-start(f32[1,128]{1,0:T(1,128)S(1)} %get-tuple-element.51), channel_id=1, source_target_pairs={{0,3},{1,0},{2,1},{3,2},{4,7},{5,4},{6,5},{7,6},{8,11},{9,8},{10,9... | collective-permute-start | bytes 1544 | tf_op jit(solution)/shard_map/ppermute | solution.py:511

commit v6 on v5

--- a/solution.py
+++ b/solution.py
@@ -35,11 +35,13 @@
         copies.append(pltpu.make_async_copy(source.at[:, columns], received.at[i], in_sems.at[i + 1]))
     for copy in copies:
         copy.start()
-    for copy in copies:
-        copy.wait()
+    copies[0].wait()
     fee = fees[...]
     grow = jnp.log1p(-fee)
     per_fee = (1.0 - fee) / fee
+    scales = [fee * jnp.exp(-((outer_at[0] * each + r).astype(jnp.float32) + 1.0) * grow) for r in range(each)]
+    for copy in copies[1:]:
+        copy.wait()
     for r in range(each):
         for t in range(count):
             at = slice(t * LANES, (t + 1) * LANES)
@@ -49,8 +51,7 @@
             scratch[row : row + 1, :] = received[2, r : r + 1, at]
     for r in range(each):
         at, then = lines_of(r, count), lines_of(each + r, count)
-        month = (outer_at[0] * each + r).astype(jnp.float32)
-        scratch[at, :] = scratch[at, :] * (fee * jnp.exp(-(month + 1.0) * grow))
+        scratch[at, :] = scratch[at, :] * scales[r]
         scratch[then, :] = scratch[then, :] * per_fee
     copies = [pltpu.make_async_copy(scratch, sent.at[i], out_sems.at[i]) for i in range(sent.shape[0])]
     for copy in copies:

time: 74.3 us -> 74.2 us (level)
  no operation moved by 1% of the time
where the time goes in v6:
time: 74.2 us; the launch traced here: 74 us
  blocking collectives  25.7 us (35%)
  Pallas kernels  24.3 us (33%)
  starting transfers between devices  21.3 us (29%)
  waiting for transfers between devices  1.26 us (2%)
  between operations  0.88 us (1%)
    all_to_all x1, blocking collectives, body(): received = lax.all_to_all(parcel, ALL, 0, 0, tiled=True)  25.7 us
    ppermute x4, starting transfers between devices, swapped(): return lax.ppermute(value, 'inner', [(j, j ^ s) for j in range(inner_size)])  8.92 us
    pallas_call x1, Pallas kernels, body(): call(functools.partial(second_kernel, cells_all), 'second_date', [floats(...  7.97 us
    all_to_all x1, starting transfers between devices, body(): plan_own = lax.all_to_all(sent, 'outer', 0, 0, tiled=True)  7.6 us
    pallas_call x1, Pallas kernels, body(): call(functools.partial(first_other_kernel, cell_size), 'first_date_other'...  5.83 us
    pallas_call x1, Pallas kernels, body(): call(first_own_kernel, 'first_date_own', [floats(1, local), state, line,...  5.75 us
    ppermute x3, starting transfers between devices, body(): lax.ppermute(others[s - 1], 'cell', [(k, (k + s) % cell_size) for k in ra...  4.8 us
    pallas_call x1, Pallas kernels, body(): call(parcel_kernel, 'parcel', floats(outer_size, 2 * each * own, LANES),...  1.8 us
  transfers between devices with their start and end apart: 8, of which 2 were waited for; matrix products, arithmetic and copies ran while one was open for 1% of the time, Pallas kernels for 11%

profile of v6, /device:TPU:1, one launch (start us, length us, event | category | flops | bytes accessed | tf_op | source)
XLA Modules:
  0.0 74.0 jit_solution(2157412565184836305)
XLA Ops:
  0.6 0.0 copy-start.1
  0.6 0.0 copy-start.9
  0.7 0.0 copy-start.8
  0.7 0.0 copy-start.7
  0.7 0.0 copy-start.6
  0.7 0.0 copy-start.5
  0.7 0.0 copy-start.4
  0.7 0.0 copy-start.3
  0.7 1.8 %parcel.1 = f32[16,48,128]{2,1,0:T(8,128)} custom-call(s32[1]{0:T(128)} %bitcast.3.outer_at, s32[1]{0:T(128)} %bitcast.inner_at, f32[3,2048]{1,0:T(4,128)} %premium.1, f32[3,2048]{1,0:T(4,128)} %charge.1, f32[3,2048]{1,0:T(4,128)} %mortality.1, f32[2,8,128]{2,1,0:T(8,128)} %bitcast.25), custom_call_target="tpu_custom_call" | custom-call | tf_op jit(solution)/shard_map/parcel/pallas_call | solution.py:441
  2.5 7.6 %all-to-all-start = ((f32[16,48,128]{2,1,0:T(8,128)}), f32[16,48,128]{2,1,0:T(8,128)S(1)}, u32[]{:S(2)}, u32[]{:S(2)}) async-start(f32[16,48,128]{2,1,0:T(8,128)} %parcel.1), calls=%async_computation | async-start | bytes 786432 | tf_op jit(solution)/shard_map/all_to_all | solution.py:458
  10.2 0.0 copy-done.9
  10.2 0.0 copy-done.8
  10.2 0.1 fusion.8
  10.3 7.0 %collective-permute-start.2 = (f32[32,60]{1,0:T(8,128)S(1)}, f32[32,60]{1,0:T(8,128)S(1)}, u32[]{:S(2)}, u32[]{:S(2)}) collective-permute-start(f32[32,60]{1,0:T(8,128)S(1)} %pad_maximum_fusion), channel_id=1, source_target_pairs={{0,8},{4,12},{8,0},{12,4},{1,9},{5,13},{9,1},{13,5},{2,10},{6,14},... | collective-permute-start | bytes 23048 | tf_op jit(solution)/shard_map/ppermute | solution.py:465
  17.3 0.0 copy-done.1
  17.3 0.0 copy-done.7
  17.3 0.0 copy-done.6
  17.3 0.0 copy-done.5
  17.3 0.0 copy-done.4
  17.3 0.0 copy-done.3
  17.3 0.0 copy-start.10
  17.3 0.0 copy-start
  17.3 0.0 copy-start.2
  17.3 1.7 %prepare.1 = (f32[5,16,128]{2,1,0:T(8,128)S(1)}, f32[768,128]{1,0:T(8,128)S(1)}, f32[768,128]{1,0:T(8,128)S(1)}, f32[768,128]{1,0:T(8,128)S(1)}, f32[768,128]{1,0:T(8,128)S(1)}, /*index=5*/f32[16,60]{1,0:T(8,128)S(1)}) custom-call(s32[1]{0:T(128)} %bitcast.inner_at, f32[16,48]{1,0:T(8,128)S(1)} %copy-done.3, s32[2,8,128]{2,1,0:T(8,128)S(1)} %bitcast.27, ...), custom_call_target="tpu_custom_call" | custom-call | flops 16777216000 | bytes 4194304 | tf_op jit(solution)/shard_map/prepare/pallas_call | solution.py:471
  19.0 1.3 %collective-permute-start.1 = (f32[16,60]{1,0:T(8,128)S(1)}, f32[16,60]{1,0:T(8,128)S(1)}, u32[]{:S(2)}, u32[]{:S(2)}) collective-permute-start(f32[16,60]{1,0:T(8,128)S(1)} %get-tuple-element.43), channel_id=1, source_target_pairs={{0,4},{4,0},{8,12},{12,8},{1,5},{5,1},{9,13},{13,9},{2,6},{6,2},{1... | collective-permute-start | bytes 11528 | tf_op jit(solution)/shard_map/ppermute | solution.py:465
  20.3 0.0 collective-permute-done.2.far_rates.far
  20.3 0.1 collective-permute-start.3
  20.4 0.0 copy-done.10
  20.4 0.3 fusion.block_hot
  20.8 0.0 all-to-all-done.plan.plan_own
  20.8 0.5 collective-permute-start
  21.3 0.0 collective-permute-done.1.near_rates.near
  21.3 0.2 collective-permute-done.3.across_rates.across
  21.5 0.0 copy-done
  21.5 0.0 copy-done.2
  21.5 5.7 %first_date_own.1 = (f32[1,2048]{1,0:T(1,128)S(1)}, f32[3,8,128]{2,1,0:T(8,128)S(1)}, f32[1,128]{1,0:T(1,128)S(1)}, f32[36,64,128]{2,1,0:T(8,128)S(1)}, f32[36,64,128]{2,1,0:T(8,128)S(1)}) custom-call(s32[1]{0:T(128)} %bitcast.inner_at, f32[4,24]{1,0:T(4,128)S(1)} %copy-done, f32[4]{0:T(128)S(1)} %copy-done.2, ...), custom_call_target="tpu_custom_call" | custom-call | flops 83886080000 | bytes 20971520 | tf_op jit(solution)/shard_map/first_date_own/pallas_call | solution.py:492
  27.3 0.0 collective-permute-done.plan.plan_other
  27.3 5.8 %first_date_other.1 = (f32[1,2048]{1,0:T(1,128)S(1)}, f32[3,8,128]{2,1,0:T(8,128)S(1)}, f32[1,128]{1,0:T(1,128)S(1)}, f32[1,128]{1,0:T(1,128)S(1)}, f32[1,128]{1,0:T(1,128)S(1)}, /*index=5*/f32[1,128]{1,0:T(1,128)S(1)}) custom-call(s32[1]{0:T(128)} %bitcast.inner_at, s32[1]{0:T(128)} %bitcast.2.cell_at, f32[4,24]{1,0:T(4,128)S(1)} %copy-done, ...), custom_call_target="tpu_custom_call" | custom-call | tf_op jit(solution)/shard_map/first_date_other/pallas_call | solution.py:500
  33.1 1.1 %collective-permute-start.4 = (f32[1,128]{1,0:T(1,128)S(1)}, f32[1,128]{1,0:T(1,128)S(1)}, u32[]{:S(2)}, u32[]{:S(2)}) collective-permute-start(f32[1,128]{1,0:T(1,128)S(1)} %get-tuple-element.49), channel_id=1, source_target_pairs={{0,1},{1,2},{2,3},{3,0},{4,5},{5,6},{6,7},{7,4},{8,9},{9,10},{10,1... | collective-permute-start | bytes 1544 | tf_op jit(solution)/shard_map/ppermute | solution.py:512
  34.2 3.0 %collective-permute-start.5 = (f32[1,128]{1,0:T(1,128)S(1)}, f32[1,128]{1,0:T(1,128)S(1)}, u32[]{:S(2)}, u32[]{:S(2)}) collective-permute-start(f32[1,128]{1,0:T(1,128)S(1)} %get-tuple-element.50), channel_id=1, source_target_pairs={{0,2},{1,3},{2,0},{3,1},{4,6},{5,7},{6,4},{7,5},{8,10},{9,11},{10,... | collective-permute-start | bytes 1544 | tf_op jit(solution)/shard_map/ppermute | solution.py:512
  37.2 0.7 collective-permute-start.6
  37.9 0.6 second_tables.1
  38.5 0.0 collective-permute-done.4.next_one
  38.6 0.0 collective-permute-done.5.next_two
  38.6 1.0 %collective-permute-done.6.next_three = f32[1,128]{1,0:T(1,128)S(1)} collective-permute-done((f32[1,128]{1,0:T(1,128)S(1)}, f32[1,128]{1,0:T(1,128)S(1)}, u32[]{:S(2)}, u32[]{:S(2)}) %collective-permute-start.6) | collective-permute-done | bytes 544 | tf_op jit(solution)/shard_map/ppermute | solution.py:512
  39.6 8.0 %second_date.1 = (f32[2,1,2048]{2,1,0:T(1,128)}, f32[256,128]{1,0:T(8,128)S(1)}, f32[1,128]{1,0:T(1,128)S(1)}) custom-call(s32[1]{0:T(128)} %bitcast.inner_at, f32[4,24]{1,0:T(4,128)S(1)} %copy-done, f32[4]{0:T(128)S(1)} %copy-done.2, s32[1]{0:T(128)} %bitcast.1.place, f32[1,128]{1,0:T(1,128)S(1)} %get-tuple-element.48.kept_here, ...), custom_call_target="tpu_custom_call" | custom-call | tf_op jit(solution)/shard_map/second_date/pallas_call | solution.py:520
  47.6 25.7 %all_to_all.16 = f32[256,1,128]{2,1,0:T(1,128)S(1)} all-to-all(f32[256,1,128]{2,1,0:T(1,128)S(1)} %bitcast.24), channel_id=1, replica_groups=mesh['outer'=16,'inner'=4,'cell'=4] {'outer','inner','cell'}, dimensions={0} | all-to-all | bytes 262144 | tf_op jit(solution)/shard_map/all_to_all | solution.py:533
  73.3 0.7 last_sums.1
  (1 shorter events, 0.0 us)
Async XLA Ops:
  0.6 16.6 %copy-start.1 = (f32[2048]{0:T(1024)S(1)}, f32[2048]{0:T(1024)}, u32[]{:S(2)}) copy-start(f32[2048]{0:T(1024)} %param.23) | copy-start | bytes 24580
  0.6 9.5 %copy-start.9 = (f32[4,16,24]{2,1,0:T(8,128)S(1)}, f32[4,16,24]{2,1,0:T(8,128)}, u32[]{:S(2)}) copy-start(f32[4,16,24]{2,1,0:T(8,128)} %param.25) | copy-start | bytes 18436
  0.7 9.5 %copy-start.8 = (f32[4,16,36]{2,1,0:T(8,128)S(1)}, f32[4,16,36]{2,1,0:T(8,128)}, u32[]{:S(2)}) copy-start(f32[4,16,36]{2,1,0:T(8,128)} %param.24) | copy-start | bytes 27652
  0.7 16.6 %copy-start.7 = (f32[2048]{0:T(1024)S(1)}, f32[2048]{0:T(1024)}, u32[]{:S(2)}) copy-start(f32[2048]{0:T(1024)} %param.22) | copy-start | bytes 24580
  0.7 16.6 %copy-start.6 = (f32[2048]{0:T(1024)S(1)}, f32[2048]{0:T(1024)}, u32[]{:S(2)}) copy-start(f32[2048]{0:T(1024)} %param.21) | copy-start | bytes 24580
  0.7 16.6 %copy-start.5 = (s32[2048]{0:T(1024)S(1)}, s32[2048]{0:T(1024)}, u32[]{:S(2)}) copy-start(s32[2048]{0:T(1024)} %param.19) | copy-start | bytes 24580
  0.7 16.6 %copy-start.4 = (s32[2048]{0:T(1024)S(1)}, s32[2048]{0:T(1024)}, u32[]{:S(2)}) copy-start(s32[2048]{0:T(1024)} %param.18) | copy-start | bytes 24580
  0.7 16.6 %copy-start.3 = (f32[16,48]{1,0:T(8,128)S(1)}, f32[16,48]{1,0:T(8,128)}, u32[]{:S(2)}) copy-start(f32[16,48]{1,0:T(8,128)} %lapse_table.1) | copy-start | bytes 9220
  2.5 18.3 %all-to-all-start = ((f32[16,48,128]{2,1,0:T(8,128)}), f32[16,48,128]{2,1,0:T(8,128)S(1)}, u32[]{:S(2)}, u32[]{:S(2)}) async-start(f32[16,48,128]{2,1,0:T(8,128)} %parcel.1), calls=%async_computation | async-start | bytes 786432 | tf_op jit(solution)/shard_map/all_to_all | solution.py:458
  10.3 10.1 %collective-permute-start.2 = (f32[32,60]{1,0:T(8,128)S(1)}, f32[32,60]{1,0:T(8,128)S(1)}, u32[]{:S(2)}, u32[]{:S(2)}) collective-permute-start(f32[32,60]{1,0:T(8,128)S(1)} %pad_maximum_fusion), channel_id=1, source_target_pairs={{0,8},{4,12},{8,0},{12,4},{1,9},{5,13},{9,1},{13,5},{2,10},{6,14},... | collective-permute-start | bytes 23048 | tf_op jit(solution)/shard_map/ppermute | solution.py:465
  17.3 3.1 %copy-start.10 = (s32[2048]{0:T(1024)S(1)}, s32[2048]{0:T(1024)}, u32[]{:S(2)}) copy-start(s32[2048]{0:T(1024)} %param.20) | copy-start | bytes 24580
  17.3 4.2 %copy-start = (f32[4,24]{1,0:T(4,128)S(1)}, f32[4,24]{1,0:T(4,128)}, u32[]{:S(2)}) copy-start(f32[4,24]{1,0:T(4,128)} %world.5) | copy-start | bytes 1156
  17.3 4.2 %copy-start.2 = (f32[4]{0:T(128)S(1)}, f32[4]{0:T(128)}, u32[]{:S(2)}) copy-start(f32[4]{0:T(128)} %spread.5) | copy-start | bytes 52
  19.0 2.3 %collective-permute-start.1 = (f32[16,60]{1,0:T(8,128)S(1)}, f32[16,60]{1,0:T(8,128)S(1)}, u32[]{:S(2)}, u32[]{:S(2)}) collective-permute-start(f32[16,60]{1,0:T(8,128)S(1)} %get-tuple-element.43), channel_id=1, source_target_pairs={{0,4},{4,0},{8,12},{12,8},{1,5},{5,1},{9,13},{13,9},{2,6},{6,2},{1... | collective-permute-start | bytes 11528 | tf_op jit(solution)/shard_map/ppermute | solution.py:465
  20.3 1.2 %collective-permute-start.3 = (f32[32,60]{1,0:T(8,128)S(1)}, f32[32,60]{1,0:T(8,128)S(1)}, u32[]{:S(2)}, u32[]{:S(2)}) collective-permute-start(f32[32,60]{1,0:T(8,128)S(1)} %collective-permute-done.2.far_rates.far), channel_id=1, source_target_pairs={{0,4},{4,0},{8,12},{12,8},{1,5},{5,1},{9,13},{13,9},{2,6},{6,2},{1... | collective-permute-start | bytes 23048 | tf_op jit(solution)/shard_map/ppermute | solution.py:465
  20.8 6.5 %collective-permute-start = (f32[16,48,128]{2,1,0:T(8,128)S(1)}, f32[16,48,128]{2,1,0:T(8,128)S(1)}, u32[]{:S(2)}, u32[]{:S(2)}) collective-permute-start(f32[16,48,128]{2,1,0:T(8,128)S(1)} %all-to-all-done.plan.plan_own), channel_id=1, source_target_pairs={{0,4},{4,0},{8,12},{12,8},{1,5},{5,1},{9,13},{13,9},{2,6},{6,2},{1... | collective-permute-start | bytes 1179656 | tf_op jit(solution)/shard_map/ppermute | solution.py:465
  33.1 5.4 %collective-permute-start.4 = (f32[1,128]{1,0:T(1,128)S(1)}, f32[1,128]{1,0:T(1,128)S(1)}, u32[]{:S(2)}, u32[]{:S(2)}) collective-permute-start(f32[1,128]{1,0:T(1,128)S(1)} %get-tuple-element.49), channel_id=1, source_target_pairs={{0,1},{1,2},{2,3},{3,0},{4,5},{5,6},{6,7},{7,4},{8,9},{9,10},{10,1... | collective-permute-start | bytes 1544 | tf_op jit(solution)/shard_map/ppermute | solution.py:512
  34.2 4.3 %collective-permute-start.5 = (f32[1,128]{1,0:T(1,128)S(1)}, f32[1,128]{1,0:T(1,128)S(1)}, u32[]{:S(2)}, u32[]{:S(2)}) collective-permute-start(f32[1,128]{1,0:T(1,128)S(1)} %get-tuple-element.50), channel_id=1, source_target_pairs={{0,2},{1,3},{2,0},{3,1},{4,6},{5,7},{6,4},{7,5},{8,10},{9,11},{10,... | collective-permute-start | bytes 1544 | tf_op jit(solution)/shard_map/ppermute | solution.py:512
  37.2 2.4 %collective-permute-start.6 = (f32[1,128]{1,0:T(1,128)S(1)}, f32[1,128]{1,0:T(1,128)S(1)}, u32[]{:S(2)}, u32[]{:S(2)}) collective-permute-start(f32[1,128]{1,0:T(1,128)S(1)} %get-tuple-element.51), channel_id=1, source_target_pairs={{0,3},{1,0},{2,1},{3,2},{4,7},{5,4},{6,5},{7,6},{8,11},{9,8},{10,9... | collective-permute-start | bytes 1544 | tf_op jit(solution)/shard_map/ppermute | solution.py:512
